TPU v7x, 32 devices: a whole 2x2x4 slice. The times are simulated.
32 devices in a mesh: tok: 8 (over y, x, core), tp: 4 (over z).
Axes of the slice: x: 2, y: 2, z: 4, core: 2. Of those that a mesh axis runs over, the one named last changes fastest.
Arguments:
- hidden: bfloat16 [16384, 8192], P('tok', 'tp'), may hold values from -6 to 6
- key_value_weight: bfloat16 [8192, 2, 1024], P('tp'), may hold values from -0.09375 to 0.09375
- adapter_down_weight: bfloat16 [16, 8192, 128], P('tok', 'tp'), may hold values from -0.0625 to 0.0625
- adapter_up_weight: bfloat16 [16, 2, 64, 1024], P('tok', None, None, 'tp'), may hold values from -0.75 to 0.75
- tenant_per_block: int32 [128], P('tok'), may hold values from 0 to 15, as said below
Outputs:
- kv: bfloat16 [16384, 2, 1024], P('tok', None, 'tp')
Inputs may be any that keep to these rules, and one draw needn't show every extreme that they name: `tenant_per_block`: the index of tok that holds tenant t is t // 2. The blocks of one index of tok have at most 4 tenant held by any one index, and 1 indices hold tenants of exactly 4 blocks of every index.
All inputs are finite; a program needn't handle non-finite values.
Results may differ from a plain program's by a relative error of at most 0.02.
Values may be sent and summed in bfloat16 or wider, within the bound.
No kernel may reach another device: no remote copies, remote signals or barrier semaphores. Data moves between devices by JAX's collectives and lax.ppermute only.
A program may use at most 128 MiB of HBM per device.

v0:
```python
import jax
import jax.numpy as jnp
from jax import lax
from jax.sharding import PartitionSpec as P


def up_terms(low, up_sel, rows, adapter_rank_index):
    count = low.shape[0]
    shaped = low.reshape(count, rows, 2, adapter_rank_index)
    return jnp.einsum("brhk,bhkc->brhc", shaped, up_sel, preferred_element_type=jnp.float32).astype(
        jnp.bfloat16
    )


def local(hidden, key_value_weight, adapter_down_weight, adapter_up_weight, tenant_per_block):
    tok_rows, local_width = hidden.shape
    blk_count = tenant_per_block.shape[0]
    rows = tok_rows // blk_count
    key_value_partial = adapter_up_weight.shape[3]
    adapter_rank_index = adapter_down_weight.shape[2] // 2
    partial_value = jnp.dot(
        hidden, key_value_weight.reshape(local_width, -1), preferred_element_type=jnp.float32
    )
    base = lax.psum_scatter(
        partial_value.reshape(tok_rows, 2, -1).astype(jnp.bfloat16),
        "tp",
        scatter_dimension=2,
        tiled=True,
    ).astype(jnp.float32)
    blocks = hidden.reshape(blk_count, rows, local_width)
    gathered_down_maps = lax.all_gather(adapter_down_weight, "tok", axis=0, tiled=True)
    gathered_up_maps = lax.all_gather(adapter_up_weight, "tok", axis=0, tiled=True)
    down_sel = jnp.take(gathered_down_maps, tenant_per_block, axis=0)
    low = jnp.einsum("brd,bdk->brk", blocks, down_sel, preferred_element_type=jnp.float32)
    low = lax.psum(low.astype(jnp.bfloat16), "tp")
    up_sel = jnp.take(gathered_up_maps, tenant_per_block, axis=0)
    adapt = up_terms(low, up_sel, rows, adapter_rank_index)
    total = base + adapt.reshape(tok_rows, 2, key_value_partial).astype(jnp.float32)
    return total.astype(jnp.bfloat16)


def solution(mesh):
    in_specs = (
        P("tok", "tp"),
        P("tp", None, None),
        P("tok", "tp", None),
        P("tok", None, None, "tp"),
        P("tok"),
    )
    out_specs = P("tok", None, "tp")
    return jax.shard_map(local, mesh=mesh, in_specs=in_specs, out_specs=out_specs, check_vma=False)
```

profile of v0, /device:TPU:0, one launch (start us, length us, event | category | flops | bytes accessed | tf_op | source)
XLA Modules:
  0.0 303.0 jit_solution(15175898767640918454)
XLA Ops:
  6.5 0.0 all-gather.5.cloned.1.call-start
  6.5 0.7 all-gather.5.cloned.1.call-update
  7.3 0.0 all-gather.3.cloned.1.call-start
  7.3 0.7 all-gather.3.cloned.1.call-update
  8.0 0.0 all-reduce.2.cloned.1.call-start
  8.1 10.1 %copy.15 = bf16[256,8,2,1024]{3,1,2,0:T(8,128)(2,1)} copy(bf16[256,8,2,1024]{3,2,1,0:T(2,128)(2,1)} %bitcast.24) | data formatting | bytes 16777216
  18.2 0.0 copy-start
  18.2 11.7 %copy.10 = bf16[2048,2048]{1,0:T(8,128)(2,1)} copy(bf16[2048,2048]{0,1:T(8,128)(2,1)} %bitcast.23) | data formatting | bytes 16777216 | tf_op jit(solution)/shard_map/dot_general | solution.py:21
  29.9 0.0 copy-done
  30.0 36.4 %all-gather.5.cloned.1.call-done = bf16[16,2048,128]{2,1,0:T(8,128)(2,1)} async-done(((bf16[2,2048,128]{2,1,0:T(8,128)(2,1)}), bf16[16,2048,128]{2,1,0:T(8,128)(2,1)}) %all-gather.5.cloned.1.call-update) | async-done | bytes 8388624 | tf_op jit(solution)/shard_map/all_gather | solution.py:31
  66.4 8.2 %gather_fusion.1 = bf16[16,2048,128]{2,1,0:T(8,128)(2,1)} fusion(bf16[16,2048,128]{2,1,0:T(8,128)(2,1)} %all-gather.5.cloned.1.call-done, s32[1024]{0:T(1024)S(1)} %pad_clamp_fusion), kind=kCustom, calls=%fused_computation.1 | custom fusion | bytes 16777280 | tf_op jit(solution)/shard_map/jit(_take)/gather | solution.py:33
  74.5 9.4 %fusion.10 = bf16[16,128,128]{2,1,0:T(8,128)(2,1)} fusion(bf16[16,128,2048]{2,1,0:T(8,128)(2,1)} %bitcast.27, bf16[16,2048,128]{2,1,0:T(8,128)(2,1)} %gather_fusion.1, pred[16]{0:T(512)(128)(4,1)S(1)} %compare_and_fusion), kind=kOutput, calls=%fused_computation.12 | convolution fusion | flops 1078198272 | bytes 17301520 | tf_op jit(solution)/shard_map/brd,bdk->brk/dot_general | solution.py:34
  84.0 0.0 all-reduce.2.cloned.1.call-update
  84.0 0.2 reduce-scatter.2.cloned.1.call-start
  84.2 23.9 %fusion.5 = bf16[2048,2,1024]{2,0,1:T(8,128)(2,1)} fusion(bf16[2,1024,2048]{2,1,0:T(8,128)(2,1)} %bitcast.25, bf16[2048,2048]{1,0:T(8,128)(2,1)} %param.5), kind=kOutput, calls=%fused_computation.7 | convolution fusion | flops 17184063488 | bytes 25165824 | tf_op jit(solution)/shard_map/dot_general | solution.py:21
  108.1 0.0 reduce-scatter.2.cloned.1.call-update
  108.2 0.0 all-gather.3.cloned.1.call-done
  108.2 1.8 gather_fusion
  110.0 22.4 %all-reduce.2.cloned.1.call-done = bf16[16,128,2,64]{1,3,2,0:T(8,128)(2,1)} async-done(((bf16[16,128,2,64]{1,3,2,0:T(8,128)(2,1)}), bf16[16,128,2,64]{1,3,2,0:T(8,128)(2,1)}) %all-reduce.2.cloned.1.call-update) | async-done | bytes 524304 | tf_op jit(solution)/shard_map/psum | solution.py:35
  132.4 1.8 convert_bitcast_fusion
  134.3 2.3 copy.12
  136.5 142.6 %reduce-scatter.2.cloned.1.call-done = bf16[2048,2,256]{2,0,1:T(8,128)(2,1)} async-done(((bf16[2048,2,1024]{2,0,1:T(8,128)(2,1)}), bf16[2048,2,256]{2,0,1:T(8,128)(2,1)}) %reduce-scatter.2.cloned.1.call-update) | async-done | bytes 2097168 | tf_op jit(solution)/shard_map/reduce_scatter | solution.py:24
  279.2 3.3 %fusion.8 = bf16[2048,2,256]{2,0,1:T(8,128)(2,1)S(1)} fusion(f32[16,128,2,256]{3,1,0,2:T(8,128)} %copy.12, bf16[2048,2,256]{2,0,1:T(8,128)(2,1)} %reduce-scatter.2.cloned.1.call-done), kind=kLoop, calls=%fused_computation.9 | loop fusion | flops 3145728 | bytes 8388608 | tf_op jit(solution)/shard_map/convert_element_type | solution.py:39
  282.5 14.0 %copy.13 = bf16[2048,2,256]{2,1,0:T(2,128)(2,1)} copy(bf16[2048,2,256]{2,0,1:T(8,128)(2,1)S(1)} %fusion.8) | data formatting | bytes 4194304 | tf_op jit(solution)/shard_map/convert_element_type | solution.py:39
  (3 shorter events, 0.0 us)
Async XLA Ops:
  6.5 59.8 %all-gather.5.cloned.1.call-start = ((), (), s32[]{:S(2)}) async-start(), calls=%async_computation.3 | async-start | bytes 9437184 | tf_op jit(solution)/shard_map/all_gather | solution.py:31
  7.3 100.9 %all-gather.3.cloned.1.call-start = ((), (), s32[]{:S(2)}) async-start(), calls=%async_computation.2 | async-start | bytes 1179648 | tf_op jit(solution)/shard_map/all_gather | solution.py:32
  8.0 124.4 %all-reduce.2.cloned.1.call-start = ((), (), s32[]{:S(2)}) async-start(), calls=%async_computation.4 | async-start | bytes 1048576 | tf_op jit(solution)/shard_map/psum | solution.py:35
  18.2 11.7 %copy-start = (s32[16]{0:T(128)S(1)}, s32[16]{0:T(128)}, u32[]{:S(2)}) copy-start(s32[16]{0:T(128)} %param.9) | copy-start | bytes 196
  84.0 195.1 %reduce-scatter.2.cloned.1.call-start = ((), (), s32[]{:S(2)}) async-start(), calls=%async_computation.1 | async-start | bytes 10485760 | tf_op jit(solution)/shard_map/reduce_scatter | solution.py:24
Sparse Core Ops, SparseCore 0:
  9.2 57.0 all-gather.4
  68.3 23.4 all-gather.2
  94.1 38.2 all-reduce.1
  134.7 144.4 reduce-scatter.1
where the time goes:
time: 304 us; the launch traced here: 303 us
  waiting for transfers between devices  203 us (67%)
  local copies, waits for them, and re-layouts  48.2 us (16%)
  matrix products  35.2 us (12%)
  between operations  13.2 us (4%)
  other arithmetic  3.35 us (1%)
    reduce_scatter x1, waiting for transfers between devices, local(): lax.psum_scatter(partial_value.reshape(tok_rows, 2, -1).astype(jnp.bfloat...  143 us
    all_gather x1, waiting for transfers between devices, local(): lax.all_gather(adapter_down_weight, 'tok', axis=0, tiled=True)  36.4 us
    dot_general x1, matrix products, local(): jnp.dot(hidden, key_value_weight.reshape(local_width, -1), preferred_elem...  23.9 us
    psum x1, waiting for transfers between devices, local(): low = lax.psum(low.astype(jnp.bfloat16), 'tp')  22.4 us
    convert_element_type x1, local copies, waits for them, and re-layouts, local(): return total.astype(jnp.bfloat16)  14 us
    dot_general x1, local copies, waits for them, and re-layouts, local(): jnp.dot(hidden, key_value_weight.reshape(local_width, -1), preferred_elem...  11.7 us
    unnamed x3, local copies, waits for them, and re-layouts  10.2 us
    dot_general x1, matrix products, local(): jnp.einsum('brd,bdk->brk', blocks, down_sel, preferred_element_type=jnp.f...  9.44 us
  transfers between devices with their start and end apart: 4, of which 3 were waited for; matrix products, arithmetic and copies ran while one was open for 23% of the time, Pallas kernels for 0%

commit v1 on v0

v1 whole, which is shorter than its diff:
```python
import jax
import jax.numpy as jnp
import numpy as np
from jax import lax
from jax.experimental import pallas as pl
from jax.experimental.pallas import tpu as pltpu
from jax.sharding import PartitionSpec as P

UNITS = 4
SCALE = 0.25
VMEM_BYTES = 63 * 1024 * 1024


def line_plan(n):
    sends = {}
    slots = np.zeros((n, n), np.int32)
    for i in range(n):
        order = []
        for c in range(n):
            if c == i:
                continue
            forward = c > i
            time = n - c + i if forward else c + n - i
            parity = (i if forward else i - 1) % 2
            order.append((time, 1 - parity, c, parity, i + 1 if forward else i - 1))
        order.sort()
        for k, (time, _, c, parity, to) in enumerate(order):
            slots[i, k] = c
            sends.setdefault((time, parity), []).append((i, to, k))
        slots[i, n - 1] = i
    return slots, sends


def by_device(table, axis):
    return jnp.asarray(table)[lax.axis_index(axis)]


def params():
    return pltpu.CompilerParams(vmem_limit_bytes=VMEM_BYTES)


def estimate(microseconds):
    return pl.CostEstimate(flops=1, bytes_accessed=int(microseconds * 3.69e6 * SCALE), transcendentals=0)


HERE = pl.BlockSpec(memory_space=pl.ANY)


def first_piece(hidden, weight, which, rows, chunk):
    width = hidden.shape[1]
    steps = 2
    depth = width // steps

    def body(which_ref, hidden_ref, weight_ref, flat_ref, out_ref, total):
        k = pl.program_id(0)
        flat_ref[...] = weight_ref[...].reshape(depth, 2 * chunk)
        term = jnp.dot(hidden_ref[...], flat_ref[...], preferred_element_type=jnp.float32)

        @pl.when(k == 0)
        def _():
            total[...] = term

        @pl.when(k > 0)
        def _():
            total[...] += term

        @pl.when(k == steps - 1)
        def _():
            out_ref[...] = total[...].astype(out_ref.dtype)

    return pl.pallas_call(
        body,
        name="first_piece",
        grid_spec=pltpu.PrefetchScalarGridSpec(
            num_scalar_prefetch=1,
            grid=(steps,),
            in_specs=[
                pl.BlockSpec((rows, depth), lambda k, c: (0, k)),
                pl.BlockSpec((depth, 2, chunk), lambda k, c: (k, 0, c[0])),
            ],
            out_specs=[
                pl.BlockSpec((depth, 2 * chunk), lambda k, c: (k, 0)),
                pl.BlockSpec((rows, 2 * chunk), lambda k, c: (0, 0)),
            ],
            scratch_shapes=[pltpu.VMEM((rows, 2 * chunk), jnp.float32)],
        ),
        out_shape=[
            jax.ShapeDtypeStruct((width, 2 * chunk), jnp.bfloat16),
            jax.ShapeDtypeStruct((rows, 2 * chunk), jnp.bfloat16),
        ],
        compiler_params=params(),
        cost_estimate=estimate(5.5),
    )(which, hidden, weight)


def row_outputs(cuts, block, columns):
    specs, shapes, places = [], [], []
    first = 0
    for rows in cuts:
        count = rows // block

        def index(i, first=first, count=count):
            return jnp.clip(i - first, 0, count - 1), 0

        specs.append((block, columns, index))
        shapes.append(jax.ShapeDtypeStruct((rows, columns), jnp.bfloat16))
        places.append((first, first + count))
        first += count
    return specs, shapes, places


def more_rows(hidden, flat, start, cuts, after):
    width, columns = flat.shape
    block = 512
    skip = start // block
    specs, shapes, places = row_outputs(cuts, block, columns)

    def body(hidden_ref, flat_ref, *refs):
        i = pl.program_id(0)
        value = jnp.dot(hidden_ref[...], flat_ref[...], preferred_element_type=jnp.float32).astype(jnp.bfloat16)
        for ref, (low, high) in zip(refs[len(after) :], places):

            @pl.when((i >= low) & (i < high))
            def _(ref=ref):
                ref[...] = value

    return pl.pallas_call(
        body,
        name="more_rows",
        grid=(sum(cuts) // block,),
        in_specs=[
            pl.BlockSpec((block, width), lambda i: (skip + i, 0)),
            pl.BlockSpec((width, columns), lambda i: (0, 0)),
        ]
        + [HERE] * len(after),
        out_specs=[pl.BlockSpec((b, c), index) for b, c, index in specs],
        out_shape=shapes,
        compiler_params=params(),
        cost_estimate=estimate(2.5 * sum(cuts) / block),
    )(hidden, flat, *after)


def other_slots(hidden, weight, which, cuts, chunk, after):
    tok_rows, width = hidden.shape
    count = len(cuts)
    steps = 4
    depth = width // steps
    block = 512
    out_specs, out_shapes, targets = [], [], []
    for slot_cuts in cuts:
        specs, shapes, places = row_outputs(slot_cuts, block, 2 * chunk)
        targets.append([(len(out_specs) + k, place) for k, place in enumerate(places)])
        for b, c, index in specs:
            out_specs.append(pl.BlockSpec((b, c), lambda i, w, index=index: index(i - steps)))
        out_shapes += shapes

    def body(which_ref, hidden_ref, *refs):
        weight_refs = refs[:count]
        outs = refs[count + len(after) : -1]
        flat = refs[-1]
        i = pl.program_id(0)

        @pl.when(i < steps)
        def _():
            for s in range(count):
                flat[s, pl.ds(pl.multiple_of(i * depth, depth), depth), :] = weight_refs[s][...].reshape(
                    depth, 2 * chunk
                )

        @pl.when(i >= steps)
        def _():
            for s in range(count):
                value = jnp.dot(hidden_ref[...], flat[s], preferred_element_type=jnp.float32).astype(jnp.bfloat16)
                for k, (low, high) in targets[s]:

                    @pl.when((i >= steps + low) & (i < steps + high))
                    def _(k=k, value=value):
                        outs[k][...] = value

    arrays = pl.pallas_call(
        body,
        name="other_slots",
        grid_spec=pltpu.PrefetchScalarGridSpec(
            num_scalar_prefetch=1,
            grid=(steps + tok_rows // block,),
            in_specs=[pl.BlockSpec((block, width), lambda i, w: (jnp.maximum(i - steps, 0), 0))]
            + [
                pl.BlockSpec((depth, 2, chunk), lambda i, w, s=s: (jnp.minimum(i, steps - 1), 0, w[s]))
                for s in range(count)
            ]
            + [HERE] * len(after),
            out_specs=out_specs,
            scratch_shapes=[pltpu.VMEM((count, width, 2 * chunk), jnp.bfloat16)],
        ),
        out_shape=out_shapes,
        compiler_params=params(),
        cost_estimate=estimate(8 + 1.3 * count * tok_rows / block),
    )(which, hidden, *[weight] * count, *after)
    return [[arrays[k] for k, _ in target] for target in targets]


def segment_specs(terms, start, block):
    specs, operands, layout = [], [], []
    for term in terms:
        places = []
        for first, array in term:
            count = array.shape[0] // block
            places.append((len(operands), (first - start) // block))
            operands.append(array)

            def index(i, *_, shift=(first - start) // block, count=count):
                return jnp.clip(i - shift, 0, count - 1), 0

            specs.append(pl.BlockSpec((block, array.shape[1]), index))
        layout.append(places)
    return specs, operands, layout


def term_sum(i, refs, layout):
    total = None
    for places in layout:
        value = refs[places[0][0]][...].astype(jnp.float32)
        for place, shift in places[1:]:
            value = jnp.where(i >= shift, refs[place][...].astype(jnp.float32), value)
        total = value if total is None else total + value
    return total


def added(start, rows, terms, after):
    columns = terms[0][0][1].shape[1]
    block = 512 if columns > 128 else rows
    specs, operands, layout = segment_specs(terms, start, block)

    def body(*refs):
        refs[-1][...] = term_sum(pl.program_id(0), refs, layout).astype(jnp.bfloat16)

    return pl.pallas_call(
        body,
        name="added",
        grid=(rows // block,),
        in_specs=specs + [HERE] * len(after),
        out_specs=pl.BlockSpec((block, columns), lambda i: (i, 0)),
        out_shape=jax.ShapeDtypeStruct((rows, columns), jnp.bfloat16),
        compiler_params=params(),
        cost_estimate=estimate(1.3 * rows * columns / 262144),
    )(*operands, *after)


def low_terms(hidden, down_maps, tenants, after):
    tok_rows, width = hidden.shape
    count = tenants.shape[0]
    rows = tok_rows // count
    columns = down_maps.shape[2]
    per = 4 if count % 4 == 0 else 1

    def body(tenant_ref, hidden_ref, *refs):
        for k in range(per):
            part = slice(k * rows, (k + 1) * rows)
            refs[-1][part, :] = jnp.dot(
                hidden_ref[part, :], refs[k][0], preferred_element_type=jnp.float32
            ).astype(jnp.bfloat16)

    return pl.pallas_call(
        body,
        name="low_terms",
        grid_spec=pltpu.PrefetchScalarGridSpec(
            num_scalar_prefetch=1,
            grid=(count // per,),
            in_specs=[pl.BlockSpec((per * rows, width), lambda b, t: (b, 0))]
            + [
                pl.BlockSpec((1, width, columns), lambda b, t, k=k: (t[b * per + k], 0, 0))
                for k in range(per)
            ]
            + [HERE] * len(after),
            out_specs=pl.BlockSpec((per * rows, columns), lambda b, t: (b, 0)),
        ),
        out_shape=jax.ShapeDtypeStruct((tok_rows, columns), jnp.bfloat16),
        compiler_params=params(),
        cost_estimate=estimate(8.6),
    )(tenants, hidden, *[down_maps] * per, *after)


def with_adapter(start, rows, terms, low_parts, up_maps, tenants, after):
    rank, chunk = up_maps.shape[2:]
    blk_rows = low_parts[0].shape[0] // tenants.shape[0]
    block = 512
    per = block // blk_rows
    skip = start // block
    specs, operands, layout = segment_specs(terms, start, block)
    n_low = len(low_parts)

    def body(tenant_ref, *refs):
        up_refs, low_refs, term_refs = refs[:per], refs[per : per + n_low], refs[per + n_low :]
        low = low_refs[0][...].astype(jnp.float32)
        for ref in low_refs[1:]:
            low = low + ref[...].astype(jnp.float32)
        low = low.astype(jnp.bfloat16)
        total = term_sum(pl.program_id(0), term_refs, layout)
        for k in range(per):
            part = slice(k * blk_rows, (k + 1) * blk_rows)
            for h in range(2):
                columns = slice(h * chunk, (h + 1) * chunk)
                adapt = jnp.dot(
                    low[part, h * rank : (h + 1) * rank], up_refs[k][0, h], preferred_element_type=jnp.float32
                )
                refs[-1][part, columns] = (total[part, columns] + adapt).astype(jnp.bfloat16)

    return pl.pallas_call(
        body,
        name="with_adapter",
        grid_spec=pltpu.PrefetchScalarGridSpec(
            num_scalar_prefetch=1,
            grid=(rows // block,),
            in_specs=[
                pl.BlockSpec((1, 2, rank, chunk), lambda b, t, k=k: (t[(skip + b) * per + k], 0, 0, 0))
                for k in range(per)
            ]
            + [pl.BlockSpec((block, 2 * rank), lambda b, t: (skip + b, 0)) for _ in low_parts]
            + specs
            + [HERE] * len(after),
            out_specs=pl.BlockSpec((block, 2 * chunk), lambda b, t: (b, 0)),
        ),
        out_shape=jax.ShapeDtypeStruct((rows, 2 * chunk), jnp.bfloat16),
        compiler_params=params(),
        cost_estimate=estimate(2 * rows / block),
    )(tenants, *[up_maps] * per, *low_parts, *operands, *after)


def finish(start, rows, out_rows, terms, previous):
    chunk = terms[0][0][1].shape[1] // 2
    block = 512
    skip = start // block
    specs, operands, layout = segment_specs(terms, start, block)
    aliases = {}
    if previous is not None:
        aliases = {len(operands): 0}
        specs.append(HERE)
        operands.append(previous)

    def body(*refs):
        total = term_sum(pl.program_id(0), refs, layout)
        refs[-1][...] = total.astype(jnp.bfloat16).reshape(block, 2, chunk)

    return pl.pallas_call(
        body,
        name="finish",
        grid=(rows // block,),
        in_specs=specs,
        out_specs=pl.BlockSpec((block, 2, chunk), lambda i: (skip + i, 0, 0)),
        out_shape=jax.ShapeDtypeStruct((out_rows, 2, chunk), jnp.bfloat16),
        input_output_aliases=aliases,
        compiler_params=params(),
        cost_estimate=estimate(1.3 * rows / block),
    )(*operands)


def local(n, hidden, key_value_weight, adapter_down_weight, adapter_up_weight, tenant_per_block):
    tok_rows, local_width = hidden.shape
    chunk = adapter_up_weight.shape[3]
    unit = tok_rows // UNITS
    slots, sends = line_plan(n)

    down_maps = lax.all_gather(adapter_down_weight, "tok", axis=0, tiled=True)
    up_maps = lax.all_gather(adapter_up_weight, "tok", axis=0, tiled=True)

    which = by_device(slots, "tp")
    partial = {}
    received = {}
    last = []

    def pick(segments, start, rows):
        return [(f, a) for f, a in segments if f < start + rows and start < f + a.shape[0]]

    def ordered(array):
        last[:] = [array]
        return array

    def cut(arrays, start=0):
        segments = []
        for array in arrays:
            segments.append((start, array))
            start += array.shape[0]
        return segments

    def send(time, parity, u, count, after=(), again=False):
        start, rows = u * unit, count * unit
        ks = sorted({k for _, _, k in sends[time, parity]})
        earlier = pick(received.get((time - 1, 1 - parity), []), start, rows)
        own = pick(partial[ks[0]], start, rows)
        if len(ks) > 1:
            table = np.zeros((n,), np.int32)
            for i, _, k in sends[time, parity]:
                table[i] = k
            mine = by_device(table, "tp")
            ((_, value),) = own
            for k in ks[1:]:
                ((_, other),) = pick(partial[k], start, rows)
                value = jnp.where(mine == k, other, value)
            own = [(start, value)]
        if earlier or again:
            terms = [own, earlier] if earlier else [own]
            value = ordered(added(start, rows, terms, last + list(after)))
        else:
            ((_, value),) = own
        moves = [(i, to) for i, to, _ in sends[time, parity]]
        with jax.named_scope(f"{'odd' if parity else 'even'}{time}_units{u}"):
            moved = lax.ppermute(value, "tp", moves)
        received.setdefault((time, parity), []).append((start, moved))
        return received[time, parity][-1][1]

    low_parts = []

    def send_low(time):
        value = low_parts[0]
        if time > 1:
            value = ordered(added(0, tok_rows, [[(0, value)], [(0, low_parts[-1])]], list(last)))
        with jax.named_scope(f"low_sums{time}"):
            low_parts.append(lax.ppermute(value, "tp", [(time - 1, time), (n - time, n - time - 1)]))

    ready = []

    def prepare(u, count):
        start, rows = u * unit, count * unit
        terms = [pick(partial[n - 1], start, rows), pick(received[n - 1, 1], start, rows)]
        value = with_adapter(start, rows, terms, low_parts, up_maps, tenant_per_block, list(last))
        ready.append((start, ordered(value)))

    result = [None]

    def complete(u, count):
        start, rows = u * unit, count * unit
        terms = [pick(ready, start, rows), pick(received[n - 1, 0], start, rows)]
        result[0] = finish(start, rows, tok_rows, terms, result[0])

    half = UNITS // 2
    flat, head = first_piece(hidden, key_value_weight, which[:1], half * unit, chunk)
    partial[0] = [(0, head)]
    if n == 4:
        send(1, 0, 0, 2)
        partial[0] += cut(more_rows(hidden, flat, half * unit, [half * unit], []), half * unit)
        send(1, 0, 2, 2)
        others = other_slots(
            hidden, key_value_weight, which[1:], [[2 * unit, 2 * unit], [tok_rows], [tok_rows]], chunk, [partial[0][1][1]]
        )
        for s, arrays in enumerate(others):
            partial[s + 1] = cut(arrays)
        ordered(partial[3][0][1])
        send(2, 0, 0, 2)
        send(2, 1, 0, 2)
        send(2, 1, 2, 2)
        low_parts.append(ordered(low_terms(hidden, down_maps, tenant_per_block, list(last))))
        send_low(1)
        send(2, 0, 2, 2, again=True)
        send(3, 1, 0, 2)
        send(3, 0, 0, 2)
        send_low(2)
        send(3, 0, 2, 1)
        send_low(3)
        send(3, 1, 2, 2)
        send(3, 0, 3, 1)
        prepare(0, 2)
        complete(0, 2)
        prepare(2, 2)
        complete(2, 1)
        complete(3, 1)
    else:
        partial[0] = [
            (0, jnp.concatenate([head] + list(more_rows(hidden, flat, half * unit, [half * unit], []))))
        ]
        others = other_slots(hidden, key_value_weight, which[1:], [[tok_rows]] * (n - 1), chunk, [head])
        for s, arrays in enumerate(others):
            partial[s + 1] = cut(arrays)
        ordered(head)
        for time in range(1, n):
            for parity in (0, 1):
                if (time, parity) in sends:
                    send(time, parity, 0, UNITS)
        low_parts.append(ordered(low_terms(hidden, down_maps, tenant_per_block, list(last))))
        for time in range(1, n):
            send_low(time)
        prepare(0, UNITS)
        complete(0, UNITS)
    return result[0]


def solution(mesh):
    n = mesh.shape["tp"]
    in_specs = (
        P("tok", "tp"),
        P("tp", None, None),
        P("tok", "tp", None),
        P("tok", None, None, "tp"),
        P("tok"),
    )
    out_specs = P("tok", None, "tp")

    def run(*args):
        return local(n, *args)

    return jax.shard_map(run, mesh=mesh, in_specs=in_specs, out_specs=out_specs, check_vma=False)
```

time: 304 us -> 178 us (0.59)
  waiting for transfers between devices: 203 us -> 25.1 us
  Pallas kernels: 0 us -> 84.7 us
  starting transfers between devices: 0.3 us -> 48.5 us
  local copies, waits for them, and re-layouts: 48.2 us -> 4.24 us
  matrix products: 35.2 us -> 0 us
  other arithmetic: 3.35 us -> 0 us
    reduce_scatter x1 -> x0, waiting for transfers between devices: 143 us -> none  [local(): lax.psum_scatter(partial_value.reshape(tok_rows, 2, -1).astype(jnp.bfloat...]
    pallas_call x0 -> x19, Pallas kernels: none -> 84.7 us  [the longest x1 24.2 us: other_slots(): pl.pallas_call(body, name='other_slots', grid_spec=pltpu.PrefetchScalarGr...]
    ppermute x0 -> x14, starting transfers between devices: none -> 48.4 us  [the longest x11 40.2 us: send(): moved = lax.ppermute(value, 'tp', moves)]
    all_gather x2, waiting for transfers between devices: 36.4 us -> 0.01 us  [the longest x1 0.01 us: local(): down_maps = lax.all_gather(adapter_down_weight, 'tok', axis=0, tiled=True)]
    dot_general x3 -> x0, matrix products: 35.2 us -> none  [the longest x1 23.9 us: local(): jnp.dot(hidden, key_value_weight.reshape(local_width, -1), preferred_elem...]
    ppermute x0 -> x14, waiting for transfers between devices: none -> 24.4 us  [the longest x11 18.9 us: send(): moved = lax.ppermute(value, 'tp', moves)]
    psum x1 -> x0, waiting for transfers between devices: 22.4 us -> none  [local(): low = lax.psum(low.astype(jnp.bfloat16), 'tp')]
    convert_element_type x2 -> x0, local copies, waits for them, and re-layouts: 16.3 us -> none  [the longest x1 14 us: local(): return total.astype(jnp.bfloat16)]
  transfers between devices with their start and end apart: 4 -> 16, of which waited for: 3 -> 5; matrix products, arithmetic and copies ran while one was open for 23% -> 1% of each run, Pallas kernels for 0% -> 47%
where the time goes in v1:
time: 178 us; the launch traced here: 176 us
  Pallas kernels  84.7 us (48%)
  starting transfers between devices  48.5 us (27%)
  waiting for transfers between devices  25.1 us (14%)
  between operations  13.5 us (8%)
  local copies, waits for them, and re-layouts  4.24 us (2%)
    ppermute x11, starting transfers between devices, send(): moved = lax.ppermute(value, 'tp', moves)  40.2 us
    pallas_call x1, Pallas kernels, other_slots(): pl.pallas_call(body, name='other_slots', grid_spec=pltpu.PrefetchScalarGr...  24.2 us
    pallas_call x10, Pallas kernels, added(): pl.pallas_call(body, name='added', grid=(rows // block,), in_specs=specs...  23 us
    ppermute x11, waiting for transfers between devices, send(): moved = lax.ppermute(value, 'tp', moves)  18.9 us
    pallas_call x1, Pallas kernels, low_terms(): pl.pallas_call(body, name='low_terms', grid_spec=pltpu.PrefetchScalarGrid...  9.15 us
    ppermute x3, starting transfers between devices, send_low(): lax.ppermute(value, 'tp', [(time - 1, time), (n - time, n - time - 1)])  8.23 us
    pallas_call x2, Pallas kernels, with_adapter(): pl.pallas_call(body, name='with_adapter', grid_spec=pltpu.PrefetchScalarG...  7.93 us
    pallas_call x3, Pallas kernels, finish(): pl.pallas_call(body, name='finish', grid=(rows // block,), in_specs=specs...  7.81 us
  transfers between devices with their start and end apart: 16, of which 5 were waited for; matrix products, arithmetic and copies ran while one was open for 1% of the time, Pallas kernels for 47%

profile of v1, /device:TPU:0, one launch (start us, length us, event | category | flops | bytes accessed | tf_op | source)
XLA Modules:
  0.0 176.0 jit_solution(8443216281502059837)
XLA Ops:
  6.5 0.7 all-gather.5.cloned.1.call-update
  7.3 0.0 all-gather.3.cloned.1.call-start
  7.3 1.2 constant_dynamic-slice_fusion
  8.5 7.0 %first_piece.1 = (bf16[2048,512]{1,0:T(8,128)(2,1)}, bf16[1024,512]{1,0:T(8,128)(2,1)}) custom-call(s32[1]{0:T(128)} %bitcast.4, bf16[2048,2048]{1,0:T(8,128)(2,1)} %hidden_ref.7, bf16[2048,2,1024]{2,1,0:T(2,128)(2,1)} %refs_2_.1), custom_call_target="tpu_custom_call" | custom-call | flops 1 | bytes 5073750 | tf_op jit(solution)/shard_map/first_piece/pallas_call | solution.py:71
  15.5 5.9 %collective-permute-start.1 = (bf16[1024,512]{1,0:T(8,128)(2,1)}, bf16[1024,512]{1,0:T(8,128)(2,1)}, u32[]{:S(2)}, u32[]{:S(2)}) collective-permute-start(bf16[1024,512]{1,0:T(8,128)(2,1)} %get-tuple-element.12.refs_0_), channel_id=1, source_target_pairs={{0,1},{3,2},{4,5},{7,6},{8,9},{11,10},{12,13},{15,14},{16,17},{19,... | collective-permute-start | bytes 3145736 | tf_op jit(solution)/shard_map/even1_units0/ppermute | solution.py:407
  21.4 5.6 %more_rows.1.refs_3_.refs_0_ = bf16[1024,512]{1,0:T(8,128)(2,1)} custom-call(bf16[2048,2048]{1,0:T(8,128)(2,1)} %hidden_ref.7, bf16[2048,512]{1,0:T(8,128)(2,1)} %get-tuple-element.11.flat_ref), custom_call_target="tpu_custom_call" | custom-call | flops 1 | bytes 4612500 | tf_op jit(solution)/shard_map/more_rows/pallas_call | solution.py:127
  27.0 2.3 %collective-permute-start = (bf16[1024,512]{1,0:T(8,128)(2,1)}, bf16[1024,512]{1,0:T(8,128)(2,1)}, u32[]{:S(2)}, u32[]{:S(2)}) collective-permute-start(bf16[1024,512]{1,0:T(8,128)(2,1)} %more_rows.1.refs_3_.refs_0_), channel_id=1, source_target_pairs={{0,1},{3,2},{4,5},{7,6},{8,9},{11,10},{12,13},{15,14},{16,17},{19,... | collective-permute-start | bytes 3145736 | tf_op jit(solution)/shard_map/even1_units2/ppermute | solution.py:407
  29.3 0.6 slice_bitcast_fusion.which_ref
  29.9 24.2 %other_slots.1 = (bf16[1024,512]{1,0:T(8,128)(2,1)}, bf16[1024,512]{1,0:T(8,128)(2,1)}, bf16[2048,512]{1,0:T(8,128)(2,1)}, bf16[2048,512]{1,0:T(8,128)(2,1)}) custom-call(s32[3]{0:T(128)} %slice_bitcast_fusion.which_ref, bf16[2048,2048]{1,0:T(8,128)(2,1)} %hidden_ref.7, bf16[2048,2,1024]{2,1,0:T(2,128)(2,1)} %refs_2_.1, bf16[2048,2,1024]{2,1,0:T(2,128)(2,1)} %refs_2_.1, ...), custom_call_target="tpu_custom_call" | custom-call | flops 1 | bytes 21771000 | tf_op jit(solution)/shard_map/other_slots/pallas_call | solution.py:180
  54.1 2.3 %collective-permute-start.4 = (bf16[1024,512]{1,0:T(8,128)(2,1)}, bf16[1024,512]{1,0:T(8,128)(2,1)}, u32[]{:S(2)}, u32[]{:S(2)}) collective-permute-start(bf16[1024,512]{1,0:T(8,128)(2,1)} %get-tuple-element.15.refs_0_), channel_id=1, source_target_pairs={{0,1},{3,2},{4,5},{7,6},{8,9},{11,10},{12,13},{15,14},{16,17},{19,... | collective-permute-start | bytes 3145736 | tf_op jit(solution)/shard_map/even2_units0/ppermute | solution.py:407
  56.4 2.5 %added.10.refs_2_ = bf16[1024,512]{1,0:T(8,128)(2,1)} custom-call(bf16[1024,512]{1,0:T(8,128)(2,1)} %get-tuple-element.12.refs_0_, bf16[1024,512]{1,0:T(8,128)(2,1)} %collective-permute-done.1.refs_1_, bf16[2048,512]{1,0:T(8,128)(2,1)} %get-tuple-element.13.refs_2_.refs_8_), custom_call_target="tpu_custom_call" | custom-call | flops 1 | bytes 2398500 | tf_op jit(solution)/shard_map/added/pallas_call | solution.py:237
  58.9 1.7 collective-permute-start.3
  60.5 6.2 %collective-permute-done.refs_1_ = bf16[1024,512]{1,0:T(8,128)(2,1)} collective-permute-done((bf16[1024,512]{1,0:T(8,128)(2,1)}, bf16[1024,512]{1,0:T(8,128)(2,1)}, u32[]{:S(2)}, u32[]{:S(2)}) %collective-permute-start) | collective-permute-done | bytes 1048608 | tf_op jit(solution)/shard_map/even1_units2/ppermute | solution.py:407
  66.7 2.4 %added.11.refs_4_ = bf16[1024,512]{1,0:T(8,128)(2,1)} custom-call(bf16[1024,512]{1,0:T(8,128)(2,1)} %more_rows.1.refs_3_.refs_0_, bf16[1024,512]{1,0:T(8,128)(2,1)} %collective-permute-done.refs_1_, bf16[1024,512]{1,0:T(8,128)(2,1)} %added.10.refs_2_), custom_call_target="tpu_custom_call" | custom-call | flops 1 | bytes 2398500 | tf_op jit(solution)/shard_map/added/pallas_call | solution.py:237
  69.2 1.7 collective-permute-start.6
  70.8 9.2 %low_terms.1.refs_1_.refs_0_.refs_4_ = bf16[2048,128]{1,0:T(8,128)(2,1)} custom-call(s32[16]{0:T(128)} %tenant_ref.5, bf16[2048,2048]{1,0:T(8,128)(2,1)} %hidden_ref.7, bf16[16,2048,128]{2,1,0:T(8,128)(2,1)} %all-gather.5.cloned.1.call-done.refs_0_.refs_1_.refs_2_.refs_3_, ...), custom_call_target="tpu_custom_call" | custom-call | flops 1 | bytes 7933500 | tf_op jit(solution)/shard_map/low_terms/pallas_call | solution.py:263
  80.0 6.3 %collective-permute-start.2 = (bf16[2048,128]{1,0:T(8,128)(2,1)}, bf16[2048,128]{1,0:T(8,128)(2,1)S(1)}, u32[]{:S(2)}, u32[]{:S(2)}) collective-permute-start(bf16[2048,128]{1,0:T(8,128)(2,1)} %low_terms.1.refs_1_.refs_0_.refs_4_), channel_id=1, source_target_pairs={{0,1},{3,2},{4,5},{7,6},{8,9},{11,10},{12,13},{15,14},{16,17},{19,... | collective-permute-start | bytes 1572872 | tf_op jit(solution)/shard_map/low_sums1/ppermute | solution.py:418
  86.3 2.1 %added.12.refs_2_ = bf16[1024,512]{1,0:T(8,128)(2,1)} custom-call(bf16[1024,512]{1,0:T(8,128)(2,1)} %get-tuple-element.16.refs_0_, bf16[2048,128]{1,0:T(8,128)(2,1)} %low_terms.1.refs_1_.refs_0_.refs_4_), custom_call_target="tpu_custom_call" | custom-call | flops 1 | bytes 2398500 | tf_op jit(solution)/shard_map/added/pallas_call | solution.py:237
  88.3 2.3 %collective-permute-start.8 = (bf16[1024,512]{1,0:T(8,128)(2,1)}, bf16[1024,512]{1,0:T(8,128)(2,1)}, u32[]{:S(2)}, u32[]{:S(2)}) collective-permute-start(bf16[1024,512]{1,0:T(8,128)(2,1)} %added.12.refs_2_), channel_id=1, source_target_pairs={{0,1},{3,2},{4,5},{7,6},{8,9},{11,10},{12,13},{15,14},{16,17},{19,... | collective-permute-start | bytes 3145736 | tf_op jit(solution)/shard_map/even2_units2/ppermute | solution.py:407
  90.6 0.0 all-gather.3.cloned.1.call-update
  90.7 0.0 collective-permute-done.4.refs_1_
  90.7 2.5 %added.13.refs_2_ = bf16[1024,512]{1,0:T(8,128)(2,1)} custom-call(bf16[1024,512]{1,0:T(8,128)(2,1)} %get-tuple-element.15.refs_0_, bf16[1024,512]{1,0:T(8,128)(2,1)} %collective-permute-done.4.refs_1_, bf16[1024,512]{1,0:T(8,128)(2,1)} %added.12.refs_2_), custom_call_target="tpu_custom_call" | custom-call | flops 1 | bytes 2398500 | tf_op jit(solution)/shard_map/added/pallas_call | solution.py:237
  93.1 2.5 %added.14.refs_2_ = bf16[1024,512]{1,0:T(8,128)(2,1)} custom-call(bf16[2048,512]{1,0:T(8,128)(2,1)} %get-tuple-element.14.refs_0_, bf16[1024,512]{1,0:T(8,128)(2,1)} %collective-permute-done.3.refs_1_, bf16[1024,512]{1,0:T(8,128)(2,1)} %added.13.refs_2_), custom_call_target="tpu_custom_call" | custom-call | flops 1 | bytes 2398500 | tf_op jit(solution)/shard_map/added/pallas_call | solution.py:237
  95.6 4.9 %collective-permute-done.2.refs_1_.refs_5_ = bf16[2048,128]{1,0:T(8,128)(2,1)S(1)} collective-permute-done((bf16[2048,128]{1,0:T(8,128)(2,1)}, bf16[2048,128]{1,0:T(8,128)(2,1)S(1)}, u32[]{:S(2)}, u32[]{:S(2)}) %collective-permute-start.2) | collective-permute-done | bytes 524320 | tf_op jit(solution)/shard_map/low_sums1/ppermute | solution.py:418
  100.4 0.8 copy-done
  101.2 2.2 %added.15.refs_2_ = bf16[2048,128]{1,0:T(8,128)(2,1)} custom-call(bf16[2048,128]{1,0:T(8,128)(2,1)} %low_terms.1.refs_1_.refs_0_.refs_4_, bf16[2048,128]{1,0:T(8,128)(2,1)} %copy-done, bf16[1024,512]{1,0:T(8,128)(2,1)} %added.14.refs_2_), custom_call_target="tpu_custom_call" | custom-call | flops 1 | bytes 1199250 | tf_op jit(solution)/shard_map/added/pallas_call | solution.py:237
  103.4 0.7 collective-permute-start.5
  104.1 1.7 collective-permute-start.10
  105.8 5.9 %collective-permute-start.13 = (bf16[1024,512]{1,0:T(8,128)(2,1)}, bf16[1024,512]{1,0:T(8,128)(2,1)}, u32[]{:S(2)}, u32[]{:S(2)}) collective-permute-start(bf16[1024,512]{1,0:T(8,128)(2,1)} %added.14.refs_2_), channel_id=1, source_target_pairs={{0,1},{1,0},{2,3},{3,2},{4,5},{5,4},{6,7},{7,6},{8,9},{9,8},{10,11... | collective-permute-start | bytes 3145736 | tf_op jit(solution)/shard_map/even3_units0/ppermute | solution.py:407
  111.7 0.0 collective-permute-done.6.refs_1_
  111.7 2.2 %added.16.refs_2_ = bf16[512,512]{1,0:T(8,128)(2,1)} custom-call(bf16[2048,512]{1,0:T(8,128)(2,1)} %get-tuple-element.14.refs_0_, bf16[1024,512]{1,0:T(8,128)(2,1)} %collective-permute-done.6.refs_1_, bf16[2048,128]{1,0:T(8,128)(2,1)} %added.15.refs_2_), custom_call_target="tpu_custom_call" | custom-call | flops 1 | bytes 1199250 | tf_op jit(solution)/shard_map/added/pallas_call | solution.py:237
  113.9 0.9 copy-done.1
  114.8 2.1 %added.17.refs_2_ = bf16[2048,128]{1,0:T(8,128)(2,1)} custom-call(bf16[2048,128]{1,0:T(8,128)(2,1)} %low_terms.1.refs_1_.refs_0_.refs_4_, bf16[2048,128]{1,0:T(8,128)(2,1)} %copy-done.1, bf16[512,512]{1,0:T(8,128)(2,1)} %added.16.refs_2_), custom_call_target="tpu_custom_call" | custom-call | flops 1 | bytes 1199250 | tf_op jit(solution)/shard_map/added/pallas_call | solution.py:237
  116.9 6.0 %collective-permute-done.8.refs_1_ = bf16[1024,512]{1,0:T(8,128)(2,1)} collective-permute-done((bf16[1024,512]{1,0:T(8,128)(2,1)}, bf16[1024,512]{1,0:T(8,128)(2,1)}, u32[]{:S(2)}, u32[]{:S(2)}) %collective-permute-start.8) | collective-permute-done | bytes 1048608 | tf_op jit(solution)/shard_map/even2_units2/ppermute | solution.py:407
  122.9 2.4 %added.18.refs_2_ = bf16[1024,512]{1,0:T(8,128)(2,1)} custom-call(bf16[1024,512]{1,0:T(8,128)(2,1)} %get-tuple-element.16.refs_0_, bf16[1024,512]{1,0:T(8,128)(2,1)} %collective-permute-done.8.refs_1_, bf16[2048,128]{1,0:T(8,128)(2,1)} %added.17.refs_2_), custom_call_target="tpu_custom_call" | custom-call | flops 1 | bytes 2398500 | tf_op jit(solution)/shard_map/added/pallas_call | solution.py:237
  125.3 1.7 collective-permute-start.9
  127.0 1.3 collective-permute-start.7
  128.3 4.7 %collective-permute-start.12 = (bf16[512,512]{1,0:T(8,128)(2,1)}, bf16[512,512]{1,0:T(8,128)(2,1)}, u32[]{:S(2)}, u32[]{:S(2)}) collective-permute-start(bf16[512,512]{1,0:T(8,128)(2,1)} %added.16.refs_2_), channel_id=1, source_target_pairs={{0,1},{1,0},{2,3},{3,2},{4,5},{5,4},{6,7},{7,6},{8,9},{9,8},{10,11... | collective-permute-start | bytes 1572872 | tf_op jit(solution)/shard_map/even3_units2/ppermute | solution.py:407
  133.0 2.1 %added.19.refs_10_ = bf16[512,512]{1,0:T(8,128)(2,1)} custom-call(bf16[2048,512]{1,0:T(8,128)(2,1)} %get-tuple-element.14.refs_0_, bf16[1024,512]{1,0:T(8,128)(2,1)} %collective-permute-done.6.refs_1_, bf16[1024,512]{1,0:T(8,128)(2,1)} %added.18.refs_2_), custom_call_target="tpu_custom_call" | custom-call | flops 1 | bytes 1199250 | tf_op jit(solution)/shard_map/added/pallas_call | solution.py:237
  135.2 10.1 %collective-permute-start.11 = (bf16[512,512]{1,0:T(8,128)(2,1)}, bf16[512,512]{1,0:T(8,128)(2,1)}, u32[]{:S(2)}, u32[]{:S(2)}) collective-permute-start(bf16[512,512]{1,0:T(8,128)(2,1)} %added.19.refs_10_), channel_id=1, source_target_pairs={{0,1},{1,0},{2,3},{3,2},{4,5},{5,4},{6,7},{7,6},{8,9},{9,8},{10,11... | collective-permute-start | bytes 1572872 | tf_op jit(solution)/shard_map/even3_units3/ppermute | solution.py:407
  145.3 0.6 collective-permute-done.7.refs_7_
  146.0 0.8 copy-done.2
  146.8 4.0 %with_adapter.2.refs_10_.refs_0_ = bf16[1024,512]{1,0:T(8,128)(2,1)} custom-call(s32[16]{0:T(128)} %tenant_ref.5, bf16[16,2,64,256]{3,2,1,0:T(8,128)(2,1)} %all-gather.3.cloned.1.call-done.refs_0_.refs_1_.refs_2_.refs_3_, bf16[16,2,64,256]{3,2,1,0:T(8,128)(2,1)} %all-gather.3.cloned.1.call-done.refs_0_.refs_1_.refs_2_.refs_3_, ...), custom_call_target="tpu_custom_call" | custom-call | flops 1 | bytes 3690000 | tf_op jit(solution)/shard_map/with_adapter/pallas_call | solution.py:308
  150.7 2.9 %finish.3.refs_2_ = bf16[2048,2,256]{2,1,0:T(2,128)(2,1)} custom-call(bf16[1024,512]{1,0:T(8,128)(2,1)} %with_adapter.2.refs_10_.refs_0_, bf16[1024,512]{1,0:T(8,128)(2,1)} %collective-permute-done.13.refs_1_), custom_call_target="tpu_custom_call" | custom-call | flops 1 | bytes 2398500 | tf_op jit(solution)/shard_map/finish/pallas_call | solution.py:344
  153.7 4.0 %with_adapter.3.refs_0_ = bf16[1024,512]{1,0:T(8,128)(2,1)} custom-call(s32[16]{0:T(128)} %tenant_ref.5, bf16[16,2,64,256]{3,2,1,0:T(8,128)(2,1)} %all-gather.3.cloned.1.call-done.refs_0_.refs_1_.refs_2_.refs_3_, bf16[16,2,64,256]{3,2,1,0:T(8,128)(2,1)} %all-gather.3.cloned.1.call-done.refs_0_.refs_1_.refs_2_.refs_3_, ...), custom_call_target="tpu_custom_call" | custom-call | flops 1 | bytes 3690000 | tf_op jit(solution)/shard_map/with_adapter/pallas_call | solution.py:308
  157.6 2.4 %finish.4.refs_2_ = bf16[2048,2,256]{2,1,0:T(2,128)(2,1)} custom-call(bf16[1024,512]{1,0:T(8,128)(2,1)} %with_adapter.3.refs_0_, bf16[512,512]{1,0:T(8,128)(2,1)} %collective-permute-done.12.refs_1_, bf16[2048,2,256]{2,1,0:T(2,128)(2,1)} %finish.3.refs_2_), custom_call_target="tpu_custom_call", output_to_operand_aliasing={{}: (2, {})} | custom-call | flops 1 | bytes 1199250 | tf_op jit(solution)/shard_map/finish/pallas_call | solution.py:344
  160.1 6.6 %collective-permute-done.11.refs_1_ = bf16[512,512]{1,0:T(8,128)(2,1)} collective-permute-done((bf16[512,512]{1,0:T(8,128)(2,1)}, bf16[512,512]{1,0:T(8,128)(2,1)}, u32[]{:S(2)}, u32[]{:S(2)}) %collective-permute-start.11) | collective-permute-done | bytes 524320 | tf_op jit(solution)/shard_map/even3_units3/ppermute | solution.py:407
  166.7 2.4 %finish.5 = bf16[2048,2,256]{2,1,0:T(2,128)(2,1)} custom-call(bf16[1024,512]{1,0:T(8,128)(2,1)} %with_adapter.3.refs_0_, bf16[512,512]{1,0:T(8,128)(2,1)} %collective-permute-done.11.refs_1_, bf16[2048,2,256]{2,1,0:T(2,128)(2,1)} %finish.4.refs_2_), custom_call_target="tpu_custom_call", output_to_operand_aliasing={{}: (2, {})} | custom-call | flops 1 | bytes 1199250 | tf_op jit(solution)/shard_map/finish/pallas_call | solution.py:344
  (15 shorter events, 0.0 us)
Async XLA Ops:
  6.5 64.3 %all-gather.5.cloned.1.call-start = ((), (), s32[]{:S(2)}) async-start(), calls=%async_computation.1 | async-start | bytes 9437184 | tf_op jit(solution)/shard_map/all_gather | solution.py:363
  7.3 138.1 %all-gather.3.cloned.1.call-start = ((), (), s32[]{:S(2)}) async-start(), calls=%async_computation | async-start | bytes 1179648 | tf_op jit(solution)/shard_map/all_gather | solution.py:364
  15.5 40.9 %collective-permute-start.1 = (bf16[1024,512]{1,0:T(8,128)(2,1)}, bf16[1024,512]{1,0:T(8,128)(2,1)}, u32[]{:S(2)}, u32[]{:S(2)}) collective-permute-start(bf16[1024,512]{1,0:T(8,128)(2,1)} %get-tuple-element.12.refs_0_), channel_id=1, source_target_pairs={{0,1},{3,2},{4,5},{7,6},{8,9},{11,10},{12,13},{15,14},{16,17},{19,... | collective-permute-start | bytes 3145736 | tf_op jit(solution)/shard_map/even1_units0/ppermute | solution.py:407
  21.4 7.9 %copy-start.3 = (s32[1,4]{1,0:T(1,128)S(1)}, s32[1,4]{1,0:T(1,128)}, u32[]{:S(2)}) copy-start(s32[1,4]{1,0:T(1,128)} %constant_dynamic-slice_fusion) | copy-start | bytes 52
  27.0 39.7 %collective-permute-start = (bf16[1024,512]{1,0:T(8,128)(2,1)}, bf16[1024,512]{1,0:T(8,128)(2,1)}, u32[]{:S(2)}, u32[]{:S(2)}) collective-permute-start(bf16[1024,512]{1,0:T(8,128)(2,1)} %more_rows.1.refs_3_.refs_0_), channel_id=1, source_target_pairs={{0,1},{3,2},{4,5},{7,6},{8,9},{11,10},{12,13},{15,14},{16,17},{19,... | collective-permute-start | bytes 3145736 | tf_op jit(solution)/shard_map/even1_units2/ppermute | solution.py:407
  54.1 36.5 %collective-permute-start.4 = (bf16[1024,512]{1,0:T(8,128)(2,1)}, bf16[1024,512]{1,0:T(8,128)(2,1)}, u32[]{:S(2)}, u32[]{:S(2)}) collective-permute-start(bf16[1024,512]{1,0:T(8,128)(2,1)} %get-tuple-element.15.refs_0_), channel_id=1, source_target_pairs={{0,1},{3,2},{4,5},{7,6},{8,9},{11,10},{12,13},{15,14},{16,17},{19,... | collective-permute-start | bytes 3145736 | tf_op jit(solution)/shard_map/even2_units0/ppermute | solution.py:407
  58.9 34.2 %collective-permute-start.3 = (bf16[1024,512]{1,0:T(8,128)(2,1)}, bf16[1024,512]{1,0:T(8,128)(2,1)}, u32[]{:S(2)}, u32[]{:S(2)}) collective-permute-start(bf16[1024,512]{1,0:T(8,128)(2,1)} %added.10.refs_2_), channel_id=1, source_target_pairs={{1,2},{2,1},{5,6},{6,5},{9,10},{10,9},{13,14},{14,13},{17,18},{18,... | collective-permute-start | bytes 3145736 | tf_op jit(solution)/shard_map/odd2_units0/ppermute | solution.py:407
  69.2 42.5 %collective-permute-start.6 = (bf16[1024,512]{1,0:T(8,128)(2,1)}, bf16[1024,512]{1,0:T(8,128)(2,1)}, u32[]{:S(2)}, u32[]{:S(2)}) collective-permute-start(bf16[1024,512]{1,0:T(8,128)(2,1)} %added.11.refs_4_), channel_id=1, source_target_pairs={{1,2},{2,1},{5,6},{6,5},{9,10},{10,9},{13,14},{14,13},{17,18},{18,... | collective-permute-start | bytes 3145736 | tf_op jit(solution)/shard_map/odd2_units2/ppermute | solution.py:407
  80.0 20.4 %collective-permute-start.2 = (bf16[2048,128]{1,0:T(8,128)(2,1)}, bf16[2048,128]{1,0:T(8,128)(2,1)S(1)}, u32[]{:S(2)}, u32[]{:S(2)}) collective-permute-start(bf16[2048,128]{1,0:T(8,128)(2,1)} %low_terms.1.refs_1_.refs_0_.refs_4_), channel_id=1, source_target_pairs={{0,1},{3,2},{4,5},{7,6},{8,9},{11,10},{12,13},{15,14},{16,17},{19,... | collective-permute-start | bytes 1572872 | tf_op jit(solution)/shard_map/low_sums1/ppermute | solution.py:418
  88.3 34.6 %collective-permute-start.8 = (bf16[1024,512]{1,0:T(8,128)(2,1)}, bf16[1024,512]{1,0:T(8,128)(2,1)}, u32[]{:S(2)}, u32[]{:S(2)}) collective-permute-start(bf16[1024,512]{1,0:T(8,128)(2,1)} %added.12.refs_2_), channel_id=1, source_target_pairs={{0,1},{3,2},{4,5},{7,6},{8,9},{11,10},{12,13},{15,14},{16,17},{19,... | collective-permute-start | bytes 3145736 | tf_op jit(solution)/shard_map/even2_units2/ppermute | solution.py:407
  100.4 0.8 copy-start
  103.4 10.5 %collective-permute-start.5 = (bf16[2048,128]{1,0:T(8,128)(2,1)}, bf16[2048,128]{1,0:T(8,128)(2,1)S(1)}, u32[]{:S(2)}, u32[]{:S(2)}) collective-permute-start(bf16[2048,128]{1,0:T(8,128)(2,1)} %added.15.refs_2_), channel_id=1, source_target_pairs={{1,2},{2,1},{5,6},{6,5},{9,10},{10,9},{13,14},{14,13},{17,18},{18,... | collective-permute-start | bytes 1572872 | tf_op jit(solution)/shard_map/low_sums2/ppermute | solution.py:418
  104.1 31.1 %collective-permute-start.10 = (bf16[1024,512]{1,0:T(8,128)(2,1)}, bf16[1024,512]{1,0:T(8,128)(2,1)}, u32[]{:S(2)}, u32[]{:S(2)}) collective-permute-start(bf16[1024,512]{1,0:T(8,128)(2,1)} %added.13.refs_2_), channel_id=1, source_target_pairs={{1,2},{2,1},{5,6},{6,5},{9,10},{10,9},{13,14},{14,13},{17,18},{18,... | collective-permute-start | bytes 3145736 | tf_op jit(solution)/shard_map/odd3_units0/ppermute | solution.py:407
  105.8 45.0 %collective-permute-start.13 = (bf16[1024,512]{1,0:T(8,128)(2,1)}, bf16[1024,512]{1,0:T(8,128)(2,1)}, u32[]{:S(2)}, u32[]{:S(2)}) collective-permute-start(bf16[1024,512]{1,0:T(8,128)(2,1)} %added.14.refs_2_), channel_id=1, source_target_pairs={{0,1},{1,0},{2,3},{3,2},{4,5},{5,4},{6,7},{7,6},{8,9},{9,8},{10,11... | collective-permute-start | bytes 3145736 | tf_op jit(solution)/shard_map/even3_units0/ppermute | solution.py:407
  113.9 0.9 copy-start.1
  125.3 28.3 %collective-permute-start.9 = (bf16[1024,512]{1,0:T(8,128)(2,1)}, bf16[1024,512]{1,0:T(8,128)(2,1)}, u32[]{:S(2)}, u32[]{:S(2)}) collective-permute-start(bf16[1024,512]{1,0:T(8,128)(2,1)} %added.18.refs_2_), channel_id=1, source_target_pairs={{1,2},{2,1},{5,6},{6,5},{9,10},{10,9},{13,14},{14,13},{17,18},{18,... | collective-permute-start | bytes 3145736 | tf_op jit(solution)/shard_map/odd3_units2/ppermute | solution.py:407
  127.0 18.9 %collective-permute-start.7 = (bf16[2048,128]{1,0:T(8,128)(2,1)}, bf16[2048,128]{1,0:T(8,128)(2,1)S(1)}, u32[]{:S(2)}, u32[]{:S(2)}) collective-permute-start(bf16[2048,128]{1,0:T(8,128)(2,1)} %added.17.refs_2_), channel_id=1, source_target_pairs={{2,3},{1,0},{6,7},{5,4},{10,11},{9,8},{14,15},{13,12},{18,19},{17,... | collective-permute-start | bytes 1572872 | tf_op jit(solution)/shard_map/low_sums3/ppermute | solution.py:418
  128.3 29.3 %collective-permute-start.12 = (bf16[512,512]{1,0:T(8,128)(2,1)}, bf16[512,512]{1,0:T(8,128)(2,1)}, u32[]{:S(2)}, u32[]{:S(2)}) collective-permute-start(bf16[512,512]{1,0:T(8,128)(2,1)} %added.16.refs_2_), channel_id=1, source_target_pairs={{0,1},{1,0},{2,3},{3,2},{4,5},{5,4},{6,7},{7,6},{8,9},{9,8},{10,11... | collective-permute-start | bytes 1572872 | tf_op jit(solution)/shard_map/even3_units2/ppermute | solution.py:407
  135.2 31.5 %collective-permute-start.11 = (bf16[512,512]{1,0:T(8,128)(2,1)}, bf16[512,512]{1,0:T(8,128)(2,1)}, u32[]{:S(2)}, u32[]{:S(2)}) collective-permute-start(bf16[512,512]{1,0:T(8,128)(2,1)} %added.19.refs_10_), channel_id=1, source_target_pairs={{0,1},{1,0},{2,3},{3,2},{4,5},{5,4},{6,7},{7,6},{8,9},{9,8},{10,11... | collective-permute-start | bytes 1572872 | tf_op jit(solution)/shard_map/even3_units3/ppermute | solution.py:407
  146.0 0.8 copy-start.2
Sparse Core Ops, SparseCore 0:
  9.2 57.0 all-gather.4
  90.8 22.5 all-gather.2

commit v2 on v1

--- a/solution.py
+++ b/solution.py
@@ -6,9 +6,9 @@
 from jax.experimental.pallas import tpu as pltpu
 from jax.sharding import PartitionSpec as P
 
-UNITS = 4
+UNITS = 8
 SCALE = 0.25
-VMEM_BYTES = 63 * 1024 * 1024
+VMEM_BYTES = 64 * 1024 * 1024 - 256 * 1024
 
 
 def line_plan(n):
@@ -35,6 +35,13 @@
     return jnp.asarray(table)[lax.axis_index(axis)]
 
 
+def chunk_of(table, place):
+    value = int(table[0])
+    for i in range(1, len(table)):
+        value = jnp.where(place == i, int(table[i]), value)
+    return value
+
+
 def params():
     return pltpu.CompilerParams(vmem_limit_bytes=VMEM_BYTES)
 
@@ -46,7 +53,7 @@
 HERE = pl.BlockSpec(memory_space=pl.ANY)
 
 
-def first_piece(hidden, weight, which, rows, chunk):
+def first_piece(hidden, weight, place, which, rows, chunk):
     width = hidden.shape[1]
     steps = 2
     depth = width // steps
@@ -76,7 +83,7 @@
             grid=(steps,),
             in_specs=[
                 pl.BlockSpec((rows, depth), lambda k, c: (0, k)),
-                pl.BlockSpec((depth, 2, chunk), lambda k, c: (k, 0, c[0])),
+                pl.BlockSpec((depth, 2, chunk), lambda k, c: (k, 0, chunk_of(which, c[0]))),
             ],
             out_specs=[
                 pl.BlockSpec((depth, 2 * chunk), lambda k, c: (k, 0)),
@@ -90,7 +97,7 @@
         ],
         compiler_params=params(),
         cost_estimate=estimate(5.5),
-    )(which, hidden, weight)
+    )(place, hidden, weight)
 
 
 def row_outputs(cuts, block, columns):
@@ -140,7 +147,7 @@
     )(hidden, flat, *after)
 
 
-def other_slots(hidden, weight, which, cuts, chunk, after):
+def other_slots(hidden, weight, place, which, cuts, chunk, after):
     tok_rows, width = hidden.shape
     count = len(cuts)
     steps = 4
@@ -185,7 +192,7 @@
             grid=(steps + tok_rows // block,),
             in_specs=[pl.BlockSpec((block, width), lambda i, w: (jnp.maximum(i - steps, 0), 0))]
             + [
-                pl.BlockSpec((depth, 2, chunk), lambda i, w, s=s: (jnp.minimum(i, steps - 1), 0, w[s]))
+                pl.BlockSpec((depth, 2, chunk), lambda i, w, s=s: (jnp.minimum(i, steps - 1), 0, chunk_of(which[s], w[0])))
                 for s in range(count)
             ]
             + [HERE] * len(after),
@@ -195,7 +202,7 @@
         out_shape=out_shapes,
         compiler_params=params(),
         cost_estimate=estimate(8 + 1.3 * count * tok_rows / block),
-    )(which, hidden, *[weight] * count, *after)
+    )(place, hidden, *[weight] * count, *after)
     return [[arrays[k] for k, _ in target] for target in targets]
 
 
@@ -228,7 +235,7 @@
 
 def added(start, rows, terms, after):
     columns = terms[0][0][1].shape[1]
-    block = 512 if columns > 128 else rows
+    block = rows if columns <= 128 else 512 if rows % 512 == start % 512 == 0 else 256
     specs, operands, layout = segment_specs(terms, start, block)
 
     def body(*refs):
@@ -328,7 +335,7 @@
 
 def finish(start, rows, out_rows, terms, previous):
     chunk = terms[0][0][1].shape[1] // 2
-    block = 512
+    block = 512 if rows % 512 == start % 512 == 0 else 256
     skip = start // block
     specs, operands, layout = segment_specs(terms, start, block)
     aliases = {}
@@ -363,7 +370,8 @@
     down_maps = lax.all_gather(adapter_down_weight, "tok", axis=0, tiled=True)
     up_maps = lax.all_gather(adapter_up_weight, "tok", axis=0, tiled=True)
 
-    which = by_device(slots, "tp")
+    place = lax.axis_index("tp").reshape(1)
+    which = slots.T
     partial = {}
     received = {}
     last = []
@@ -410,10 +418,10 @@
 
     low_parts = []
 
-    def send_low(time):
+    def send_low(time, after=()):
         value = low_parts[0]
         if time > 1:
-            value = ordered(added(0, tok_rows, [[(0, value)], [(0, low_parts[-1])]], list(last)))
+            value = ordered(added(0, tok_rows, [[(0, value)], [(0, low_parts[-1])]], last + list(after)))
         with jax.named_scope(f"low_sums{time}"):
             low_parts.append(lax.ppermute(value, "tp", [(time - 1, time), (n - time, n - time - 1)]))
 
@@ -421,7 +429,7 @@
 
     def prepare(u, count):
         start, rows = u * unit, count * unit
-        terms = [pick(partial[n - 1], start, rows), pick(received[n - 1, 1], start, rows)]
+        terms = [pick(partial[n - 1], start, rows)]
         value = with_adapter(start, rows, terms, low_parts, up_maps, tenant_per_block, list(last))
         ready.append((start, ordered(value)))
 
@@ -429,45 +437,51 @@
 
     def complete(u, count):
         start, rows = u * unit, count * unit
-        terms = [pick(ready, start, rows), pick(received[n - 1, 0], start, rows)]
+        terms = [pick(ready, start, rows)] + [pick(received[n - 1, parity], start, rows) for parity in (0, 1)]
         result[0] = finish(start, rows, tok_rows, terms, result[0])
 
-    half = UNITS // 2
-    flat, head = first_piece(hidden, key_value_weight, which[:1], half * unit, chunk)
+    first = 2 * unit
+    flat, head = first_piece(hidden, key_value_weight, place, which[0], first, chunk)
     partial[0] = [(0, head)]
     if n == 4:
-        send(1, 0, 0, 2)
-        partial[0] += cut(more_rows(hidden, flat, half * unit, [half * unit], []), half * unit)
-        send(1, 0, 2, 2)
+        arrived = send(1, 0, 0, 2)
+        partial[0] += cut(more_rows(hidden, flat, first, [first] * 3, []), first)
+        for u in (2, 4, 6):
+            send(1, 0, u, 2)
         others = other_slots(
-            hidden, key_value_weight, which[1:], [[2 * unit, 2 * unit], [tok_rows], [tok_rows]], chunk, [partial[0][1][1]]
+            hidden,
+            key_value_weight,
+            place,
+            which[1:],
+            [[tok_rows // 2] * 2, [tok_rows], [tok_rows]],
+            chunk,
+            [partial[0][-1][1], arrived],
         )
         for s, arrays in enumerate(others):
             partial[s + 1] = cut(arrays)
         ordered(partial[3][0][1])
-        send(2, 0, 0, 2)
-        send(2, 1, 0, 2)
-        send(2, 1, 2, 2)
+        send(2, 0, 0, 4)
+        send(2, 1, 0, 4)
+        send(2, 1, 4, 4)
         low_parts.append(ordered(low_terms(hidden, down_maps, tenant_per_block, list(last))))
         send_low(1)
-        send(2, 0, 2, 2, again=True)
-        send(3, 1, 0, 2)
-        send(3, 0, 0, 2)
+        send(2, 0, 4, 4, again=True)
+        send(3, 1, 0, 4)
+        send(3, 0, 0, 4)
         send_low(2)
-        send(3, 0, 2, 1)
+        send(3, 0, 4, 2)
         send_low(3)
-        send(3, 1, 2, 2)
-        send(3, 0, 3, 1)
-        prepare(0, 2)
-        complete(0, 2)
-        prepare(2, 2)
-        complete(2, 1)
-        complete(3, 1)
+        send(3, 1, 4, 4)
+        send(3, 0, 6, 2)
+        prepare(0, 8)
+        complete(0, 4)
+        complete(4, 2)
+        complete(6, 2)
     else:
         partial[0] = [
-            (0, jnp.concatenate([head] + list(more_rows(hidden, flat, half * unit, [half * unit], []))))
+            (0, jnp.concatenate([head] + list(more_rows(hidden, flat, first, [tok_rows - first], []))))
         ]
-        others = other_slots(hidden, key_value_weight, which[1:], [[tok_rows]] * (n - 1), chunk, [head])
+        others = other_slots(hidden, key_value_weight, place, which[1:], [[tok_rows]] * (n - 1), chunk, [head])
         for s, arrays in enumerate(others):
             partial[s + 1] = cut(arrays)
         ordered(head)

time: 178 us -> 174 us (0.978)
  waiting for transfers between devices: 25.1 us -> 30.6 us
  local copies, waits for them, and re-layouts: 4.24 us -> 0 us
  starting transfers between devices: 48.5 us -> 45.7 us
    ppermute x3, waiting for transfers between devices: 5.51 us -> 14.2 us  [send_low(): lax.ppermute(value, 'tp', [(time - 1, time), (n - time, n - time - 1)])]
    ppermute x11 -> x13, starting transfers between devices: 40.2 us -> 35.5 us  [send(): moved = lax.ppermute(value, 'tp', moves)]
    ppermute x11 -> x13, waiting for transfers between devices: 18.9 us -> 15.6 us  [send(): moved = lax.ppermute(value, 'tp', moves)]
    pallas_call x1, Pallas kernels: 5.64 us -> 8.16 us  [more_rows(): pl.pallas_call(body, name='more_rows', grid=(sum(cuts) // block,), in_spe...]
    unnamed x8 -> x0, local copies, waits for them, and re-layouts: 2.46 us -> none
    pallas_call x2 -> x1, Pallas kernels: 7.93 us -> 5.73 us  [with_adapter(): pl.pallas_call(body, name='with_adapter', grid_spec=pltpu.PrefetchScalarG...]
    pallas_call x1, Pallas kernels: 6.97 us -> 4.78 us  [first_piece(): pl.pallas_call(body, name='first_piece', grid_spec=pltpu.PrefetchScalarGr...]
    ppermute x3, starting transfers between devices: 8.23 us -> 10.1 us  [send_low(): lax.ppermute(value, 'tp', [(time - 1, time), (n - time, n - time - 1)])]
  transfers between devices with their start and end apart: 16 -> 18, of which waited for: 5 -> 6; matrix products, arithmetic and copies ran while one was open for 1% -> 0% of each run, Pallas kernels for 47% -> 47%
where the time goes in v2:
time: 174 us; the launch traced here: 173 us
  Pallas kernels  83.1 us (48%)
  starting transfers between devices  45.7 us (26%)
  waiting for transfers between devices  30.6 us (18%)
  between operations  13.5 us (8%)
    ppermute x13, starting transfers between devices, send(): moved = lax.ppermute(value, 'tp', moves)  35.5 us
    pallas_call x10, Pallas kernels, added(): pl.pallas_call(body, name='added', grid=(rows // block,), in_specs=specs...  23.8 us
    pallas_call x1, Pallas kernels, other_slots(): pl.pallas_call(body, name='other_slots', grid_spec=pltpu.PrefetchScalarGr...  23.6 us
    ppermute x13, waiting for transfers between devices, send(): moved = lax.ppermute(value, 'tp', moves)  15.6 us
    ppermute x3, waiting for transfers between devices, send_low(): lax.ppermute(value, 'tp', [(time - 1, time), (n - time, n - time - 1)])  14.2 us
    ppermute x3, starting transfers between devices, send_low(): lax.ppermute(value, 'tp', [(time - 1, time), (n - time, n - time - 1)])  10.1 us
    pallas_call x3, Pallas kernels, finish(): pl.pallas_call(body, name='finish', grid=(rows // block,), in_specs=specs...  8.56 us
    pallas_call x1, Pallas kernels, low_terms(): pl.pallas_call(body, name='low_terms', grid_spec=pltpu.PrefetchScalarGrid...  8.54 us
  transfers between devices with their start and end apart: 18, of which 6 were waited for; matrix products, arithmetic and copies ran while one was open for 0% of the time, Pallas kernels for 47%

profile of v2, /device:TPU:0, one launch (start us, length us, event | category | flops | bytes accessed | tf_op | source)
XLA Modules:
  0.0 172.8 jit_solution(12546052353105479604)
XLA Ops:
  6.5 0.7 all-gather.5.cloned.1.call-update
  7.3 0.0 all-gather.3.cloned.1.call-start
  7.3 4.8 %first_piece.1 = (bf16[2048,512]{1,0:T(8,128)(2,1)}, bf16[512,512]{1,0:T(8,128)(2,1)}) custom-call(s32[1]{0:T(128)} %bitcast.which_ref, bf16[2048,2048]{1,0:T(8,128)(2,1)} %hidden_ref.7, bf16[2048,2,1024]{2,1,0:T(2,128)(2,1)} %refs_2_.1), custom_call_target="tpu_custom_call" | custom-call | flops 1 | bytes 5073750 | tf_op jit(solution)/shard_map/first_piece/pallas_call | solution.py:78
  12.1 5.7 %collective-permute-start.2 = (bf16[512,512]{1,0:T(8,128)(2,1)}, bf16[512,512]{1,0:T(8,128)(2,1)}, u32[]{:S(2)}, u32[]{:S(2)}) collective-permute-start(bf16[512,512]{1,0:T(8,128)(2,1)} %get-tuple-element.17.refs_0_), channel_id=1, source_target_pairs={{0,1},{3,2},{4,5},{7,6},{8,9},{11,10},{12,13},{15,14},{16,17},{19,... | collective-permute-start | bytes 1572872 | tf_op jit(solution)/shard_map/even1_units0/ppermute | solution.py:415
  17.8 8.2 %more_rows.1 = (bf16[512,512]{1,0:T(8,128)(2,1)}, bf16[512,512]{1,0:T(8,128)(2,1)}, bf16[512,512]{1,0:T(8,128)(2,1)}) custom-call(bf16[2048,2048]{1,0:T(8,128)(2,1)} %hidden_ref.7, bf16[2048,512]{1,0:T(8,128)(2,1)} %get-tuple-element.14.flat_ref), custom_call_target="tpu_custom_call" | custom-call | flops 1 | bytes 6918750 | tf_op jit(solution)/shard_map/more_rows/pallas_call | solution.py:134
  26.0 2.1 %collective-permute-start.3 = (bf16[512,512]{1,0:T(8,128)(2,1)}, bf16[512,512]{1,0:T(8,128)(2,1)}, u32[]{:S(2)}, u32[]{:S(2)}) collective-permute-start(bf16[512,512]{1,0:T(8,128)(2,1)} %get-tuple-element.18.refs_1_), channel_id=1, source_target_pairs={{0,1},{3,2},{4,5},{7,6},{8,9},{11,10},{12,13},{15,14},{16,17},{19,... | collective-permute-start | bytes 1572872 | tf_op jit(solution)/shard_map/even1_units2/ppermute | solution.py:415
  28.1 2.1 %collective-permute-start.1 = (bf16[512,512]{1,0:T(8,128)(2,1)}, bf16[512,512]{1,0:T(8,128)(2,1)}, u32[]{:S(2)}, u32[]{:S(2)}) collective-permute-start(bf16[512,512]{1,0:T(8,128)(2,1)} %get-tuple-element.16.refs_3_.refs_1_), channel_id=1, source_target_pairs={{0,1},{3,2},{4,5},{7,6},{8,9},{11,10},{12,13},{15,14},{16,17},{19,... | collective-permute-start | bytes 1572872 | tf_op jit(solution)/shard_map/even1_units6/ppermute | solution.py:415
  30.2 2.1 %collective-permute-start = (bf16[512,512]{1,0:T(8,128)(2,1)}, bf16[512,512]{1,0:T(8,128)(2,1)}, u32[]{:S(2)}, u32[]{:S(2)}) collective-permute-start(bf16[512,512]{1,0:T(8,128)(2,1)} %get-tuple-element.15.refs_0_), channel_id=1, source_target_pairs={{0,1},{3,2},{4,5},{7,6},{8,9},{11,10},{12,13},{15,14},{16,17},{19,... | collective-permute-start | bytes 1572872 | tf_op jit(solution)/shard_map/even1_units4/ppermute | solution.py:415
  32.2 0.0 collective-permute-done.2.refs_4_.refs_2_
  32.2 23.6 %other_slots.1 = (bf16[1024,512]{1,0:T(8,128)(2,1)}, bf16[1024,512]{1,0:T(8,128)(2,1)}, bf16[2048,512]{1,0:T(8,128)(2,1)}, bf16[2048,512]{1,0:T(8,128)(2,1)}) custom-call(s32[1]{0:T(128)} %bitcast.which_ref, bf16[2048,2048]{1,0:T(8,128)(2,1)} %hidden_ref.7, bf16[2048,2,1024]{2,1,0:T(2,128)(2,1)} %refs_2_.1, bf16[2048,2,1024]{2,1,0:T(2,128)(2,1)} %refs_2_.1, ...), custom_call_target="tpu_custom_call" | custom-call | flops 1 | bytes 21771000 | tf_op jit(solution)/shard_map/other_slots/pallas_call | solution.py:187
  55.9 2.5 %collective-permute-start.6 = (bf16[1024,512]{1,0:T(8,128)(2,1)}, bf16[1024,512]{1,0:T(8,128)(2,1)}, u32[]{:S(2)}, u32[]{:S(2)}) collective-permute-start(bf16[1024,512]{1,0:T(8,128)(2,1)} %get-tuple-element.21.refs_0_), channel_id=1, source_target_pairs={{0,1},{3,2},{4,5},{7,6},{8,9},{11,10},{12,13},{15,14},{16,17},{19,... | collective-permute-start | bytes 3145736 | tf_op jit(solution)/shard_map/even2_units0/ppermute | solution.py:415
  58.4 0.0 collective-permute-done.3.refs_3_
  58.4 2.9 %added.10.refs_4_ = bf16[1024,512]{1,0:T(8,128)(2,1)} custom-call(bf16[512,512]{1,0:T(8,128)(2,1)} %get-tuple-element.17.refs_0_, bf16[512,512]{1,0:T(8,128)(2,1)} %get-tuple-element.18.refs_1_, bf16[512,512]{1,0:T(8,128)(2,1)} %collective-permute-done.2.refs_4_.refs_2_, bf16[512,512]{1,0:T(8,128)(2,1)} %collective-permute-done.3.refs_3_, ...), custom_call_target="tpu_custom_call" | custom-call | flops 1 | bytes 2398500 | tf_op jit(solution)/shard_map/added/pallas_call | solution.py:244
  61.2 1.7 collective-permute-start.5
  62.9 0.0 collective-permute-done.1.refs_3_
  62.9 0.2 collective-permute-done.refs_2_
  63.1 2.9 %added.11.refs_4_ = bf16[1024,512]{1,0:T(8,128)(2,1)} custom-call(bf16[512,512]{1,0:T(8,128)(2,1)} %get-tuple-element.15.refs_0_, bf16[512,512]{1,0:T(8,128)(2,1)} %get-tuple-element.16.refs_3_.refs_1_, bf16[512,512]{1,0:T(8,128)(2,1)} %collective-permute-done.refs_2_, bf16[512,512]{1,0:T(8,128)(2,1)} %collective-permute-done.1.refs_3_, ...), custom_call_target="tpu_custom_call" | custom-call | flops 1 | bytes 2398500 | tf_op jit(solution)/shard_map/added/pallas_call | solution.py:244
  66.0 1.7 collective-permute-start.8
  67.7 8.5 %low_terms.1.refs_1_.refs_0_.refs_4_ = bf16[2048,128]{1,0:T(8,128)(2,1)} custom-call(s32[16]{0:T(128)} %tenant_ref.3, bf16[2048,2048]{1,0:T(8,128)(2,1)} %hidden_ref.7, bf16[16,2048,128]{2,1,0:T(8,128)(2,1)} %all-gather.5.cloned.1.call-done.refs_0_.refs_1_.refs_2_.refs_3_, ...), custom_call_target="tpu_custom_call" | custom-call | flops 1 | bytes 7933500 | tf_op jit(solution)/shard_map/low_terms/pallas_call | solution.py:270
  76.2 7.4 %collective-permute-start.4 = (bf16[2048,128]{1,0:T(8,128)(2,1)}, bf16[2048,128]{1,0:T(8,128)(2,1)}, u32[]{:S(2)}, u32[]{:S(2)}) collective-permute-start(bf16[2048,128]{1,0:T(8,128)(2,1)} %low_terms.1.refs_1_.refs_0_.refs_4_), channel_id=1, source_target_pairs={{0,1},{3,2},{4,5},{7,6},{8,9},{11,10},{12,13},{15,14},{16,17},{19,... | collective-permute-start | bytes 1572872 | tf_op jit(solution)/shard_map/low_sums1/ppermute | solution.py:426
  83.6 2.0 %added.12.refs_2_ = bf16[1024,512]{1,0:T(8,128)(2,1)} custom-call(bf16[1024,512]{1,0:T(8,128)(2,1)} %get-tuple-element.22.refs_0_, bf16[2048,128]{1,0:T(8,128)(2,1)} %low_terms.1.refs_1_.refs_0_.refs_4_), custom_call_target="tpu_custom_call" | custom-call | flops 1 | bytes 2398500 | tf_op jit(solution)/shard_map/added/pallas_call | solution.py:244
  85.6 2.3 %collective-permute-start.10 = (bf16[1024,512]{1,0:T(8,128)(2,1)}, bf16[1024,512]{1,0:T(8,128)(2,1)}, u32[]{:S(2)}, u32[]{:S(2)}) collective-permute-start(bf16[1024,512]{1,0:T(8,128)(2,1)} %added.12.refs_2_), channel_id=1, source_target_pairs={{0,1},{3,2},{4,5},{7,6},{8,9},{11,10},{12,13},{15,14},{16,17},{19,... | collective-permute-start | bytes 3145736 | tf_op jit(solution)/shard_map/even2_units4/ppermute | solution.py:415
  87.9 0.0 all-gather.3.cloned.1.call-update
  88.0 2.5 %added.13.refs_2_ = bf16[1024,512]{1,0:T(8,128)(2,1)} custom-call(bf16[1024,512]{1,0:T(8,128)(2,1)} %get-tuple-element.21.refs_0_, bf16[1024,512]{1,0:T(8,128)(2,1)} %collective-permute-done.6.refs_1_, bf16[1024,512]{1,0:T(8,128)(2,1)} %added.12.refs_2_), custom_call_target="tpu_custom_call" | custom-call | flops 1 | bytes 2398500 | tf_op jit(solution)/shard_map/added/pallas_call | solution.py:244
  90.4 0.0 collective-permute-done.5.refs_1_
  90.4 2.5 %added.14.refs_2_ = bf16[1024,512]{1,0:T(8,128)(2,1)} custom-call(bf16[2048,512]{1,0:T(8,128)(2,1)} %get-tuple-element.20.refs_0_, bf16[1024,512]{1,0:T(8,128)(2,1)} %collective-permute-done.5.refs_1_, bf16[1024,512]{1,0:T(8,128)(2,1)} %added.13.refs_2_), custom_call_target="tpu_custom_call" | custom-call | flops 1 | bytes 2398500 | tf_op jit(solution)/shard_map/added/pallas_call | solution.py:244
  92.9 4.0 %collective-permute-done.4.refs_1_.refs_5_ = bf16[2048,128]{1,0:T(8,128)(2,1)} collective-permute-done((bf16[2048,128]{1,0:T(8,128)(2,1)}, bf16[2048,128]{1,0:T(8,128)(2,1)}, u32[]{:S(2)}, u32[]{:S(2)}) %collective-permute-start.4) | collective-permute-done | bytes 524320 | tf_op jit(solution)/shard_map/low_sums1/ppermute | solution.py:426
  96.9 2.1 %added.15.refs_2_ = bf16[2048,128]{1,0:T(8,128)(2,1)} custom-call(bf16[2048,128]{1,0:T(8,128)(2,1)} %low_terms.1.refs_1_.refs_0_.refs_4_, bf16[2048,128]{1,0:T(8,128)(2,1)} %collective-permute-done.4.refs_1_.refs_5_, bf16[1024,512]{1,0:T(8,128)(2,1)} %added.14.refs_2_), custom_call_target="tpu_custom_call" | custom-call | flops 1 | bytes 1199250 | tf_op jit(solution)/shard_map/added/pallas_call | solution.py:244
  99.0 1.4 collective-permute-start.7
  100.4 4.8 %collective-permute-start.14 = (bf16[1024,512]{1,0:T(8,128)(2,1)}, bf16[1024,512]{1,0:T(8,128)(2,1)}, u32[]{:S(2)}, u32[]{:S(2)}) collective-permute-start(bf16[1024,512]{1,0:T(8,128)(2,1)} %added.14.refs_2_), channel_id=1, source_target_pairs={{0,1},{1,0},{2,3},{3,2},{4,5},{5,4},{6,7},{7,6},{8,9},{9,8},{10,11... | collective-permute-start | bytes 3145736 | tf_op jit(solution)/shard_map/even3_units0/ppermute | solution.py:415
  105.2 1.6 collective-permute-start.15
  106.8 2.2 %added.16.refs_2_ = bf16[512,512]{1,0:T(8,128)(2,1)} custom-call(bf16[2048,512]{1,0:T(8,128)(2,1)} %get-tuple-element.20.refs_0_, bf16[1024,512]{1,0:T(8,128)(2,1)} %collective-permute-done.8.refs_1_, bf16[2048,128]{1,0:T(8,128)(2,1)} %added.15.refs_2_), custom_call_target="tpu_custom_call" | custom-call | flops 1 | bytes 1199250 | tf_op jit(solution)/shard_map/added/pallas_call | solution.py:244
  109.0 0.0 collective-permute-done.7.refs_1_.refs_6_
  109.0 2.2 %added.17.refs_2_ = bf16[2048,128]{1,0:T(8,128)(2,1)} custom-call(bf16[2048,128]{1,0:T(8,128)(2,1)} %low_terms.1.refs_1_.refs_0_.refs_4_, bf16[2048,128]{1,0:T(8,128)(2,1)} %collective-permute-done.7.refs_1_.refs_6_, bf16[512,512]{1,0:T(8,128)(2,1)} %added.16.refs_2_), custom_call_target="tpu_custom_call" | custom-call | flops 1 | bytes 1199250 | tf_op jit(solution)/shard_map/added/pallas_call | solution.py:244
  111.2 8.1 %collective-permute-done.10.refs_1_ = bf16[1024,512]{1,0:T(8,128)(2,1)} collective-permute-done((bf16[1024,512]{1,0:T(8,128)(2,1)}, bf16[1024,512]{1,0:T(8,128)(2,1)}, u32[]{:S(2)}, u32[]{:S(2)}) %collective-permute-start.10) | collective-permute-done | bytes 1048608 | tf_op jit(solution)/shard_map/even2_units4/ppermute | solution.py:415
  119.3 2.5 %added.18.refs_2_ = bf16[1024,512]{1,0:T(8,128)(2,1)} custom-call(bf16[1024,512]{1,0:T(8,128)(2,1)} %get-tuple-element.22.refs_0_, bf16[1024,512]{1,0:T(8,128)(2,1)} %collective-permute-done.10.refs_1_, bf16[2048,128]{1,0:T(8,128)(2,1)} %added.17.refs_2_), custom_call_target="tpu_custom_call" | custom-call | flops 1 | bytes 2398500 | tf_op jit(solution)/shard_map/added/pallas_call | solution.py:244
  121.8 1.6 collective-permute-start.12
  123.4 1.3 collective-permute-start.9
  124.7 7.4 %collective-permute-start.13 = (bf16[512,512]{1,0:T(8,128)(2,1)}, bf16[512,512]{1,0:T(8,128)(2,1)}, u32[]{:S(2)}, u32[]{:S(2)}) collective-permute-start(bf16[512,512]{1,0:T(8,128)(2,1)} %added.16.refs_2_), channel_id=1, source_target_pairs={{0,1},{1,0},{2,3},{3,2},{4,5},{5,4},{6,7},{7,6},{8,9},{9,8},{10,11... | collective-permute-start | bytes 1572872 | tf_op jit(solution)/shard_map/even3_units4/ppermute | solution.py:415
  132.1 2.1 %added.19.refs_9_ = bf16[512,512]{1,0:T(8,128)(2,1)} custom-call(bf16[2048,512]{1,0:T(8,128)(2,1)} %get-tuple-element.20.refs_0_, bf16[1024,512]{1,0:T(8,128)(2,1)} %collective-permute-done.8.refs_1_, bf16[1024,512]{1,0:T(8,128)(2,1)} %added.18.refs_2_), custom_call_target="tpu_custom_call" | custom-call | flops 1 | bytes 1199250 | tf_op jit(solution)/shard_map/added/pallas_call | solution.py:244
  134.2 10.2 %collective-permute-done.9.refs_7_ = bf16[2048,128]{1,0:T(8,128)(2,1)} collective-permute-done((bf16[2048,128]{1,0:T(8,128)(2,1)}, bf16[2048,128]{1,0:T(8,128)(2,1)}, u32[]{:S(2)}, u32[]{:S(2)}) %collective-permute-start.9) | collective-permute-done | bytes 524320 | tf_op jit(solution)/shard_map/low_sums3/ppermute | solution.py:426
  144.4 5.7 %with_adapter.1.refs_0_ = bf16[2048,512]{1,0:T(8,128)(2,1)} custom-call(s32[16]{0:T(128)} %tenant_ref.3, bf16[16,2,64,256]{3,2,1,0:T(8,128)(2,1)} %all-gather.3.cloned.1.call-done.refs_0_.refs_1_.refs_2_.refs_3_, bf16[16,2,64,256]{3,2,1,0:T(8,128)(2,1)} %all-gather.3.cloned.1.call-done.refs_0_.refs_1_.refs_2_.refs_3_, ...), custom_call_target="tpu_custom_call" | custom-call | flops 1 | bytes 7380000 | tf_op jit(solution)/shard_map/with_adapter/pallas_call | solution.py:315
  150.2 0.0 collective-permute-done.15.refs_2_
  150.2 3.2 %finish.3.refs_3_ = bf16[2048,2,256]{2,1,0:T(2,128)(2,1)} custom-call(bf16[2048,512]{1,0:T(8,128)(2,1)} %with_adapter.1.refs_0_, bf16[1024,512]{1,0:T(8,128)(2,1)} %collective-permute-done.14.refs_1_, bf16[1024,512]{1,0:T(8,128)(2,1)} %collective-permute-done.15.refs_2_), custom_call_target="tpu_custom_call" | custom-call | flops 1 | bytes 2398500 | tf_op jit(solution)/shard_map/finish/pallas_call | solution.py:351
  153.4 2.2 %collective-permute-done.13.refs_1_ = bf16[512,512]{1,0:T(8,128)(2,1)} collective-permute-done((bf16[512,512]{1,0:T(8,128)(2,1)}, bf16[512,512]{1,0:T(8,128)(2,1)}, u32[]{:S(2)}, u32[]{:S(2)}) %collective-permute-start.13) | collective-permute-done | bytes 524320 | tf_op jit(solution)/shard_map/even3_units4/ppermute | solution.py:415
  155.7 2.7 %finish.4.refs_3_ = bf16[2048,2,256]{2,1,0:T(2,128)(2,1)} custom-call(bf16[2048,512]{1,0:T(8,128)(2,1)} %with_adapter.1.refs_0_, bf16[512,512]{1,0:T(8,128)(2,1)} %collective-permute-done.13.refs_1_, bf16[1024,512]{1,0:T(8,128)(2,1)} %collective-permute-done.12.refs_2_, bf16[2048,2,256]{2,1,0:T(2,128)(2,1)} %finish.3.refs_3_), custom_call_target="tpu_custom_call", output_to_operand_aliasing={{}: (3, {})} | custom-call | flops 1 | bytes 1199250 | tf_op jit(solution)/shard_map/finish/pallas_call | solution.py:351
  158.3 5.0 %collective-permute-done.11.refs_1_ = bf16[512,512]{1,0:T(8,128)(2,1)} collective-permute-done((bf16[512,512]{1,0:T(8,128)(2,1)}, bf16[512,512]{1,0:T(8,128)(2,1)}, u32[]{:S(2)}, u32[]{:S(2)}) %collective-permute-start.11) | collective-permute-done | bytes 524320 | tf_op jit(solution)/shard_map/even3_units6/ppermute | solution.py:415
  163.3 2.7 %finish.5 = bf16[2048,2,256]{2,1,0:T(2,128)(2,1)} custom-call(bf16[2048,512]{1,0:T(8,128)(2,1)} %with_adapter.1.refs_0_, bf16[512,512]{1,0:T(8,128)(2,1)} %collective-permute-done.11.refs_1_, bf16[1024,512]{1,0:T(8,128)(2,1)} %collective-permute-done.12.refs_2_, bf16[2048,2,256]{2,1,0:T(2,128)(2,1)} %finish.4.refs_3_), custom_call_target="tpu_custom_call", output_to_operand_aliasing={{}: (3, {})} | custom-call | flops 1 | bytes 1199250 | tf_op jit(solution)/shard_map/finish/pallas_call | solution.py:351
  (8 shorter events, 0.0 us)
Async XLA Ops:
  6.5 61.1 %all-gather.5.cloned.1.call-start = ((), (), s32[]{:S(2)}) async-start(), calls=%async_computation.1 | async-start | bytes 9437184 | tf_op jit(solution)/shard_map/all_gather | solution.py:370
  7.3 137.2 %all-gather.3.cloned.1.call-start = ((), (), s32[]{:S(2)}) async-start(), calls=%async_computation | async-start | bytes 1179648 | tf_op jit(solution)/shard_map/all_gather | solution.py:371
  12.1 20.2 %collective-permute-start.2 = (bf16[512,512]{1,0:T(8,128)(2,1)}, bf16[512,512]{1,0:T(8,128)(2,1)}, u32[]{:S(2)}, u32[]{:S(2)}) collective-permute-start(bf16[512,512]{1,0:T(8,128)(2,1)} %get-tuple-element.17.refs_0_), channel_id=1, source_target_pairs={{0,1},{3,2},{4,5},{7,6},{8,9},{11,10},{12,13},{15,14},{16,17},{19,... | collective-permute-start | bytes 1572872 | tf_op jit(solution)/shard_map/even1_units0/ppermute | solution.py:415
  26.0 32.4 %collective-permute-start.3 = (bf16[512,512]{1,0:T(8,128)(2,1)}, bf16[512,512]{1,0:T(8,128)(2,1)}, u32[]{:S(2)}, u32[]{:S(2)}) collective-permute-start(bf16[512,512]{1,0:T(8,128)(2,1)} %get-tuple-element.18.refs_1_), channel_id=1, source_target_pairs={{0,1},{3,2},{4,5},{7,6},{8,9},{11,10},{12,13},{15,14},{16,17},{19,... | collective-permute-start | bytes 1572872 | tf_op jit(solution)/shard_map/even1_units2/ppermute | solution.py:415
  28.1 34.8 %collective-permute-start.1 = (bf16[512,512]{1,0:T(8,128)(2,1)}, bf16[512,512]{1,0:T(8,128)(2,1)}, u32[]{:S(2)}, u32[]{:S(2)}) collective-permute-start(bf16[512,512]{1,0:T(8,128)(2,1)} %get-tuple-element.16.refs_3_.refs_1_), channel_id=1, source_target_pairs={{0,1},{3,2},{4,5},{7,6},{8,9},{11,10},{12,13},{15,14},{16,17},{19,... | collective-permute-start | bytes 1572872 | tf_op jit(solution)/shard_map/even1_units6/ppermute | solution.py:415
  30.2 33.0 %collective-permute-start = (bf16[512,512]{1,0:T(8,128)(2,1)}, bf16[512,512]{1,0:T(8,128)(2,1)}, u32[]{:S(2)}, u32[]{:S(2)}) collective-permute-start(bf16[512,512]{1,0:T(8,128)(2,1)} %get-tuple-element.15.refs_0_), channel_id=1, source_target_pairs={{0,1},{3,2},{4,5},{7,6},{8,9},{11,10},{12,13},{15,14},{16,17},{19,... | collective-permute-start | bytes 1572872 | tf_op jit(solution)/shard_map/even1_units4/ppermute | solution.py:415
  55.9 32.1 %collective-permute-start.6 = (bf16[1024,512]{1,0:T(8,128)(2,1)}, bf16[1024,512]{1,0:T(8,128)(2,1)}, u32[]{:S(2)}, u32[]{:S(2)}) collective-permute-start(bf16[1024,512]{1,0:T(8,128)(2,1)} %get-tuple-element.21.refs_0_), channel_id=1, source_target_pairs={{0,1},{3,2},{4,5},{7,6},{8,9},{11,10},{12,13},{15,14},{16,17},{19,... | collective-permute-start | bytes 3145736 | tf_op jit(solution)/shard_map/even2_units0/ppermute | solution.py:415
  61.2 29.2 %collective-permute-start.5 = (bf16[1024,512]{1,0:T(8,128)(2,1)}, bf16[1024,512]{1,0:T(8,128)(2,1)}, u32[]{:S(2)}, u32[]{:S(2)}) collective-permute-start(bf16[1024,512]{1,0:T(8,128)(2,1)} %added.10.refs_4_), channel_id=1, source_target_pairs={{1,2},{2,1},{5,6},{6,5},{9,10},{10,9},{13,14},{14,13},{17,18},{18,... | collective-permute-start | bytes 3145736 | tf_op jit(solution)/shard_map/odd2_units0/ppermute | solution.py:415
  66.0 40.8 %collective-permute-start.8 = (bf16[1024,512]{1,0:T(8,128)(2,1)}, bf16[1024,512]{1,0:T(8,128)(2,1)}, u32[]{:S(2)}, u32[]{:S(2)}) collective-permute-start(bf16[1024,512]{1,0:T(8,128)(2,1)} %added.11.refs_4_), channel_id=1, source_target_pairs={{1,2},{2,1},{5,6},{6,5},{9,10},{10,9},{13,14},{14,13},{17,18},{18,... | collective-permute-start | bytes 3145736 | tf_op jit(solution)/shard_map/odd2_units4/ppermute | solution.py:415
  76.2 20.6 %collective-permute-start.4 = (bf16[2048,128]{1,0:T(8,128)(2,1)}, bf16[2048,128]{1,0:T(8,128)(2,1)}, u32[]{:S(2)}, u32[]{:S(2)}) collective-permute-start(bf16[2048,128]{1,0:T(8,128)(2,1)} %low_terms.1.refs_1_.refs_0_.refs_4_), channel_id=1, source_target_pairs={{0,1},{3,2},{4,5},{7,6},{8,9},{11,10},{12,13},{15,14},{16,17},{19,... | collective-permute-start | bytes 1572872 | tf_op jit(solution)/shard_map/low_sums1/ppermute | solution.py:426
  85.6 33.7 %collective-permute-start.10 = (bf16[1024,512]{1,0:T(8,128)(2,1)}, bf16[1024,512]{1,0:T(8,128)(2,1)}, u32[]{:S(2)}, u32[]{:S(2)}) collective-permute-start(bf16[1024,512]{1,0:T(8,128)(2,1)} %added.12.refs_2_), channel_id=1, source_target_pairs={{0,1},{3,2},{4,5},{7,6},{8,9},{11,10},{12,13},{15,14},{16,17},{19,... | collective-permute-start | bytes 3145736 | tf_op jit(solution)/shard_map/even2_units4/ppermute | solution.py:415
  99.0 10.0 %collective-permute-start.7 = (bf16[2048,128]{1,0:T(8,128)(2,1)}, bf16[2048,128]{1,0:T(8,128)(2,1)}, u32[]{:S(2)}, u32[]{:S(2)}) collective-permute-start(bf16[2048,128]{1,0:T(8,128)(2,1)} %added.15.refs_2_), channel_id=1, source_target_pairs={{1,2},{2,1},{5,6},{6,5},{9,10},{10,9},{13,14},{14,13},{17,18},{18,... | collective-permute-start | bytes 1572872 | tf_op jit(solution)/shard_map/low_sums2/ppermute | solution.py:426
  100.4 49.8 %collective-permute-start.14 = (bf16[1024,512]{1,0:T(8,128)(2,1)}, bf16[1024,512]{1,0:T(8,128)(2,1)}, u32[]{:S(2)}, u32[]{:S(2)}) collective-permute-start(bf16[1024,512]{1,0:T(8,128)(2,1)} %added.14.refs_2_), channel_id=1, source_target_pairs={{0,1},{1,0},{2,3},{3,2},{4,5},{5,4},{6,7},{7,6},{8,9},{9,8},{10,11... | collective-permute-start | bytes 3145736 | tf_op jit(solution)/shard_map/even3_units0/ppermute | solution.py:415
  105.2 45.0 %collective-permute-start.15 = (bf16[1024,512]{1,0:T(8,128)(2,1)}, bf16[1024,512]{1,0:T(8,128)(2,1)}, u32[]{:S(2)}, u32[]{:S(2)}) collective-permute-start(bf16[1024,512]{1,0:T(8,128)(2,1)} %added.13.refs_2_), channel_id=1, source_target_pairs={{1,2},{2,1},{5,6},{6,5},{9,10},{10,9},{13,14},{14,13},{17,18},{18,... | collective-permute-start | bytes 3145736 | tf_op jit(solution)/shard_map/odd3_units0/ppermute | solution.py:415
  121.8 33.9 %collective-permute-start.12 = (bf16[1024,512]{1,0:T(8,128)(2,1)}, bf16[1024,512]{1,0:T(8,128)(2,1)}, u32[]{:S(2)}, u32[]{:S(2)}) collective-permute-start(bf16[1024,512]{1,0:T(8,128)(2,1)} %added.18.refs_2_), channel_id=1, source_target_pairs={{1,2},{2,1},{5,6},{6,5},{9,10},{10,9},{13,14},{14,13},{17,18},{18,... | collective-permute-start | bytes 3145736 | tf_op jit(solution)/shard_map/odd3_units4/ppermute | solution.py:415
  123.4 21.0 %collective-permute-start.9 = (bf16[2048,128]{1,0:T(8,128)(2,1)}, bf16[2048,128]{1,0:T(8,128)(2,1)}, u32[]{:S(2)}, u32[]{:S(2)}) collective-permute-start(bf16[2048,128]{1,0:T(8,128)(2,1)} %added.17.refs_2_), channel_id=1, source_target_pairs={{2,3},{1,0},{6,7},{5,4},{10,11},{9,8},{14,15},{13,12},{18,19},{17,... | collective-permute-start | bytes 1572872 | tf_op jit(solution)/shard_map/low_sums3/ppermute | solution.py:426
  124.7 30.9 %collective-permute-start.13 = (bf16[512,512]{1,0:T(8,128)(2,1)}, bf16[512,512]{1,0:T(8,128)(2,1)}, u32[]{:S(2)}, u32[]{:S(2)}) collective-permute-start(bf16[512,512]{1,0:T(8,128)(2,1)} %added.16.refs_2_), channel_id=1, source_target_pairs={{0,1},{1,0},{2,3},{3,2},{4,5},{5,4},{6,7},{7,6},{8,9},{9,8},{10,11... | collective-permute-start | bytes 1572872 | tf_op jit(solution)/shard_map/even3_units4/ppermute | solution.py:415
  144.4 18.9 %collective-permute-start.11 = (bf16[512,512]{1,0:T(8,128)(2,1)}, bf16[512,512]{1,0:T(8,128)(2,1)}, u32[]{:S(2)}, u32[]{:S(2)}) collective-permute-start(bf16[512,512]{1,0:T(8,128)(2,1)} %added.19.refs_9_), channel_id=1, source_target_pairs={{0,1},{1,0},{2,3},{3,2},{4,5},{5,4},{6,7},{7,6},{8,9},{9,8},{10,11... | collective-permute-start | bytes 1572872 | tf_op jit(solution)/shard_map/even3_units6/ppermute | solution.py:415
Sparse Core Ops, SparseCore 0:
  9.2 57.0 all-gather.4
  88.1 22.0 all-gather.2

commit v3 on v2

--- a/solution.py
+++ b/solution.py
@@ -448,20 +448,19 @@
         partial[0] += cut(more_rows(hidden, flat, first, [first] * 3, []), first)
         for u in (2, 4, 6):
             send(1, 0, u, 2)
-        others = other_slots(
-            hidden,
-            key_value_weight,
-            place,
-            which[1:],
-            [[tok_rows // 2] * 2, [tok_rows], [tok_rows]],
-            chunk,
-            [partial[0][-1][1], arrived],
-        )
-        for s, arrays in enumerate(others):
-            partial[s + 1] = cut(arrays)
-        ordered(partial[3][0][1])
+
+        def others(s, cuts, after):
+            results = other_slots(
+                hidden, key_value_weight, place, which[s : s + len(cuts)], cuts, chunk, after
+            )
+            for k, arrays in enumerate(results):
+                partial[s + k] = cut(arrays)
+            ordered(results[0][0])
+
+        others(1, [[tok_rows // 2] * 2], [partial[0][-1][1], arrived])
         send(2, 0, 0, 4)
         send(2, 1, 0, 4)
+        others(2, [[tok_rows], [tok_rows]], list(last))
         send(2, 1, 4, 4)
         low_parts.append(ordered(low_terms(hidden, down_maps, tenant_per_block, list(last))))
         send_low(1)

time: 174 us -> 174 us (level)
  starting transfers between devices: 45.7 us -> 39.6 us
  Pallas kernels: 83.1 us -> 87.9 us
    pallas_call x1 -> x2, Pallas kernels: 23.6 us -> 27.9 us  [other_slots(): pl.pallas_call(body, name='other_slots', grid_spec=pltpu.PrefetchScalarGr...]
    ppermute x3, starting transfers between devices: 10.1 us -> 6.5 us  [send_low(): lax.ppermute(value, 'tp', [(time - 1, time), (n - time, n - time - 1)])]
    ppermute x13, starting transfers between devices: 35.5 us -> 33.1 us  [send(): moved = lax.ppermute(value, 'tp', moves)]
    ppermute x13, waiting for transfers between devices: 15.6 us -> 17.5 us  [send(): moved = lax.ppermute(value, 'tp', moves)]
  transfers between devices with their start and end apart: 18 -> 18, of which waited for: 6 -> 5; matrix products, arithmetic and copies ran while one was open for 0% -> 0% of each run, Pallas kernels for 47% -> 49%
where the time goes in v3:
time: 174 us; the launch traced here: 173 us
  Pallas kernels  87.9 us (51%)
  starting transfers between devices  39.6 us (23%)
  waiting for transfers between devices  31.9 us (18%)
  between operations  13.5 us (8%)
    ppermute x13, starting transfers between devices, send(): moved = lax.ppermute(value, 'tp', moves)  33.1 us
    pallas_call x2, Pallas kernels, other_slots(): pl.pallas_call(body, name='other_slots', grid_spec=pltpu.PrefetchScalarGr...  27.9 us
    pallas_call x10, Pallas kernels, added(): pl.pallas_call(body, name='added', grid=(rows // block,), in_specs=specs...  23.7 us
    ppermute x13, waiting for transfers between devices, send(): moved = lax.ppermute(value, 'tp', moves)  17.5 us
    ppermute x3, waiting for transfers between devices, send_low(): lax.ppermute(value, 'tp', [(time - 1, time), (n - time, n - time - 1)])  13.6 us
    pallas_call x1, Pallas kernels, low_terms(): pl.pallas_call(body, name='low_terms', grid_spec=pltpu.PrefetchScalarGrid...  9.13 us
    pallas_call x3, Pallas kernels, finish(): pl.pallas_call(body, name='finish', grid=(rows // block,), in_specs=specs...  8.56 us
    pallas_call x1, Pallas kernels, more_rows(): pl.pallas_call(body, name='more_rows', grid=(sum(cuts) // block,), in_spe...  8.08 us
  transfers between devices with their start and end apart: 18, of which 5 were waited for; matrix products, arithmetic and copies ran while one was open for 0% of the time, Pallas kernels for 49%

profile of v3, /device:TPU:0, one launch (start us, length us, event | category | flops | bytes accessed | tf_op | source)
XLA Modules:
  0.0 172.9 jit_solution(7798238937086986979)
XLA Ops:
  6.5 0.7 all-gather.5.cloned.1.call-update
  7.3 0.0 all-gather.3.cloned.1.call-start
  7.3 4.8 %first_piece.1 = (bf16[2048,512]{1,0:T(8,128)(2,1)}, bf16[512,512]{1,0:T(8,128)(2,1)}) custom-call(s32[1]{0:T(128)} %bitcast.which_ref, bf16[2048,2048]{1,0:T(8,128)(2,1)} %hidden_ref.9, bf16[2048,2,1024]{2,1,0:T(2,128)(2,1)} %refs_1_.1), custom_call_target="tpu_custom_call" | custom-call | flops 1 | bytes 5073750 | tf_op jit(solution)/shard_map/first_piece/pallas_call | solution.py:78
  12.1 5.7 %collective-permute-start.2 = (bf16[512,512]{1,0:T(8,128)(2,1)}, bf16[512,512]{1,0:T(8,128)(2,1)}, u32[]{:S(2)}, u32[]{:S(2)}) collective-permute-start(bf16[512,512]{1,0:T(8,128)(2,1)} %get-tuple-element.17.refs_0_), channel_id=1, source_target_pairs={{0,1},{3,2},{4,5},{7,6},{8,9},{11,10},{12,13},{15,14},{16,17},{19,... | collective-permute-start | bytes 1572872 | tf_op jit(solution)/shard_map/even1_units0/ppermute | solution.py:415
  17.9 8.1 %more_rows.1 = (bf16[512,512]{1,0:T(8,128)(2,1)}, bf16[512,512]{1,0:T(8,128)(2,1)}, bf16[512,512]{1,0:T(8,128)(2,1)}) custom-call(bf16[2048,2048]{1,0:T(8,128)(2,1)} %hidden_ref.9, bf16[2048,512]{1,0:T(8,128)(2,1)} %get-tuple-element.14.flat_ref), custom_call_target="tpu_custom_call" | custom-call | flops 1 | bytes 6918750 | tf_op jit(solution)/shard_map/more_rows/pallas_call | solution.py:134
  25.9 2.1 %collective-permute-start.3 = (bf16[512,512]{1,0:T(8,128)(2,1)}, bf16[512,512]{1,0:T(8,128)(2,1)}, u32[]{:S(2)}, u32[]{:S(2)}) collective-permute-start(bf16[512,512]{1,0:T(8,128)(2,1)} %get-tuple-element.18.refs_1_), channel_id=1, source_target_pairs={{0,1},{3,2},{4,5},{7,6},{8,9},{11,10},{12,13},{15,14},{16,17},{19,... | collective-permute-start | bytes 1572872 | tf_op jit(solution)/shard_map/even1_units2/ppermute | solution.py:415
  28.1 2.1 %collective-permute-start.1 = (bf16[512,512]{1,0:T(8,128)(2,1)}, bf16[512,512]{1,0:T(8,128)(2,1)}, u32[]{:S(2)}, u32[]{:S(2)}) collective-permute-start(bf16[512,512]{1,0:T(8,128)(2,1)} %get-tuple-element.16.refs_1_), channel_id=1, source_target_pairs={{0,1},{3,2},{4,5},{7,6},{8,9},{11,10},{12,13},{15,14},{16,17},{19,... | collective-permute-start | bytes 1572872 | tf_op jit(solution)/shard_map/even1_units6/ppermute | solution.py:415
  30.1 2.1 %collective-permute-start = (bf16[512,512]{1,0:T(8,128)(2,1)}, bf16[512,512]{1,0:T(8,128)(2,1)}, u32[]{:S(2)}, u32[]{:S(2)}) collective-permute-start(bf16[512,512]{1,0:T(8,128)(2,1)} %get-tuple-element.15.refs_0_), channel_id=1, source_target_pairs={{0,1},{3,2},{4,5},{7,6},{8,9},{11,10},{12,13},{15,14},{16,17},{19,... | collective-permute-start | bytes 1572872 | tf_op jit(solution)/shard_map/even1_units4/ppermute | solution.py:415
  32.2 0.0 collective-permute-done.2.refs_2_
  32.2 11.3 %other_slots.2 = (bf16[1024,512]{1,0:T(8,128)(2,1)}, bf16[1024,512]{1,0:T(8,128)(2,1)}) custom-call(s32[1]{0:T(128)} %bitcast.which_ref, bf16[2048,2048]{1,0:T(8,128)(2,1)} %hidden_ref.9, bf16[2048,2,1024]{2,1,0:T(2,128)(2,1)} %refs_1_.1, bf16[512,512]{1,0:T(8,128)(2,1)} %get-tuple-element.16.refs_1_, bf16[512,512]{1,0:T(8,128)(2,1)} %collective-permute-done.2.refs_2_), custom_call_target="tpu_custom_call" | custom-call | flops 1 | bytes 12177000 | tf_op jit(solution)/shard_map/other_slots/pallas_call | solution.py:187
  43.5 2.3 %collective-permute-start.6 = (bf16[1024,512]{1,0:T(8,128)(2,1)}, bf16[1024,512]{1,0:T(8,128)(2,1)}, u32[]{:S(2)}, u32[]{:S(2)}) collective-permute-start(bf16[1024,512]{1,0:T(8,128)(2,1)} %get-tuple-element.19.refs_4_.refs_0_), channel_id=1, source_target_pairs={{0,1},{3,2},{4,5},{7,6},{8,9},{11,10},{12,13},{15,14},{16,17},{19,... | collective-permute-start | bytes 3145736 | tf_op jit(solution)/shard_map/even2_units0/ppermute | solution.py:415
  45.8 2.9 %added.10.refs_2_ = bf16[1024,512]{1,0:T(8,128)(2,1)} custom-call(bf16[512,512]{1,0:T(8,128)(2,1)} %get-tuple-element.17.refs_0_, bf16[512,512]{1,0:T(8,128)(2,1)} %get-tuple-element.18.refs_1_, bf16[512,512]{1,0:T(8,128)(2,1)} %collective-permute-done.2.refs_2_, bf16[512,512]{1,0:T(8,128)(2,1)} %collective-permute-done.3.refs_3_, ...), custom_call_target="tpu_custom_call" | custom-call | flops 1 | bytes 2398500 | tf_op jit(solution)/shard_map/added/pallas_call | solution.py:244
  48.7 1.7 collective-permute-start.5
  50.3 16.6 %other_slots.3 = (bf16[2048,512]{1,0:T(8,128)(2,1)}, bf16[2048,512]{1,0:T(8,128)(2,1)}) custom-call(s32[1]{0:T(128)} %bitcast.which_ref, bf16[2048,2048]{1,0:T(8,128)(2,1)} %hidden_ref.9, bf16[2048,2,1024]{2,1,0:T(2,128)(2,1)} %refs_1_.1, bf16[2048,2,1024]{2,1,0:T(2,128)(2,1)} %refs_1_.1, bf16[1024,512]{1,0:T(8,128)(2,1)} %added.10.refs_2_), custom_call_target="tpu_custom_call" | custom-call | flops 1 | bytes 16974000 | tf_op jit(solution)/shard_map/other_slots/pallas_call | solution.py:187
  66.9 2.8 %added.11.refs_4_ = bf16[1024,512]{1,0:T(8,128)(2,1)} custom-call(bf16[512,512]{1,0:T(8,128)(2,1)} %get-tuple-element.15.refs_0_, bf16[512,512]{1,0:T(8,128)(2,1)} %get-tuple-element.16.refs_1_, bf16[512,512]{1,0:T(8,128)(2,1)} %collective-permute-done.refs_2_, bf16[512,512]{1,0:T(8,128)(2,1)} %collective-permute-done.1.refs_3_, ...), custom_call_target="tpu_custom_call" | custom-call | flops 1 | bytes 2398500 | tf_op jit(solution)/shard_map/added/pallas_call | solution.py:244
  69.8 1.7 collective-permute-start.8
  71.4 9.1 %low_terms.1.refs_1_.refs_0_.refs_4_ = bf16[2048,128]{1,0:T(8,128)(2,1)} custom-call(s32[16]{0:T(128)} %tenant_ref.3, bf16[2048,2048]{1,0:T(8,128)(2,1)} %hidden_ref.9, bf16[16,2048,128]{2,1,0:T(8,128)(2,1)} %all-gather.5.cloned.1.call-done.refs_0_.refs_1_.refs_2_.refs_3_, ...), custom_call_target="tpu_custom_call" | custom-call | flops 1 | bytes 7933500 | tf_op jit(solution)/shard_map/low_terms/pallas_call | solution.py:270
  80.5 3.8 %collective-permute-start.4 = (bf16[2048,128]{1,0:T(8,128)(2,1)}, bf16[2048,128]{1,0:T(8,128)(2,1)}, u32[]{:S(2)}, u32[]{:S(2)}) collective-permute-start(bf16[2048,128]{1,0:T(8,128)(2,1)} %low_terms.1.refs_1_.refs_0_.refs_4_), channel_id=1, source_target_pairs={{0,1},{3,2},{4,5},{7,6},{8,9},{11,10},{12,13},{15,14},{16,17},{19,... | collective-permute-start | bytes 1572872 | tf_op jit(solution)/shard_map/low_sums1/ppermute | solution.py:426
  84.3 2.0 %added.12.refs_2_ = bf16[1024,512]{1,0:T(8,128)(2,1)} custom-call(bf16[1024,512]{1,0:T(8,128)(2,1)} %get-tuple-element.21.refs_0_, bf16[2048,128]{1,0:T(8,128)(2,1)} %low_terms.1.refs_1_.refs_0_.refs_4_), custom_call_target="tpu_custom_call" | custom-call | flops 1 | bytes 2398500 | tf_op jit(solution)/shard_map/added/pallas_call | solution.py:244
  86.4 2.3 %collective-permute-start.10 = (bf16[1024,512]{1,0:T(8,128)(2,1)}, bf16[1024,512]{1,0:T(8,128)(2,1)}, u32[]{:S(2)}, u32[]{:S(2)}) collective-permute-start(bf16[1024,512]{1,0:T(8,128)(2,1)} %added.12.refs_2_), channel_id=1, source_target_pairs={{0,1},{3,2},{4,5},{7,6},{8,9},{11,10},{12,13},{15,14},{16,17},{19,... | collective-permute-start | bytes 3145736 | tf_op jit(solution)/shard_map/even2_units4/ppermute | solution.py:415
  88.6 0.0 all-gather.3.cloned.1.call-update
  88.7 0.0 collective-permute-done.6.refs_1_
  88.7 2.5 %added.13.refs_2_ = bf16[1024,512]{1,0:T(8,128)(2,1)} custom-call(bf16[1024,512]{1,0:T(8,128)(2,1)} %get-tuple-element.19.refs_4_.refs_0_, bf16[1024,512]{1,0:T(8,128)(2,1)} %collective-permute-done.6.refs_1_, bf16[1024,512]{1,0:T(8,128)(2,1)} %added.12.refs_2_), custom_call_target="tpu_custom_call" | custom-call | flops 1 | bytes 2398500 | tf_op jit(solution)/shard_map/added/pallas_call | solution.py:244
  91.1 0.0 collective-permute-done.5.refs_1_
  91.1 2.5 %added.14.refs_2_ = bf16[1024,512]{1,0:T(8,128)(2,1)} custom-call(bf16[2048,512]{1,0:T(8,128)(2,1)} %get-tuple-element.20.refs_4_.refs_0_, bf16[1024,512]{1,0:T(8,128)(2,1)} %collective-permute-done.5.refs_1_, bf16[1024,512]{1,0:T(8,128)(2,1)} %added.13.refs_2_), custom_call_target="tpu_custom_call" | custom-call | flops 1 | bytes 2398500 | tf_op jit(solution)/shard_map/added/pallas_call | solution.py:244
  93.6 3.4 %collective-permute-done.4.refs_1_.refs_5_ = bf16[2048,128]{1,0:T(8,128)(2,1)} collective-permute-done((bf16[2048,128]{1,0:T(8,128)(2,1)}, bf16[2048,128]{1,0:T(8,128)(2,1)}, u32[]{:S(2)}, u32[]{:S(2)}) %collective-permute-start.4) | collective-permute-done | bytes 524320 | tf_op jit(solution)/shard_map/low_sums1/ppermute | solution.py:426
  97.0 2.1 %added.15.refs_2_ = bf16[2048,128]{1,0:T(8,128)(2,1)} custom-call(bf16[2048,128]{1,0:T(8,128)(2,1)} %low_terms.1.refs_1_.refs_0_.refs_4_, bf16[2048,128]{1,0:T(8,128)(2,1)} %collective-permute-done.4.refs_1_.refs_5_, bf16[1024,512]{1,0:T(8,128)(2,1)} %added.14.refs_2_), custom_call_target="tpu_custom_call" | custom-call | flops 1 | bytes 1199250 | tf_op jit(solution)/shard_map/added/pallas_call | solution.py:244
  99.1 1.5 collective-permute-start.7
  100.6 4.7 %collective-permute-start.14 = (bf16[1024,512]{1,0:T(8,128)(2,1)}, bf16[1024,512]{1,0:T(8,128)(2,1)}, u32[]{:S(2)}, u32[]{:S(2)}) collective-permute-start(bf16[1024,512]{1,0:T(8,128)(2,1)} %added.14.refs_2_), channel_id=1, source_target_pairs={{0,1},{1,0},{2,3},{3,2},{4,5},{5,4},{6,7},{7,6},{8,9},{9,8},{10,11... | collective-permute-start | bytes 3145736 | tf_op jit(solution)/shard_map/even3_units0/ppermute | solution.py:415
  105.3 1.6 collective-permute-start.15
  106.9 0.0 collective-permute-done.8.refs_1_
  106.9 2.2 %added.16.refs_2_ = bf16[512,512]{1,0:T(8,128)(2,1)} custom-call(bf16[2048,512]{1,0:T(8,128)(2,1)} %get-tuple-element.20.refs_4_.refs_0_, bf16[1024,512]{1,0:T(8,128)(2,1)} %collective-permute-done.8.refs_1_, bf16[2048,128]{1,0:T(8,128)(2,1)} %added.15.refs_2_), custom_call_target="tpu_custom_call" | custom-call | flops 1 | bytes 1199250 | tf_op jit(solution)/shard_map/added/pallas_call | solution.py:244
  109.1 0.0 collective-permute-done.7.refs_1_.refs_6_
  109.1 2.1 %added.17.refs_2_ = bf16[2048,128]{1,0:T(8,128)(2,1)} custom-call(bf16[2048,128]{1,0:T(8,128)(2,1)} %low_terms.1.refs_1_.refs_0_.refs_4_, bf16[2048,128]{1,0:T(8,128)(2,1)} %collective-permute-done.7.refs_1_.refs_6_, bf16[512,512]{1,0:T(8,128)(2,1)} %added.16.refs_2_), custom_call_target="tpu_custom_call" | custom-call | flops 1 | bytes 1199250 | tf_op jit(solution)/shard_map/added/pallas_call | solution.py:244
  111.2 8.3 %collective-permute-done.10.refs_1_ = bf16[1024,512]{1,0:T(8,128)(2,1)} collective-permute-done((bf16[1024,512]{1,0:T(8,128)(2,1)}, bf16[1024,512]{1,0:T(8,128)(2,1)}, u32[]{:S(2)}, u32[]{:S(2)}) %collective-permute-start.10) | collective-permute-done | bytes 1048608 | tf_op jit(solution)/shard_map/even2_units4/ppermute | solution.py:415
  119.5 2.5 %added.18.refs_2_ = bf16[1024,512]{1,0:T(8,128)(2,1)} custom-call(bf16[1024,512]{1,0:T(8,128)(2,1)} %get-tuple-element.21.refs_0_, bf16[1024,512]{1,0:T(8,128)(2,1)} %collective-permute-done.10.refs_1_, bf16[2048,128]{1,0:T(8,128)(2,1)} %added.17.refs_2_), custom_call_target="tpu_custom_call" | custom-call | flops 1 | bytes 2398500 | tf_op jit(solution)/shard_map/added/pallas_call | solution.py:244
  122.0 1.6 collective-permute-start.12
  123.6 1.3 collective-permute-start.9
  124.9 5.2 %collective-permute-start.13 = (bf16[512,512]{1,0:T(8,128)(2,1)}, bf16[512,512]{1,0:T(8,128)(2,1)}, u32[]{:S(2)}, u32[]{:S(2)}) collective-permute-start(bf16[512,512]{1,0:T(8,128)(2,1)} %added.16.refs_2_), channel_id=1, source_target_pairs={{0,1},{1,0},{2,3},{3,2},{4,5},{5,4},{6,7},{7,6},{8,9},{9,8},{10,11... | collective-permute-start | bytes 1572872 | tf_op jit(solution)/shard_map/even3_units4/ppermute | solution.py:415
  130.1 2.1 %added.19.refs_9_ = bf16[512,512]{1,0:T(8,128)(2,1)} custom-call(bf16[2048,512]{1,0:T(8,128)(2,1)} %get-tuple-element.20.refs_4_.refs_0_, bf16[1024,512]{1,0:T(8,128)(2,1)} %collective-permute-done.8.refs_1_, bf16[1024,512]{1,0:T(8,128)(2,1)} %added.18.refs_2_), custom_call_target="tpu_custom_call" | custom-call | flops 1 | bytes 1199250 | tf_op jit(solution)/shard_map/added/pallas_call | solution.py:244
  132.3 10.2 %collective-permute-done.9.refs_7_ = bf16[2048,128]{1,0:T(8,128)(2,1)} collective-permute-done((bf16[2048,128]{1,0:T(8,128)(2,1)}, bf16[2048,128]{1,0:T(8,128)(2,1)}, u32[]{:S(2)}, u32[]{:S(2)}) %collective-permute-start.9) | collective-permute-done | bytes 524320 | tf_op jit(solution)/shard_map/low_sums3/ppermute | solution.py:426
  142.5 5.7 %with_adapter.1.refs_0_ = bf16[2048,512]{1,0:T(8,128)(2,1)} custom-call(s32[16]{0:T(128)} %tenant_ref.3, bf16[16,2,64,256]{3,2,1,0:T(8,128)(2,1)} %all-gather.3.cloned.1.call-done.refs_0_.refs_1_.refs_2_.refs_3_, bf16[16,2,64,256]{3,2,1,0:T(8,128)(2,1)} %all-gather.3.cloned.1.call-done.refs_0_.refs_1_.refs_2_.refs_3_, ...), custom_call_target="tpu_custom_call" | custom-call | flops 1 | bytes 7380000 | tf_op jit(solution)/shard_map/with_adapter/pallas_call | solution.py:315
  148.2 0.0 collective-permute-done.14.refs_1_
  148.2 3.2 %finish.3.refs_3_ = bf16[2048,2,256]{2,1,0:T(2,128)(2,1)} custom-call(bf16[2048,512]{1,0:T(8,128)(2,1)} %with_adapter.1.refs_0_, bf16[1024,512]{1,0:T(8,128)(2,1)} %collective-permute-done.14.refs_1_, bf16[1024,512]{1,0:T(8,128)(2,1)} %collective-permute-done.15.refs_2_), custom_call_target="tpu_custom_call" | custom-call | flops 1 | bytes 2398500 | tf_op jit(solution)/shard_map/finish/pallas_call | solution.py:351
  151.5 2.3 %collective-permute-done.13.refs_1_ = bf16[512,512]{1,0:T(8,128)(2,1)} collective-permute-done((bf16[512,512]{1,0:T(8,128)(2,1)}, bf16[512,512]{1,0:T(8,128)(2,1)}, u32[]{:S(2)}, u32[]{:S(2)}) %collective-permute-start.13) | collective-permute-done | bytes 524320 | tf_op jit(solution)/shard_map/even3_units4/ppermute | solution.py:415
  153.7 2.7 %finish.4.refs_3_ = bf16[2048,2,256]{2,1,0:T(2,128)(2,1)} custom-call(bf16[2048,512]{1,0:T(8,128)(2,1)} %with_adapter.1.refs_0_, bf16[512,512]{1,0:T(8,128)(2,1)} %collective-permute-done.13.refs_1_, bf16[1024,512]{1,0:T(8,128)(2,1)} %collective-permute-done.12.refs_2_, bf16[2048,2,256]{2,1,0:T(2,128)(2,1)} %finish.3.refs_3_), custom_call_target="tpu_custom_call", output_to_operand_aliasing={{}: (3, {})} | custom-call | flops 1 | bytes 1199250 | tf_op jit(solution)/shard_map/finish/pallas_call | solution.py:351
  156.4 7.0 %collective-permute-done.11.refs_1_ = bf16[512,512]{1,0:T(8,128)(2,1)} collective-permute-done((bf16[512,512]{1,0:T(8,128)(2,1)}, bf16[512,512]{1,0:T(8,128)(2,1)}, u32[]{:S(2)}, u32[]{:S(2)}) %collective-permute-start.11) | collective-permute-done | bytes 524320 | tf_op jit(solution)/shard_map/even3_units6/ppermute | solution.py:415
  163.4 2.7 %finish.5 = bf16[2048,2,256]{2,1,0:T(2,128)(2,1)} custom-call(bf16[2048,512]{1,0:T(8,128)(2,1)} %with_adapter.1.refs_0_, bf16[512,512]{1,0:T(8,128)(2,1)} %collective-permute-done.11.refs_1_, bf16[1024,512]{1,0:T(8,128)(2,1)} %collective-permute-done.12.refs_2_, bf16[2048,2,256]{2,1,0:T(2,128)(2,1)} %finish.4.refs_3_), custom_call_target="tpu_custom_call", output_to_operand_aliasing={{}: (3, {})} | custom-call | flops 1 | bytes 1199250 | tf_op jit(solution)/shard_map/finish/pallas_call | solution.py:351
  (9 shorter events, 0.0 us)
Async XLA Ops:
  6.5 64.9 %all-gather.5.cloned.1.call-start = ((), (), s32[]{:S(2)}) async-start(), calls=%async_computation.1 | async-start | bytes 9437184 | tf_op jit(solution)/shard_map/all_gather | solution.py:370
  7.3 135.2 %all-gather.3.cloned.1.call-start = ((), (), s32[]{:S(2)}) async-start(), calls=%async_computation | async-start | bytes 1179648 | tf_op jit(solution)/shard_map/all_gather | solution.py:371
  12.1 20.1 %collective-permute-start.2 = (bf16[512,512]{1,0:T(8,128)(2,1)}, bf16[512,512]{1,0:T(8,128)(2,1)}, u32[]{:S(2)}, u32[]{:S(2)}) collective-permute-start(bf16[512,512]{1,0:T(8,128)(2,1)} %get-tuple-element.17.refs_0_), channel_id=1, source_target_pairs={{0,1},{3,2},{4,5},{7,6},{8,9},{11,10},{12,13},{15,14},{16,17},{19,... | collective-permute-start | bytes 1572872 | tf_op jit(solution)/shard_map/even1_units0/ppermute | solution.py:415
  25.9 19.8 %collective-permute-start.3 = (bf16[512,512]{1,0:T(8,128)(2,1)}, bf16[512,512]{1,0:T(8,128)(2,1)}, u32[]{:S(2)}, u32[]{:S(2)}) collective-permute-start(bf16[512,512]{1,0:T(8,128)(2,1)} %get-tuple-element.18.refs_1_), channel_id=1, source_target_pairs={{0,1},{3,2},{4,5},{7,6},{8,9},{11,10},{12,13},{15,14},{16,17},{19,... | collective-permute-start | bytes 1572872 | tf_op jit(solution)/shard_map/even1_units2/ppermute | solution.py:415
  28.1 38.9 %collective-permute-start.1 = (bf16[512,512]{1,0:T(8,128)(2,1)}, bf16[512,512]{1,0:T(8,128)(2,1)}, u32[]{:S(2)}, u32[]{:S(2)}) collective-permute-start(bf16[512,512]{1,0:T(8,128)(2,1)} %get-tuple-element.16.refs_1_), channel_id=1, source_target_pairs={{0,1},{3,2},{4,5},{7,6},{8,9},{11,10},{12,13},{15,14},{16,17},{19,... | collective-permute-start | bytes 1572872 | tf_op jit(solution)/shard_map/even1_units6/ppermute | solution.py:415
  30.1 36.8 %collective-permute-start = (bf16[512,512]{1,0:T(8,128)(2,1)}, bf16[512,512]{1,0:T(8,128)(2,1)}, u32[]{:S(2)}, u32[]{:S(2)}) collective-permute-start(bf16[512,512]{1,0:T(8,128)(2,1)} %get-tuple-element.15.refs_0_), channel_id=1, source_target_pairs={{0,1},{3,2},{4,5},{7,6},{8,9},{11,10},{12,13},{15,14},{16,17},{19,... | collective-permute-start | bytes 1572872 | tf_op jit(solution)/shard_map/even1_units4/ppermute | solution.py:415
  43.5 45.2 %collective-permute-start.6 = (bf16[1024,512]{1,0:T(8,128)(2,1)}, bf16[1024,512]{1,0:T(8,128)(2,1)}, u32[]{:S(2)}, u32[]{:S(2)}) collective-permute-start(bf16[1024,512]{1,0:T(8,128)(2,1)} %get-tuple-element.19.refs_4_.refs_0_), channel_id=1, source_target_pairs={{0,1},{3,2},{4,5},{7,6},{8,9},{11,10},{12,13},{15,14},{16,17},{19,... | collective-permute-start | bytes 3145736 | tf_op jit(solution)/shard_map/even2_units0/ppermute | solution.py:415
  48.7 42.5 %collective-permute-start.5 = (bf16[1024,512]{1,0:T(8,128)(2,1)}, bf16[1024,512]{1,0:T(8,128)(2,1)}, u32[]{:S(2)}, u32[]{:S(2)}) collective-permute-start(bf16[1024,512]{1,0:T(8,128)(2,1)} %added.10.refs_2_), channel_id=1, source_target_pairs={{1,2},{2,1},{5,6},{6,5},{9,10},{10,9},{13,14},{14,13},{17,18},{18,... | collective-permute-start | bytes 3145736 | tf_op jit(solution)/shard_map/odd2_units0/ppermute | solution.py:415
  69.8 37.1 %collective-permute-start.8 = (bf16[1024,512]{1,0:T(8,128)(2,1)}, bf16[1024,512]{1,0:T(8,128)(2,1)}, u32[]{:S(2)}, u32[]{:S(2)}) collective-permute-start(bf16[1024,512]{1,0:T(8,128)(2,1)} %added.11.refs_4_), channel_id=1, source_target_pairs={{1,2},{2,1},{5,6},{6,5},{9,10},{10,9},{13,14},{14,13},{17,18},{18,... | collective-permute-start | bytes 3145736 | tf_op jit(solution)/shard_map/odd2_units4/ppermute | solution.py:415
  80.5 16.5 %collective-permute-start.4 = (bf16[2048,128]{1,0:T(8,128)(2,1)}, bf16[2048,128]{1,0:T(8,128)(2,1)}, u32[]{:S(2)}, u32[]{:S(2)}) collective-permute-start(bf16[2048,128]{1,0:T(8,128)(2,1)} %low_terms.1.refs_1_.refs_0_.refs_4_), channel_id=1, source_target_pairs={{0,1},{3,2},{4,5},{7,6},{8,9},{11,10},{12,13},{15,14},{16,17},{19,... | collective-permute-start | bytes 1572872 | tf_op jit(solution)/shard_map/low_sums1/ppermute | solution.py:426
  86.4 33.1 %collective-permute-start.10 = (bf16[1024,512]{1,0:T(8,128)(2,1)}, bf16[1024,512]{1,0:T(8,128)(2,1)}, u32[]{:S(2)}, u32[]{:S(2)}) collective-permute-start(bf16[1024,512]{1,0:T(8,128)(2,1)} %added.12.refs_2_), channel_id=1, source_target_pairs={{0,1},{3,2},{4,5},{7,6},{8,9},{11,10},{12,13},{15,14},{16,17},{19,... | collective-permute-start | bytes 3145736 | tf_op jit(solution)/shard_map/even2_units4/ppermute | solution.py:415
  99.1 9.9 %collective-permute-start.7 = (bf16[2048,128]{1,0:T(8,128)(2,1)}, bf16[2048,128]{1,0:T(8,128)(2,1)}, u32[]{:S(2)}, u32[]{:S(2)}) collective-permute-start(bf16[2048,128]{1,0:T(8,128)(2,1)} %added.15.refs_2_), channel_id=1, source_target_pairs={{1,2},{2,1},{5,6},{6,5},{9,10},{10,9},{13,14},{14,13},{17,18},{18,... | collective-permute-start | bytes 1572872 | tf_op jit(solution)/shard_map/low_sums2/ppermute | solution.py:426
  100.6 47.6 %collective-permute-start.14 = (bf16[1024,512]{1,0:T(8,128)(2,1)}, bf16[1024,512]{1,0:T(8,128)(2,1)}, u32[]{:S(2)}, u32[]{:S(2)}) collective-permute-start(bf16[1024,512]{1,0:T(8,128)(2,1)} %added.14.refs_2_), channel_id=1, source_target_pairs={{0,1},{1,0},{2,3},{3,2},{4,5},{5,4},{6,7},{7,6},{8,9},{9,8},{10,11... | collective-permute-start | bytes 3145736 | tf_op jit(solution)/shard_map/even3_units0/ppermute | solution.py:415
  105.3 42.9 %collective-permute-start.15 = (bf16[1024,512]{1,0:T(8,128)(2,1)}, bf16[1024,512]{1,0:T(8,128)(2,1)}, u32[]{:S(2)}, u32[]{:S(2)}) collective-permute-start(bf16[1024,512]{1,0:T(8,128)(2,1)} %added.13.refs_2_), channel_id=1, source_target_pairs={{1,2},{2,1},{5,6},{6,5},{9,10},{10,9},{13,14},{14,13},{17,18},{18,... | collective-permute-start | bytes 3145736 | tf_op jit(solution)/shard_map/odd3_units0/ppermute | solution.py:415
  122.0 31.7 %collective-permute-start.12 = (bf16[1024,512]{1,0:T(8,128)(2,1)}, bf16[1024,512]{1,0:T(8,128)(2,1)}, u32[]{:S(2)}, u32[]{:S(2)}) collective-permute-start(bf16[1024,512]{1,0:T(8,128)(2,1)} %added.18.refs_2_), channel_id=1, source_target_pairs={{1,2},{2,1},{5,6},{6,5},{9,10},{10,9},{13,14},{14,13},{17,18},{18,... | collective-permute-start | bytes 3145736 | tf_op jit(solution)/shard_map/odd3_units4/ppermute | solution.py:415
  123.6 18.9 %collective-permute-start.9 = (bf16[2048,128]{1,0:T(8,128)(2,1)}, bf16[2048,128]{1,0:T(8,128)(2,1)}, u32[]{:S(2)}, u32[]{:S(2)}) collective-permute-start(bf16[2048,128]{1,0:T(8,128)(2,1)} %added.17.refs_2_), channel_id=1, source_target_pairs={{2,3},{1,0},{6,7},{5,4},{10,11},{9,8},{14,15},{13,12},{18,19},{17,... | collective-permute-start | bytes 1572872 | tf_op jit(solution)/shard_map/low_sums3/ppermute | solution.py:426
  124.9 28.8 %collective-permute-start.13 = (bf16[512,512]{1,0:T(8,128)(2,1)}, bf16[512,512]{1,0:T(8,128)(2,1)}, u32[]{:S(2)}, u32[]{:S(2)}) collective-permute-start(bf16[512,512]{1,0:T(8,128)(2,1)} %added.16.refs_2_), channel_id=1, source_target_pairs={{0,1},{1,0},{2,3},{3,2},{4,5},{5,4},{6,7},{7,6},{8,9},{9,8},{10,11... | collective-permute-start | bytes 1572872 | tf_op jit(solution)/shard_map/even3_units4/ppermute | solution.py:415
  142.5 20.9 %collective-permute-start.11 = (bf16[512,512]{1,0:T(8,128)(2,1)}, bf16[512,512]{1,0:T(8,128)(2,1)}, u32[]{:S(2)}, u32[]{:S(2)}) collective-permute-start(bf16[512,512]{1,0:T(8,128)(2,1)} %added.19.refs_9_), channel_id=1, source_target_pairs={{0,1},{1,0},{2,3},{3,2},{4,5},{5,4},{6,7},{7,6},{8,9},{9,8},{10,11... | collective-permute-start | bytes 1572872 | tf_op jit(solution)/shard_map/even3_units6/ppermute | solution.py:415
Sparse Core Ops, SparseCore 0:
  9.2 57.0 all-gather.4
  88.8 23.1 all-gather.2

commit v4 on v3

--- a/solution.py
+++ b/solution.py
@@ -53,12 +53,13 @@
 HERE = pl.BlockSpec(memory_space=pl.ANY)
 
 
-def first_piece(hidden, weight, place, which, rows, chunk):
+def first_piece(hidden, weight, place, which, rows, chunk, after):
     width = hidden.shape[1]
     steps = 2
     depth = width // steps
 
-    def body(which_ref, hidden_ref, weight_ref, flat_ref, out_ref, total):
+    def body(place_ref, hidden_ref, weight_ref, *refs):
+        flat_ref, out_ref, total = refs[-3:]
         k = pl.program_id(0)
         flat_ref[...] = weight_ref[...].reshape(depth, 2 * chunk)
         term = jnp.dot(hidden_ref[...], flat_ref[...], preferred_element_type=jnp.float32)
@@ -84,7 +85,8 @@
             in_specs=[
                 pl.BlockSpec((rows, depth), lambda k, c: (0, k)),
                 pl.BlockSpec((depth, 2, chunk), lambda k, c: (k, 0, chunk_of(which, c[0]))),
-            ],
+            ]
+            + [HERE] * len(after),
             out_specs=[
                 pl.BlockSpec((depth, 2 * chunk), lambda k, c: (k, 0)),
                 pl.BlockSpec((rows, 2 * chunk), lambda k, c: (0, 0)),
@@ -97,7 +99,7 @@
         ],
         compiler_params=params(),
         cost_estimate=estimate(5.5),
-    )(place, hidden, weight)
+    )(place, hidden, weight, *after)
 
 
 def row_outputs(cuts, block, columns):
@@ -253,18 +255,57 @@
     )(*operands, *after)
 
 
-def low_terms(hidden, down_maps, tenants, after):
+def copied(arrays, after):
+    count, rows, columns = arrays[0].shape
+
+    def body(*refs):
+        for k in range(len(arrays)):
+            refs[k - len(arrays)][...] = refs[k][...]
+
+    block = pl.BlockSpec((1, rows, columns), lambda i: (i, 0, 0))
+    return pl.pallas_call(
+        body,
+        name="copied",
+        grid=(count,),
+        in_specs=[block] * len(arrays) + [HERE] * len(after),
+        out_specs=[block] * len(arrays),
+        out_shape=[jax.ShapeDtypeStruct(array.shape, array.dtype) for array in arrays],
+        compiler_params=params(),
+        cost_estimate=estimate(2),
+    )(*arrays, *after)
+
+
+def low_terms(hidden, sources, places, after):
     tok_rows, width = hidden.shape
-    count = tenants.shape[0]
+    count = places.shape[0]
     rows = tok_rows // count
-    columns = down_maps.shape[2]
-    per = 4 if count % 4 == 0 else 1
-
-    def body(tenant_ref, hidden_ref, *refs):
+    length, _, columns = sources[0].shape
+    per = 4
+
+    def body(place_ref, hidden_ref, *refs):
+        source_refs = refs[: len(sources)]
+        out_ref, maps, sems = refs[-3:]
+        i = pl.program_id(0)
+
+        def fetch(source, index, b):
+            return pltpu.make_async_copy(source.at[index, pl.ds(0, width)], maps.at[b], sems.at[b])
+
+        @pl.when(i == 0)
+        def _():
+            for b in range(count):
+                place = place_ref[b]
+                for k, source in enumerate(source_refs):
+
+                    @pl.when(place // length == k)
+                    def _(source=source, place=place, b=b, k=k):
+                        fetch(source, place - k * length, b).start()
+
         for k in range(per):
+            b = i * per + k
+            fetch(source_refs[0], 0, b).wait()
             part = slice(k * rows, (k + 1) * rows)
-            refs[-1][part, :] = jnp.dot(
-                hidden_ref[part, :], refs[k][0], preferred_element_type=jnp.float32
+            out_ref[part, :] = jnp.dot(
+                hidden_ref[part, :], maps[b], preferred_element_type=jnp.float32
             ).astype(jnp.bfloat16)
 
     return pl.pallas_call(
@@ -274,30 +315,31 @@
             num_scalar_prefetch=1,
             grid=(count // per,),
             in_specs=[pl.BlockSpec((per * rows, width), lambda b, t: (b, 0))]
-            + [
-                pl.BlockSpec((1, width, columns), lambda b, t, k=k: (t[b * per + k], 0, 0))
-                for k in range(per)
-            ]
-            + [HERE] * len(after),
+            + [HERE] * (len(sources) + len(after)),
             out_specs=pl.BlockSpec((per * rows, columns), lambda b, t: (b, 0)),
+            scratch_shapes=[
+                pltpu.VMEM((count, width, columns), jnp.bfloat16),
+                pltpu.SemaphoreType.DMA((count,)),
+            ],
         ),
         out_shape=jax.ShapeDtypeStruct((tok_rows, columns), jnp.bfloat16),
         compiler_params=params(),
         cost_estimate=estimate(8.6),
-    )(tenants, hidden, *[down_maps] * per, *after)
-
-
-def with_adapter(start, rows, terms, low_parts, up_maps, tenants, after):
+    )(places, hidden, *sources, *after)
+
+
+def finish(start, rows, block, out_rows, terms, low_parts, up_maps, tenants, previous, after):
     rank, chunk = up_maps.shape[2:]
     blk_rows = low_parts[0].shape[0] // tenants.shape[0]
-    block = 512
     per = block // blk_rows
     skip = start // block
     specs, operands, layout = segment_specs(terms, start, block)
     n_low = len(low_parts)
+    kept = [] if previous is None else [previous]
 
     def body(tenant_ref, *refs):
         up_refs, low_refs, term_refs = refs[:per], refs[per : per + n_low], refs[per + n_low :]
+        out_ref = refs[-1]
         low = low_refs[0][...].astype(jnp.float32)
         for ref in low_refs[1:]:
             low = low + ref[...].astype(jnp.float32)
@@ -305,16 +347,21 @@
         total = term_sum(pl.program_id(0), term_refs, layout)
         for k in range(per):
             part = slice(k * blk_rows, (k + 1) * blk_rows)
-            for h in range(2):
-                columns = slice(h * chunk, (h + 1) * chunk)
-                adapt = jnp.dot(
-                    low[part, h * rank : (h + 1) * rank], up_refs[k][0, h], preferred_element_type=jnp.float32
-                )
-                refs[-1][part, columns] = (total[part, columns] + adapt).astype(jnp.bfloat16)
-
+            adapt = jnp.concatenate(
+                [
+                    jnp.dot(
+                        low[part, h * rank : (h + 1) * rank], up_refs[k][0, h], preferred_element_type=jnp.float32
+                    )
+                    for h in range(2)
+                ],
+                axis=1,
+            )
+            out_ref[part] = (total[part] + adapt).astype(jnp.bfloat16).reshape(blk_rows, 2, chunk)
+
+    operands = [up_maps] * per + list(low_parts) + operands + list(after) + kept
     return pl.pallas_call(
         body,
-        name="with_adapter",
+        name="finish",
         grid_spec=pltpu.PrefetchScalarGridSpec(
             num_scalar_prefetch=1,
             grid=(rows // block,),
@@ -324,51 +371,21 @@
             ]
             + [pl.BlockSpec((block, 2 * rank), lambda b, t: (skip + b, 0)) for _ in low_parts]
             + specs
-            + [HERE] * len(after),
-            out_specs=pl.BlockSpec((block, 2 * chunk), lambda b, t: (b, 0)),
+            + [HERE] * (len(after) + len(kept)),
+            out_specs=pl.BlockSpec((block, 2, chunk), lambda b, t: (skip + b, 0, 0)),
         ),
-        out_shape=jax.ShapeDtypeStruct((rows, 2 * chunk), jnp.bfloat16),
+        out_shape=jax.ShapeDtypeStruct((out_rows, 2, chunk), jnp.bfloat16),
+        input_output_aliases={len(operands): 0} if kept else {},
         compiler_params=params(),
         cost_estimate=estimate(2 * rows / block),
-    )(tenants, *[up_maps] * per, *low_parts, *operands, *after)
-
-
-def finish(start, rows, out_rows, terms, previous):
-    chunk = terms[0][0][1].shape[1] // 2
-    block = 512 if rows % 512 == start % 512 == 0 else 256
-    skip = start // block
-    specs, operands, layout = segment_specs(terms, start, block)
-    aliases = {}
-    if previous is not None:
-        aliases = {len(operands): 0}
-        specs.append(HERE)
-        operands.append(previous)
-
-    def body(*refs):
-        total = term_sum(pl.program_id(0), refs, layout)
-        refs[-1][...] = total.astype(jnp.bfloat16).reshape(block, 2, chunk)
-
-    return pl.pallas_call(
-        body,
-        name="finish",
-        grid=(rows // block,),
-        in_specs=specs,
-        out_specs=pl.BlockSpec((block, 2, chunk), lambda i: (skip + i, 0, 0)),
-        out_shape=jax.ShapeDtypeStruct((out_rows, 2, chunk), jnp.bfloat16),
-        input_output_aliases=aliases,
-        compiler_params=params(),
-        cost_estimate=estimate(1.3 * rows / block),
-    )(*operands)
-
-
-def local(n, hidden, key_value_weight, adapter_down_weight, adapter_up_weight, tenant_per_block):
+    )(tenants, *operands)
+
+
+def local(n, n_tok, hidden, key_value_weight, adapter_down_weight, adapter_up_weight, tenant_per_block):
     tok_rows, local_width = hidden.shape
     chunk = adapter_up_weight.shape[3]
     unit = tok_rows // UNITS
     slots, sends = line_plan(n)
-
-    down_maps = lax.all_gather(adapter_down_weight, "tok", axis=0, tiled=True)
-    up_maps = lax.all_gather(adapter_up_weight, "tok", axis=0, tiled=True)
 
     place = lax.axis_index("tp").reshape(1)
     which = slots.T
@@ -425,79 +442,89 @@
         with jax.named_scope(f"low_sums{time}"):
             low_parts.append(lax.ppermute(value, "tp", [(time - 1, time), (n - time, n - time - 1)]))
 
-    ready = []
-
-    def prepare(u, count):
+    result = [None]
+
+    def complete(u, count, block, after=()):
         start, rows = u * unit, count * unit
         terms = [pick(partial[n - 1], start, rows)]
-        value = with_adapter(start, rows, terms, low_parts, up_maps, tenant_per_block, list(last))
-        ready.append((start, ordered(value)))
-
-    result = [None]
-
-    def complete(u, count):
-        start, rows = u * unit, count * unit
-        terms = [pick(ready, start, rows)] + [pick(received[n - 1, parity], start, rows) for parity in (0, 1)]
-        result[0] = finish(start, rows, tok_rows, terms, result[0])
-
-    first = 2 * unit
-    flat, head = first_piece(hidden, key_value_weight, place, which[0], first, chunk)
-    partial[0] = [(0, head)]
-    if n == 4:
-        arrived = send(1, 0, 0, 2)
-        partial[0] += cut(more_rows(hidden, flat, first, [first] * 3, []), first)
-        for u in (2, 4, 6):
-            send(1, 0, u, 2)
-
-        def others(s, cuts, after):
-            results = other_slots(
-                hidden, key_value_weight, place, which[s : s + len(cuts)], cuts, chunk, after
-            )
-            for k, arrays in enumerate(results):
-                partial[s + k] = cut(arrays)
-            ordered(results[0][0])
-
-        others(1, [[tok_rows // 2] * 2], [partial[0][-1][1], arrived])
+        terms += [pick(received[n - 1, parity], start, rows) for parity in (0, 1)]
+        result[0] = finish(
+            start, rows, block, tok_rows, terms, low_parts, up_maps, tenant_per_block, result[0], after
+        )
+
+    first = 4 * unit
+    held = adapter_down_weight.shape[0]
+    maps = adapter_down_weight
+    flat, head = first_piece(hidden, key_value_weight, place, which[0], first, chunk, [])
+    partial[0] = [(0, ordered(head))]
+
+    def others(s, cuts, after):
+        results = other_slots(hidden, key_value_weight, place, which[s : s + len(cuts)], cuts, chunk, after)
+        for k, arrays in enumerate(results):
+            partial[s + k] = cut(arrays)
+        ordered(results[0][0])
+
+    if n == 4 and n_tok == 8:
+        def fetch(name, array, bits):
+            with jax.named_scope(name):
+                return lax.ppermute(array, "tok", [(i, i ^ bits) for i in range(n_tok)])
+
+        places = ((tenant_per_block // held) ^ lax.axis_index("tok")) * held + tenant_per_block % held
+        other_core, other_x, other_y = [fetch(f"maps_{bits}", maps, bits) for bits in (1, 2, 4)]
+        send(1, 0, 0, 4)
+        partial[0] += cut(more_rows(hidden, flat, first, [first], list(last)), first)
+        ordered(partial[0][1][1])
+        send(1, 0, 4, 4)
+        (again,) = copied([maps], last + [other_core, other_x, other_y])
+        ordered(again)
+        x_core, y_core = [fetch(f"maps_{bits}", again, bits) for bits in (3, 5)]
+        others(1, [[tok_rows // 2] * 2], list(last))
         send(2, 0, 0, 4)
-        send(2, 1, 0, 4)
-        others(2, [[tok_rows], [tok_rows]], list(last))
-        send(2, 1, 4, 4)
-        low_parts.append(ordered(low_terms(hidden, down_maps, tenant_per_block, list(last))))
+        upper = send(2, 1, 0, 4)
+        others(2, [[tok_rows]], list(last))
+        lower = send(2, 1, 4, 4)
+        x_again, y_again = copied([x_core, y_core], list(last))
+        ordered(x_again)
+        sources = [maps, other_core, other_x, x_core, other_y, y_core]
+        sources += [fetch("maps_6", x_again, 5), fetch("maps_7", y_again, 2)]
+        second = send(2, 0, 4, 4, after=[upper], again=True)
+        others(3, [[tok_rows]], list(last))
+        third = send(3, 1, 0, 4)
+        low_parts.append(ordered(low_terms(hidden, sources, places, list(last))))
         send_low(1)
-        send(2, 0, 4, 4, again=True)
-        send(3, 1, 0, 4)
-        send(3, 0, 0, 4)
-        send_low(2)
-        send(3, 0, 4, 2)
-        send_low(3)
+        fourth = send(3, 0, 0, 4, after=[lower, second])
+        with jax.named_scope("up_maps"):
+            ups = jnp.broadcast_to(adapter_up_weight, (n_tok,) + adapter_up_weight.shape)
+            ups = lax.all_to_all(ups, "tok", 0, 0, tiled=True)
+        up_maps = ups.reshape((n_tok * held,) + adapter_up_weight.shape[1:])
+        send_low(2, after=[third])
         send(3, 1, 4, 4)
-        send(3, 0, 6, 2)
-        prepare(0, 8)
-        complete(0, 4)
-        complete(4, 2)
-        complete(6, 2)
+        fifth = send(3, 0, 4, 2)
+        send_low(3, after=[up_maps])
+        send(3, 0, 6, 2, after=[fourth])
+        complete(0, 4, 512, after=[fifth])
+        complete(4, 2, 512)
+        complete(6, 2, 256)
     else:
-        partial[0] = [
-            (0, jnp.concatenate([head] + list(more_rows(hidden, flat, first, [tok_rows - first], []))))
-        ]
-        others = other_slots(hidden, key_value_weight, place, which[1:], [[tok_rows]] * (n - 1), chunk, [head])
-        for s, arrays in enumerate(others):
-            partial[s + 1] = cut(arrays)
-        ordered(head)
+        places = tenant_per_block
+        sources = [lax.all_gather(maps, "tok", axis=0, tiled=True)]
+        up_maps = lax.all_gather(adapter_up_weight, "tok", axis=0, tiled=True)
+        lower = more_rows(hidden, flat, first, [tok_rows - first], list(last))[0]
+        partial[0] = [(0, jnp.concatenate([head, lower]))]
+        others(1, [[tok_rows]] * (n - 1), list(last))
         for time in range(1, n):
             for parity in (0, 1):
                 if (time, parity) in sends:
                     send(time, parity, 0, UNITS)
-        low_parts.append(ordered(low_terms(hidden, down_maps, tenant_per_block, list(last))))
+        low_parts.append(ordered(low_terms(hidden, sources, places, list(last))))
         for time in range(1, n):
             send_low(time)
-        prepare(0, UNITS)
-        complete(0, UNITS)
+        complete(0, UNITS, 512)
     return result[0]
 
 
 def solution(mesh):
-    n = mesh.shape["tp"]
+    n, n_tok = mesh.shape["tp"], mesh.shape["tok"]
     in_specs = (
         P("tok", "tp"),
         P("tp", None, None),
@@ -508,6 +535,6 @@
     out_specs = P("tok", None, "tp")
 
     def run(*args):
-        return local(n, *args)
+        return local(n, n_tok, *args)
 
     return jax.shard_map(run, mesh=mesh, in_specs=in_specs, out_specs=out_specs, check_vma=False)

time: 174 us -> 173 us (level)
  between operations: 13.5 us -> 0.08 us
  starting transfers between devices: 39.6 us -> 50.9 us
  waiting for transfers between devices: 31.9 us -> 26.2 us
  Pallas kernels: 87.9 us -> 93.4 us
    ppermute x0 -> x7, starting transfers between devices: none -> 7.73 us  [fetch(): return lax.ppermute(array, 'tok', [(i, i ^ bits) for i in range(n_tok)])]
    ppermute x13 -> x11, waiting for transfers between devices: 17.5 us -> 10.7 us  [send(): moved = lax.ppermute(value, 'tp', moves)]
    ppermute x0 -> x7, waiting for transfers between devices: none -> 5.85 us  [fetch(): return lax.ppermute(array, 'tok', [(i, i ^ bits) for i in range(n_tok)])]
    all_to_all x0 -> x1, starting transfers between devices: none -> 4.25 us  [local(): ups = lax.all_to_all(ups, 'tok', 0, 0, tiled=True)]
    pallas_call x2 -> x3, Pallas kernels: 27.9 us -> 31.9 us  [other_slots(): pl.pallas_call(body, name='other_slots', grid_spec=pltpu.PrefetchScalarGr...]
    ppermute x3, waiting for transfers between devices: 13.6 us -> 9.71 us  [send_low(): lax.ppermute(value, 'tp', [(time - 1, time), (n - time, n - time - 1)])]
    pallas_call x4 -> x5, Pallas kernels: 14.3 us -> 16.9 us  [the longest x3 12.3 us: finish(): pl.pallas_call(body, name='finish', grid_spec=pltpu.PrefetchScalarGridSpe...]
    pallas_call x1, Pallas kernels: 8.08 us -> 5.62 us  [more_rows(): pl.pallas_call(body, name='more_rows', grid=(sum(cuts) // block,), in_spe...]
  transfers between devices with their start and end apart: 18 -> 22, of which waited for: 5 -> 8; matrix products, arithmetic and copies ran while one was open for 0% -> 1% of each run, Pallas kernels for 49% -> 52%
where the time goes in v4:
time: 173 us; the launch traced here: 172 us
  Pallas kernels  93.4 us (54%)
  starting transfers between devices  50.9 us (29%)
  waiting for transfers between devices  26.2 us (15%)
    ppermute x11, starting transfers between devices, send(): moved = lax.ppermute(value, 'tp', moves)  33.3 us
    pallas_call x3, Pallas kernels, other_slots(): pl.pallas_call(body, name='other_slots', grid_spec=pltpu.PrefetchScalarGr...  31.9 us
    pallas_call x10, Pallas kernels, added(): pl.pallas_call(body, name='added', grid=(rows // block,), in_specs=specs...  22.8 us
    pallas_call x3, Pallas kernels, finish(): pl.pallas_call(body, name='finish', grid_spec=pltpu.PrefetchScalarGridSpe...  12.3 us
    ppermute x11, waiting for transfers between devices, send(): moved = lax.ppermute(value, 'tp', moves)  10.7 us
    ppermute x3, waiting for transfers between devices, send_low(): lax.ppermute(value, 'tp', [(time - 1, time), (n - time, n - time - 1)])  9.71 us
    pallas_call x1, Pallas kernels, low_terms(): pl.pallas_call(body, name='low_terms', grid_spec=pltpu.PrefetchScalarGrid...  9.67 us
    ppermute x7, starting transfers between devices, fetch(): return lax.ppermute(array, 'tok', [(i, i ^ bits) for i in range(n_tok)])  7.73 us
  transfers between devices with their start and end apart: 22, of which 8 were waited for; matrix products, arithmetic and copies ran while one was open for 1% of the time, Pallas kernels for 52%

profile of v4, /device:TPU:0, one launch (start us, length us, event | category | flops | bytes accessed | tf_op | source)
XLA Modules:
  0.0 172.3 jit_solution(8164754613142349732)
XLA Ops:
  0.5 2.5 %collective-permute-start.1 = (bf16[2,2048,128]{2,1,0:T(8,128)(2,1)}, bf16[2,2048,128]{2,1,0:T(8,128)(2,1)}, u32[]{:S(2)}, u32[]{:S(2)}) collective-permute-start(bf16[2,2048,128]{2,1,0:T(8,128)(2,1)} %refs_0_.9), channel_id=1, source_target_pairs={{0,8},{4,12},{8,0},{12,4},{16,24},{20,28},{24,16},{28,20},{1,9},{5... | collective-permute-start | bytes 3145736 | tf_op jit(solution)/shard_map/maps_2/ppermute | solution.py:470
  2.9 1.5 collective-permute-start.2
  4.5 6.5 %first_piece.1 = (bf16[2048,512]{1,0:T(8,128)(2,1)}, bf16[1024,512]{1,0:T(8,128)(2,1)}) custom-call(s32[1]{0:T(128)} %bitcast.1.place_ref.which_ref, bf16[2048,2048]{1,0:T(8,128)(2,1)} %hidden_ref.11, bf16[2048,2,1024]{2,1,0:T(2,128)(2,1)} %refs_0_.8), custom_call_target="tpu_custom_call" | custom-call | flops 1 | bytes 5073750 | tf_op jit(solution)/shard_map/first_piece/pallas_call | solution.py:79
  10.9 4.5 %collective-permute-start.6 = (bf16[1024,512]{1,0:T(8,128)(2,1)}, bf16[1024,512]{1,0:T(8,128)(2,1)}, u32[]{:S(2)}, u32[]{:S(2)}) collective-permute-start(bf16[1024,512]{1,0:T(8,128)(2,1)} %get-tuple-element.12.refs_0_), channel_id=1, source_target_pairs={{0,1},{3,2},{4,5},{7,6},{8,9},{11,10},{12,13},{15,14},{16,17},{19,... | collective-permute-start | bytes 3145736 | tf_op jit(solution)/shard_map/even1_units0/ppermute | solution.py:432
  15.4 5.6 %more_rows.1.refs_1_.refs_0_ = bf16[1024,512]{1,0:T(8,128)(2,1)} custom-call(bf16[2048,2048]{1,0:T(8,128)(2,1)} %hidden_ref.11, bf16[2048,512]{1,0:T(8,128)(2,1)} %get-tuple-element.11.flat_ref, bf16[1024,512]{1,0:T(8,128)(2,1)} %get-tuple-element.12.refs_0_), custom_call_target="tpu_custom_call" | custom-call | flops 1 | bytes 4612500 | tf_op jit(solution)/shard_map/more_rows/pallas_call | solution.py:136
  21.1 2.2 %collective-permute-start.5 = (bf16[1024,512]{1,0:T(8,128)(2,1)}, bf16[1024,512]{1,0:T(8,128)(2,1)}, u32[]{:S(2)}, u32[]{:S(2)}) collective-permute-start(bf16[1024,512]{1,0:T(8,128)(2,1)} %more_rows.1.refs_1_.refs_0_), channel_id=1, source_target_pairs={{0,1},{3,2},{4,5},{7,6},{8,9},{11,10},{12,13},{15,14},{16,17},{19,... | collective-permute-start | bytes 3145736 | tf_op jit(solution)/shard_map/even1_units4/ppermute | solution.py:432
  23.3 3.8 %collective-permute-done.1.refs_3_.refs_2_ = bf16[2,2048,128]{2,1,0:T(8,128)(2,1)} collective-permute-done((bf16[2,2048,128]{2,1,0:T(8,128)(2,1)}, bf16[2,2048,128]{2,1,0:T(8,128)(2,1)}, u32[]{:S(2)}, u32[]{:S(2)}) %collective-permute-start.1) | collective-permute-done | bytes 1048608 | tf_op jit(solution)/shard_map/maps_2/ppermute | solution.py:470
  27.1 1.5 collective-permute-done.2.refs_4_
  28.6 2.1 %copied.2.refs_1_ = bf16[2,2048,128]{2,1,0:T(8,128)(2,1)} custom-call(bf16[2,2048,128]{2,1,0:T(8,128)(2,1)} %refs_0_.9, bf16[1024,512]{1,0:T(8,128)(2,1)} %more_rows.1.refs_1_.refs_0_, bf16[2,2048,128]{2,1,0:T(8,128)(2,1)} %collective-permute-done.refs_2_.refs_1_, bf16[2,2048,128]{2,1,0:T(8,128)(2,1)} %collective-permute-done.1.refs_3_.refs_2_, ...), custom_call_target="tpu_custom_call" | custom-call | flops 1 | bytes 1845000 | tf_op jit(solution)/shard_map/copied/pallas_call | solution.py:266
  30.6 1.8 %collective-permute-start.4 = (bf16[2,2048,128]{2,1,0:T(8,128)(2,1)}, bf16[2,2048,128]{2,1,0:T(8,128)(2,1)}, u32[]{:S(2)}, u32[]{:S(2)}) collective-permute-start(bf16[2,2048,128]{2,1,0:T(8,128)(2,1)} %copied.2.refs_1_), channel_id=1, source_target_pairs={{0,20},{4,16},{8,28},{12,24},{16,4},{20,0},{24,12},{28,8},{1,21},{... | collective-permute-start | bytes 3145736 | tf_op jit(solution)/shard_map/maps_5/ppermute | solution.py:470
  32.4 10.7 %other_slots.3 = (bf16[1024,512]{1,0:T(8,128)(2,1)}, bf16[1024,512]{1,0:T(8,128)(2,1)}) custom-call(s32[1]{0:T(128)} %bitcast.1.place_ref.which_ref, bf16[2048,2048]{1,0:T(8,128)(2,1)} %hidden_ref.11, bf16[2048,2,1024]{2,1,0:T(2,128)(2,1)} %refs_0_.8, bf16[2,2048,128]{2,1,0:T(8,128)(2,1)} %copied.2.refs_1_), custom_call_target="tpu_custom_call" | custom-call | flops 1 | bytes 12177000 | tf_op jit(solution)/shard_map/other_slots/pallas_call | solution.py:189
  43.1 2.5 %added.10.refs_1_ = bf16[1024,512]{1,0:T(8,128)(2,1)} custom-call(bf16[1024,512]{1,0:T(8,128)(2,1)} %get-tuple-element.12.refs_0_, bf16[1024,512]{1,0:T(8,128)(2,1)} %collective-permute-done.6.refs_1_, bf16[1024,512]{1,0:T(8,128)(2,1)} %get-tuple-element.13.refs_2_.refs_0_), custom_call_target="tpu_custom_call" | custom-call | flops 1 | bytes 2398500 | tf_op jit(solution)/shard_map/added/pallas_call | solution.py:246
  45.6 1.7 %collective-permute-start.10 = (bf16[1024,512]{1,0:T(8,128)(2,1)}, bf16[1024,512]{1,0:T(8,128)(2,1)}, u32[]{:S(2)}, u32[]{:S(2)}) collective-permute-start(bf16[1024,512]{1,0:T(8,128)(2,1)} %added.10.refs_1_), channel_id=1, source_target_pairs={{1,2},{2,1},{5,6},{6,5},{9,10},{10,9},{13,14},{14,13},{17,18},{18,... | collective-permute-start | bytes 3145736 | tf_op jit(solution)/shard_map/odd2_units0/ppermute | solution.py:432
  47.3 6.2 %collective-permute-start.9 = (bf16[1024,512]{1,0:T(8,128)(2,1)}, bf16[1024,512]{1,0:T(8,128)(2,1)}, u32[]{:S(2)}, u32[]{:S(2)}) collective-permute-start(bf16[1024,512]{1,0:T(8,128)(2,1)} %get-tuple-element.13.refs_2_.refs_0_), channel_id=1, source_target_pairs={{0,1},{3,2},{4,5},{7,6},{8,9},{11,10},{12,13},{15,14},{16,17},{19,... | collective-permute-start | bytes 3145736 | tf_op jit(solution)/shard_map/even2_units0/ppermute | solution.py:432
  53.5 10.6 %other_slots.4.refs_2_.refs_0_ = bf16[2048,512]{1,0:T(8,128)(2,1)} custom-call(s32[1]{0:T(128)} %bitcast.1.place_ref.which_ref, bf16[2048,2048]{1,0:T(8,128)(2,1)} %hidden_ref.11, bf16[2048,2,1024]{2,1,0:T(2,128)(2,1)} %refs_0_.8, bf16[1024,512]{1,0:T(8,128)(2,1)} %added.10.refs_1_), custom_call_target="tpu_custom_call" | custom-call | flops 1 | bytes 12177000 | tf_op jit(solution)/shard_map/other_slots/pallas_call | solution.py:189
  64.1 2.5 %added.11.refs_2_ = bf16[1024,512]{1,0:T(8,128)(2,1)} custom-call(bf16[1024,512]{1,0:T(8,128)(2,1)} %more_rows.1.refs_1_.refs_0_, bf16[1024,512]{1,0:T(8,128)(2,1)} %collective-permute-done.5.refs_1_, bf16[2048,512]{1,0:T(8,128)(2,1)} %other_slots.4.refs_2_.refs_0_), custom_call_target="tpu_custom_call" | custom-call | flops 1 | bytes 2398500 | tf_op jit(solution)/shard_map/added/pallas_call | solution.py:246
  66.6 2.6 %copied.3 = (bf16[2,2048,128]{2,1,0:T(8,128)(2,1)}, bf16[2,2048,128]{2,1,0:T(8,128)(2,1)}) custom-call(bf16[2,2048,128]{2,1,0:T(8,128)(2,1)} %collective-permute-done.3.refs_0_.refs_3_, bf16[2,2048,128]{2,1,0:T(8,128)(2,1)} %collective-permute-done.4.refs_1_.refs_5_, bf16[1024,512]{1,0:T(8,128)(2,1)} %added.11.refs_2_), custom_call_target="tpu_custom_call" | custom-call | flops 1 | bytes 1845000 | tf_op jit(solution)/shard_map/copied/pallas_call | solution.py:266
  69.2 1.5 collective-permute-start.8
  70.7 1.6 collective-permute-start.12
  72.3 2.1 %added.12.refs_1_ = bf16[1024,512]{1,0:T(8,128)(2,1)} custom-call(bf16[1024,512]{1,0:T(8,128)(2,1)} %get-tuple-element.16.refs_0_, bf16[2,2048,128]{2,1,0:T(8,128)(2,1)} %get-tuple-element.14.refs_1_, bf16[1024,512]{1,0:T(8,128)(2,1)} %collective-permute-done.10.refs_2_.refs_1_), custom_call_target="tpu_custom_call" | custom-call | flops 1 | bytes 2398500 | tf_op jit(solution)/shard_map/added/pallas_call | solution.py:246
  74.4 4.9 %collective-permute-start.13 = (bf16[1024,512]{1,0:T(8,128)(2,1)}, bf16[1024,512]{1,0:T(8,128)(2,1)}, u32[]{:S(2)}, u32[]{:S(2)}) collective-permute-start(bf16[1024,512]{1,0:T(8,128)(2,1)} %added.12.refs_1_), channel_id=1, source_target_pairs={{0,1},{3,2},{4,5},{7,6},{8,9},{11,10},{12,13},{15,14},{16,17},{19,... | collective-permute-start | bytes 3145736 | tf_op jit(solution)/shard_map/even2_units4/ppermute | solution.py:432
  79.3 10.6 %other_slots.5.refs_2_.refs_8_.refs_6_ = bf16[2048,512]{1,0:T(8,128)(2,1)} custom-call(s32[1]{0:T(128)} %bitcast.1.place_ref.which_ref, bf16[2048,2048]{1,0:T(8,128)(2,1)} %hidden_ref.11, bf16[2048,2,1024]{2,1,0:T(2,128)(2,1)} %refs_0_.8, bf16[1024,512]{1,0:T(8,128)(2,1)} %added.12.refs_1_), custom_call_target="tpu_custom_call" | custom-call | flops 1 | bytes 12177000 | tf_op jit(solution)/shard_map/other_slots/pallas_call | solution.py:189
  89.9 2.5 %added.13.refs_8_ = bf16[1024,512]{1,0:T(8,128)(2,1)} custom-call(bf16[1024,512]{1,0:T(8,128)(2,1)} %get-tuple-element.13.refs_2_.refs_0_, bf16[1024,512]{1,0:T(8,128)(2,1)} %collective-permute-done.9.refs_1_, bf16[2048,512]{1,0:T(8,128)(2,1)} %other_slots.5.refs_2_.refs_8_.refs_6_), custom_call_target="tpu_custom_call" | custom-call | flops 1 | bytes 2398500 | tf_op jit(solution)/shard_map/added/pallas_call | solution.py:246
  92.3 1.7 %collective-permute-start.14 = (bf16[1024,512]{1,0:T(8,128)(2,1)}, bf16[1024,512]{1,0:T(8,128)(2,1)}, u32[]{:S(2)}, u32[]{:S(2)}) collective-permute-start(bf16[1024,512]{1,0:T(8,128)(2,1)} %added.13.refs_8_), channel_id=1, source_target_pairs={{1,2},{2,1},{5,6},{6,5},{9,10},{10,9},{13,14},{14,13},{17,18},{18,... | collective-permute-start | bytes 3145736 | tf_op jit(solution)/shard_map/odd3_units0/ppermute | solution.py:432
  94.6 0.6 collective-permute-done.8.refs_7_
  95.2 9.7 %low_terms.1.refs_2_.refs_0_.refs_4_ = bf16[2048,128]{1,0:T(8,128)(2,1)} custom-call(s32[16]{0:T(128)} %fusion.place_ref, bf16[2048,2048]{1,0:T(8,128)(2,1)} %hidden_ref.11, bf16[2,2048,128]{2,1,0:T(8,128)(2,1)} %refs_0_.9, bf16[2,2048,128]{2,1,0:T(8,128)(2,1)} %collective-permute-done.refs_2_.refs_1_, ...), custom_call_target="tpu_custom_call" | custom-call | flops 1 | bytes 7933500 | tf_op jit(solution)/shard_map/low_terms/pallas_call | solution.py:311
  104.9 2.7 %collective-permute-start.11 = (bf16[2048,128]{1,0:T(8,128)(2,1)}, bf16[2048,128]{1,0:T(8,128)(2,1)}, u32[]{:S(2)}, u32[]{:S(2)}) collective-permute-start(bf16[2048,128]{1,0:T(8,128)(2,1)} %low_terms.1.refs_2_.refs_0_.refs_4_), channel_id=1, source_target_pairs={{0,1},{3,2},{4,5},{7,6},{8,9},{11,10},{12,13},{15,14},{16,17},{19,... | collective-permute-start | bytes 1572872 | tf_op jit(solution)/shard_map/low_sums1/ppermute | solution.py:443
  107.6 2.5 %added.14.refs_2_ = bf16[1024,512]{1,0:T(8,128)(2,1)} custom-call(bf16[2048,512]{1,0:T(8,128)(2,1)} %other_slots.4.refs_2_.refs_0_, bf16[1024,512]{1,0:T(8,128)(2,1)} %collective-permute-done.10.refs_2_.refs_1_, bf16[2048,128]{1,0:T(8,128)(2,1)} %low_terms.1.refs_2_.refs_0_.refs_4_, bf16[1024,512]{1,0:T(8,128)(2,1)} %collective-permute-done.12.refs_3_.refs_1_, ...), custom_call_target="tpu_custom_call" | custom-call | flops 1 | bytes 2398500 | tf_op jit(solution)/shard_map/added/pallas_call | solution.py:246
  110.0 1.2 broadcast_in_dim.3
  111.2 4.2 %all-to-all-start = ((bf16[8,2,2,64,256]{4,3,2,1,0:T(8,128)(2,1)}), bf16[8,2,2,64,256]{4,3,2,1,0:T(8,128)(2,1)}, u32[]{:S(2)}, u32[]{:S(2)}) async-start(bf16[8,2,2,64,256]{4,3,2,1,0:T(8,128)(2,1)} %broadcast_in_dim.3), calls=%async_computation | async-start | bytes 2097152 | tf_op jit(solution)/shard_map/up_maps/all_to_all | solution.py:498
  115.5 3.9 %collective-permute-done.11.refs_1_.refs_5_.refs_3_ = bf16[2048,128]{1,0:T(8,128)(2,1)} collective-permute-done((bf16[2048,128]{1,0:T(8,128)(2,1)}, bf16[2048,128]{1,0:T(8,128)(2,1)}, u32[]{:S(2)}, u32[]{:S(2)}) %collective-permute-start.11) | collective-permute-done | bytes 524320 | tf_op jit(solution)/shard_map/low_sums1/ppermute | solution.py:443
  119.4 2.1 %added.15.refs_2_ = bf16[2048,128]{1,0:T(8,128)(2,1)} custom-call(bf16[2048,128]{1,0:T(8,128)(2,1)} %low_terms.1.refs_2_.refs_0_.refs_4_, bf16[2048,128]{1,0:T(8,128)(2,1)} %collective-permute-done.11.refs_1_.refs_5_.refs_3_, bf16[1024,512]{1,0:T(8,128)(2,1)} %added.14.refs_2_, bf16[1024,512]{1,0:T(8,128)(2,1)} %collective-permute-done.14.refs_3_.refs_10_), custom_call_target="tpu_custom_call" | custom-call | flops 1 | bytes 1199250 | tf_op jit(solution)/shard_map/added/pallas_call | solution.py:246
  121.5 1.5 collective-permute-start.15
  123.0 2.4 %added.16.refs_2_ = bf16[1024,512]{1,0:T(8,128)(2,1)} custom-call(bf16[1024,512]{1,0:T(8,128)(2,1)} %get-tuple-element.16.refs_0_, bf16[1024,512]{1,0:T(8,128)(2,1)} %collective-permute-done.13.refs_4_.refs_1_, bf16[2048,128]{1,0:T(8,128)(2,1)} %added.15.refs_2_), custom_call_target="tpu_custom_call" | custom-call | flops 1 | bytes 2398500 | tf_op jit(solution)/shard_map/added/pallas_call | solution.py:246
  125.4 1.7 collective-permute-start.19
  127.1 2.1 %added.17.refs_2_ = bf16[512,512]{1,0:T(8,128)(2,1)} custom-call(bf16[2048,512]{1,0:T(8,128)(2,1)} %other_slots.4.refs_2_.refs_0_, bf16[1024,512]{1,0:T(8,128)(2,1)} %collective-permute-done.12.refs_3_.refs_1_, bf16[1024,512]{1,0:T(8,128)(2,1)} %added.16.refs_2_), custom_call_target="tpu_custom_call" | custom-call | flops 1 | bytes 1199250 | tf_op jit(solution)/shard_map/added/pallas_call | solution.py:246
  129.2 5.2 %collective-permute-start.20 = (bf16[512,512]{1,0:T(8,128)(2,1)}, bf16[512,512]{1,0:T(8,128)(2,1)}, u32[]{:S(2)}, u32[]{:S(2)}) collective-permute-start(bf16[512,512]{1,0:T(8,128)(2,1)} %added.17.refs_2_), channel_id=1, source_target_pairs={{0,1},{1,0},{2,3},{3,2},{4,5},{5,4},{6,7},{7,6},{8,9},{9,8},{10,11... | collective-permute-start | bytes 1572872 | tf_op jit(solution)/shard_map/even3_units4/ppermute | solution.py:432
  134.4 2.1 %added.18.refs_2_ = bf16[2048,128]{1,0:T(8,128)(2,1)} custom-call(bf16[2048,128]{1,0:T(8,128)(2,1)} %low_terms.1.refs_2_.refs_0_.refs_4_, bf16[2048,128]{1,0:T(8,128)(2,1)} %collective-permute-done.15.refs_1_.refs_6_.refs_4_, bf16[512,512]{1,0:T(8,128)(2,1)} %added.17.refs_2_, bf16[16,2,64,256]{3,2,1,0:T(8,128)(2,1)} %bitcast.refs_3_.refs_0_.refs_1_.refs_2_), custom_call_target="tpu_custom_call" | custom-call | flops 1 | bytes 1199250 | tf_op jit(solution)/shard_map/added/pallas_call | solution.py:246
  136.5 1.5 collective-permute-start.16
  138.0 3.9 %collective-permute-done.17.refs_3_.refs_9_ = bf16[1024,512]{1,0:T(8,128)(2,1)} collective-permute-done((bf16[1024,512]{1,0:T(8,128)(2,1)}, bf16[1024,512]{1,0:T(8,128)(2,1)}, u32[]{:S(2)}, u32[]{:S(2)}) %collective-permute-start.17) | collective-permute-done | bytes 1048608 | tf_op jit(solution)/shard_map/even3_units0/ppermute | solution.py:432
  141.9 2.1 %added.19 = bf16[512,512]{1,0:T(8,128)(2,1)} custom-call(bf16[2048,512]{1,0:T(8,128)(2,1)} %other_slots.4.refs_2_.refs_0_, bf16[1024,512]{1,0:T(8,128)(2,1)} %collective-permute-done.12.refs_3_.refs_1_, bf16[2048,128]{1,0:T(8,128)(2,1)} %added.18.refs_2_, bf16[1024,512]{1,0:T(8,128)(2,1)} %collective-permute-done.17.refs_3_.refs_9_), custom_call_target="tpu_custom_call" | custom-call | flops 1 | bytes 1199250 | tf_op jit(solution)/shard_map/added/pallas_call | solution.py:246
  144.0 3.5 %collective-permute-start.18 = (bf16[512,512]{1,0:T(8,128)(2,1)}, bf16[512,512]{1,0:T(8,128)(2,1)}, u32[]{:S(2)}, u32[]{:S(2)}) collective-permute-start(bf16[512,512]{1,0:T(8,128)(2,1)} %added.19), channel_id=1, source_target_pairs={{0,1},{1,0},{2,3},{3,2},{4,5},{5,4},{6,7},{7,6},{8,9},{9,8},{10,11... | collective-permute-start | bytes 1572872 | tf_op jit(solution)/shard_map/even3_units6/ppermute | solution.py:432
  147.5 5.6 %collective-permute-done.20.refs_11_.refs_9_ = bf16[512,512]{1,0:T(8,128)(2,1)} collective-permute-done((bf16[512,512]{1,0:T(8,128)(2,1)}, bf16[512,512]{1,0:T(8,128)(2,1)}, u32[]{:S(2)}, u32[]{:S(2)}) %collective-permute-start.20) | collective-permute-done | bytes 524320 | tf_op jit(solution)/shard_map/even3_units4/ppermute | solution.py:432
  153.1 5.8 %collective-permute-done.16.refs_7_.refs_5_ = bf16[2048,128]{1,0:T(8,128)(2,1)} collective-permute-done((bf16[2048,128]{1,0:T(8,128)(2,1)}, bf16[2048,128]{1,0:T(8,128)(2,1)}, u32[]{:S(2)}, u32[]{:S(2)}) %collective-permute-start.16) | collective-permute-done | bytes 524320 | tf_op jit(solution)/shard_map/low_sums3/ppermute | solution.py:443
  158.9 4.7 %finish.3.refs_11_ = bf16[2048,2,256]{2,1,0:T(2,128)(2,1)} custom-call(s32[16]{0:T(128)} %tenant_ref.5, bf16[16,2,64,256]{3,2,1,0:T(8,128)(2,1)} %bitcast.refs_3_.refs_0_.refs_1_.refs_2_, bf16[16,2,64,256]{3,2,1,0:T(8,128)(2,1)} %bitcast.refs_3_.refs_0_.refs_1_.refs_2_, bf16[16,2,64,256]{3,2,1,0:T(8,128)(2,1)} %bitcast.refs_3_.refs_0_.refs_1_.refs_2_, ...), custom_call_target="tpu_custom_call" | custom-call | flops 1 | bytes 3690000 | tf_op jit(solution)/shard_map/finish/pallas_call | solution.py:362
  163.7 3.9 %finish.4.refs_9_ = bf16[2048,2,256]{2,1,0:T(2,128)(2,1)} custom-call(s32[16]{0:T(128)} %tenant_ref.5, bf16[16,2,64,256]{3,2,1,0:T(8,128)(2,1)} %bitcast.refs_3_.refs_0_.refs_1_.refs_2_, bf16[16,2,64,256]{3,2,1,0:T(8,128)(2,1)} %bitcast.refs_3_.refs_0_.refs_1_.refs_2_, ...), custom_call_target="tpu_custom_call", output_to_operand_aliasing={{}: (12, {})} | custom-call | flops 1 | bytes 1845000 | tf_op jit(solution)/shard_map/finish/pallas_call | solution.py:362
  167.5 1.1 collective-permute-done.18.refs_7_
  168.6 3.7 %finish.5 = bf16[2048,2,256]{2,1,0:T(2,128)(2,1)} custom-call(s32[16]{0:T(128)} %tenant_ref.5, bf16[16,2,64,256]{3,2,1,0:T(8,128)(2,1)} %bitcast.refs_3_.refs_0_.refs_1_.refs_2_, bf16[16,2,64,256]{3,2,1,0:T(8,128)(2,1)} %bitcast.refs_3_.refs_0_.refs_1_.refs_2_, bf16[2048,128]{1,0:T(8,128)(2,1)} %low_terms.1.refs_2_.refs_0_.refs_4_, ...), custom_call_target="tpu_custom_call", output_to_operand_aliasing={{}: (10, {})} | custom-call | flops 1 | bytes 3690000 | tf_op jit(solution)/shard_map/finish/pallas_call | solution.py:362
  (23 shorter events, 1.0 us)
Async XLA Ops:
  0.0 23.3 %collective-permute-start = (bf16[2,2048,128]{2,1,0:T(8,128)(2,1)}, bf16[2,2048,128]{2,1,0:T(8,128)(2,1)}, u32[]{:S(2)}, u32[]{:S(2)}) collective-permute-start(bf16[2,2048,128]{2,1,0:T(8,128)(2,1)} %refs_0_.9), channel_id=1, source_target_pairs={{0,4},{4,0},{8,12},{12,8},{16,20},{20,16},{24,28},{28,24},{1,5},{5... | collective-permute-start | bytes 3145736 | tf_op jit(solution)/shard_map/maps_1/ppermute | solution.py:470
  0.5 26.6 %collective-permute-start.1 = (bf16[2,2048,128]{2,1,0:T(8,128)(2,1)}, bf16[2,2048,128]{2,1,0:T(8,128)(2,1)}, u32[]{:S(2)}, u32[]{:S(2)}) collective-permute-start(bf16[2,2048,128]{2,1,0:T(8,128)(2,1)} %refs_0_.9), channel_id=1, source_target_pairs={{0,8},{4,12},{8,0},{12,4},{16,24},{20,28},{24,16},{28,20},{1,9},{5... | collective-permute-start | bytes 3145736 | tf_op jit(solution)/shard_map/maps_2/ppermute | solution.py:470
  2.9 25.6 %collective-permute-start.2 = (bf16[2,2048,128]{2,1,0:T(8,128)(2,1)}, bf16[2,2048,128]{2,1,0:T(8,128)(2,1)}, u32[]{:S(2)}, u32[]{:S(2)}) collective-permute-start(bf16[2,2048,128]{2,1,0:T(8,128)(2,1)} %refs_0_.9), channel_id=1, source_target_pairs={{0,16},{4,20},{8,24},{12,28},{16,0},{20,4},{24,8},{28,12},{1,17},{... | collective-permute-start | bytes 3145736 | tf_op jit(solution)/shard_map/maps_4/ppermute | solution.py:470
  10.9 32.2 %collective-permute-start.6 = (bf16[1024,512]{1,0:T(8,128)(2,1)}, bf16[1024,512]{1,0:T(8,128)(2,1)}, u32[]{:S(2)}, u32[]{:S(2)}) collective-permute-start(bf16[1024,512]{1,0:T(8,128)(2,1)} %get-tuple-element.12.refs_0_), channel_id=1, source_target_pairs={{0,1},{3,2},{4,5},{7,6},{8,9},{11,10},{12,13},{15,14},{16,17},{19,... | collective-permute-start | bytes 3145736 | tf_op jit(solution)/shard_map/even1_units0/ppermute | solution.py:432
  21.1 43.0 %collective-permute-start.5 = (bf16[1024,512]{1,0:T(8,128)(2,1)}, bf16[1024,512]{1,0:T(8,128)(2,1)}, u32[]{:S(2)}, u32[]{:S(2)}) collective-permute-start(bf16[1024,512]{1,0:T(8,128)(2,1)} %more_rows.1.refs_1_.refs_0_), channel_id=1, source_target_pairs={{0,1},{3,2},{4,5},{7,6},{8,9},{11,10},{12,13},{15,14},{16,17},{19,... | collective-permute-start | bytes 3145736 | tf_op jit(solution)/shard_map/even1_units4/ppermute | solution.py:432
  30.6 35.9 %collective-permute-start.3 = (bf16[2,2048,128]{2,1,0:T(8,128)(2,1)}, bf16[2,2048,128]{2,1,0:T(8,128)(2,1)}, u32[]{:S(2)}, u32[]{:S(2)}) collective-permute-start(bf16[2,2048,128]{2,1,0:T(8,128)(2,1)} %copied.2.refs_1_), channel_id=1, source_target_pairs={{0,12},{4,8},{8,4},{12,0},{16,28},{20,24},{24,20},{28,16},{1,13},{... | collective-permute-start | bytes 3145736 | tf_op jit(solution)/shard_map/maps_3/ppermute | solution.py:470
  30.6 35.9 %collective-permute-start.4 = (bf16[2,2048,128]{2,1,0:T(8,128)(2,1)}, bf16[2,2048,128]{2,1,0:T(8,128)(2,1)}, u32[]{:S(2)}, u32[]{:S(2)}) collective-permute-start(bf16[2,2048,128]{2,1,0:T(8,128)(2,1)} %copied.2.refs_1_), channel_id=1, source_target_pairs={{0,20},{4,16},{8,28},{12,24},{16,4},{20,0},{24,12},{28,8},{1,21},{... | collective-permute-start | bytes 3145736 | tf_op jit(solution)/shard_map/maps_5/ppermute | solution.py:470
  45.6 26.7 %collective-permute-start.10 = (bf16[1024,512]{1,0:T(8,128)(2,1)}, bf16[1024,512]{1,0:T(8,128)(2,1)}, u32[]{:S(2)}, u32[]{:S(2)}) collective-permute-start(bf16[1024,512]{1,0:T(8,128)(2,1)} %added.10.refs_1_), channel_id=1, source_target_pairs={{1,2},{2,1},{5,6},{6,5},{9,10},{10,9},{13,14},{14,13},{17,18},{18,... | collective-permute-start | bytes 3145736 | tf_op jit(solution)/shard_map/odd2_units0/ppermute | solution.py:432
  47.3 42.6 %collective-permute-start.9 = (bf16[1024,512]{1,0:T(8,128)(2,1)}, bf16[1024,512]{1,0:T(8,128)(2,1)}, u32[]{:S(2)}, u32[]{:S(2)}) collective-permute-start(bf16[1024,512]{1,0:T(8,128)(2,1)} %get-tuple-element.13.refs_2_.refs_0_), channel_id=1, source_target_pairs={{0,1},{3,2},{4,5},{7,6},{8,9},{11,10},{12,13},{15,14},{16,17},{19,... | collective-permute-start | bytes 3145736 | tf_op jit(solution)/shard_map/even2_units0/ppermute | solution.py:432
  69.2 25.4 %collective-permute-start.7 = (bf16[2,2048,128]{2,1,0:T(8,128)(2,1)}, bf16[2,2048,128]{2,1,0:T(8,128)(2,1)}, u32[]{:S(2)}, u32[]{:S(2)}) collective-permute-start(bf16[2,2048,128]{2,1,0:T(8,128)(2,1)} %get-tuple-element.14.refs_1_), channel_id=1, source_target_pairs={{0,20},{4,16},{8,28},{12,24},{16,4},{20,0},{24,12},{28,8},{1,21},{... | collective-permute-start | bytes 3145736 | tf_op jit(solution)/shard_map/maps_6/ppermute | solution.py:470
  69.2 26.0 %collective-permute-start.8 = (bf16[2,2048,128]{2,1,0:T(8,128)(2,1)}, bf16[2,2048,128]{2,1,0:T(8,128)(2,1)}, u32[]{:S(2)}, u32[]{:S(2)}) collective-permute-start(bf16[2,2048,128]{2,1,0:T(8,128)(2,1)} %get-tuple-element.15), channel_id=1, source_target_pairs={{0,8},{4,12},{8,0},{12,4},{16,24},{20,28},{24,16},{28,20},{1,9},{5... | collective-permute-start | bytes 3145736 | tf_op jit(solution)/shard_map/maps_7/ppermute | solution.py:470
  70.7 36.9 %collective-permute-start.12 = (bf16[1024,512]{1,0:T(8,128)(2,1)}, bf16[1024,512]{1,0:T(8,128)(2,1)}, u32[]{:S(2)}, u32[]{:S(2)}) collective-permute-start(bf16[1024,512]{1,0:T(8,128)(2,1)} %added.11.refs_2_), channel_id=1, source_target_pairs={{1,2},{2,1},{5,6},{6,5},{9,10},{10,9},{13,14},{14,13},{17,18},{18,... | collective-permute-start | bytes 3145736 | tf_op jit(solution)/shard_map/odd2_units4/ppermute | solution.py:432
  74.4 33.2 %collective-permute-start.13 = (bf16[1024,512]{1,0:T(8,128)(2,1)}, bf16[1024,512]{1,0:T(8,128)(2,1)}, u32[]{:S(2)}, u32[]{:S(2)}) collective-permute-start(bf16[1024,512]{1,0:T(8,128)(2,1)} %added.12.refs_1_), channel_id=1, source_target_pairs={{0,1},{3,2},{4,5},{7,6},{8,9},{11,10},{12,13},{15,14},{16,17},{19,... | collective-permute-start | bytes 3145736 | tf_op jit(solution)/shard_map/even2_units4/ppermute | solution.py:432
  89.9 4.2 %copy-start.1 = (s32[16]{0:T(128)S(1)}, s32[16]{0:T(128)}, u32[]{:S(2)}) copy-start(s32[16]{0:T(128)} %tenant_ref.5) | copy-start | bytes 196
  92.3 23.2 %collective-permute-start.14 = (bf16[1024,512]{1,0:T(8,128)(2,1)}, bf16[1024,512]{1,0:T(8,128)(2,1)}, u32[]{:S(2)}, u32[]{:S(2)}) collective-permute-start(bf16[1024,512]{1,0:T(8,128)(2,1)} %added.13.refs_8_), channel_id=1, source_target_pairs={{1,2},{2,1},{5,6},{6,5},{9,10},{10,9},{13,14},{14,13},{17,18},{18,... | collective-permute-start | bytes 3145736 | tf_op jit(solution)/shard_map/odd3_units0/ppermute | solution.py:432
  104.8 5.2 %copy-start = (bf16[2,2,64,256]{3,2,1,0:T(8,128)(2,1)S(1)}, bf16[2,2,64,256]{3,2,1,0:T(8,128)(2,1)}, u32[]{:S(2)}) copy-start(bf16[2,2,64,256]{3,2,1,0:T(8,128)(2,1)} %param.8) | copy-start | bytes 393220
  104.9 14.5 %collective-permute-start.11 = (bf16[2048,128]{1,0:T(8,128)(2,1)}, bf16[2048,128]{1,0:T(8,128)(2,1)}, u32[]{:S(2)}, u32[]{:S(2)}) collective-permute-start(bf16[2048,128]{1,0:T(8,128)(2,1)} %low_terms.1.refs_2_.refs_0_.refs_4_), channel_id=1, source_target_pairs={{0,1},{3,2},{4,5},{7,6},{8,9},{11,10},{12,13},{15,14},{16,17},{19,... | collective-permute-start | bytes 1572872 | tf_op jit(solution)/shard_map/low_sums1/ppermute | solution.py:443
  110.0 31.8 %collective-permute-start.17 = (bf16[1024,512]{1,0:T(8,128)(2,1)}, bf16[1024,512]{1,0:T(8,128)(2,1)}, u32[]{:S(2)}, u32[]{:S(2)}) collective-permute-start(bf16[1024,512]{1,0:T(8,128)(2,1)} %added.14.refs_2_), channel_id=1, source_target_pairs={{0,1},{1,0},{2,3},{3,2},{4,5},{5,4},{6,7},{7,6},{8,9},{9,8},{10,11... | collective-permute-start | bytes 3145736 | tf_op jit(solution)/shard_map/even3_units0/ppermute | solution.py:432
  111.2 23.2 %all-to-all-start = ((bf16[8,2,2,64,256]{4,3,2,1,0:T(8,128)(2,1)}), bf16[8,2,2,64,256]{4,3,2,1,0:T(8,128)(2,1)}, u32[]{:S(2)}, u32[]{:S(2)}) async-start(bf16[8,2,2,64,256]{4,3,2,1,0:T(8,128)(2,1)} %broadcast_in_dim.3), calls=%async_computation | async-start | bytes 2097152 | tf_op jit(solution)/shard_map/up_maps/all_to_all | solution.py:498
  121.5 12.9 %collective-permute-start.15 = (bf16[2048,128]{1,0:T(8,128)(2,1)}, bf16[2048,128]{1,0:T(8,128)(2,1)}, u32[]{:S(2)}, u32[]{:S(2)}) collective-permute-start(bf16[2048,128]{1,0:T(8,128)(2,1)} %added.15.refs_2_), channel_id=1, source_target_pairs={{1,2},{2,1},{5,6},{6,5},{9,10},{10,9},{13,14},{14,13},{17,18},{18,... | collective-permute-start | bytes 1572872 | tf_op jit(solution)/shard_map/low_sums2/ppermute | solution.py:443
  125.4 38.2 %collective-permute-start.19 = (bf16[1024,512]{1,0:T(8,128)(2,1)}, bf16[1024,512]{1,0:T(8,128)(2,1)}, u32[]{:S(2)}, u32[]{:S(2)}) collective-permute-start(bf16[1024,512]{1,0:T(8,128)(2,1)} %added.16.refs_2_), channel_id=1, source_target_pairs={{1,2},{2,1},{5,6},{6,5},{9,10},{10,9},{13,14},{14,13},{17,18},{18,... | collective-permute-start | bytes 3145736 | tf_op jit(solution)/shard_map/odd3_units4/ppermute | solution.py:432
  129.2 23.9 %collective-permute-start.20 = (bf16[512,512]{1,0:T(8,128)(2,1)}, bf16[512,512]{1,0:T(8,128)(2,1)}, u32[]{:S(2)}, u32[]{:S(2)}) collective-permute-start(bf16[512,512]{1,0:T(8,128)(2,1)} %added.17.refs_2_), channel_id=1, source_target_pairs={{0,1},{1,0},{2,3},{3,2},{4,5},{5,4},{6,7},{7,6},{8,9},{9,8},{10,11... | collective-permute-start | bytes 1572872 | tf_op jit(solution)/shard_map/even3_units4/ppermute | solution.py:432
  136.5 22.4 %collective-permute-start.16 = (bf16[2048,128]{1,0:T(8,128)(2,1)}, bf16[2048,128]{1,0:T(8,128)(2,1)}, u32[]{:S(2)}, u32[]{:S(2)}) collective-permute-start(bf16[2048,128]{1,0:T(8,128)(2,1)} %added.18.refs_2_), channel_id=1, source_target_pairs={{2,3},{1,0},{6,7},{5,4},{10,11},{9,8},{14,15},{13,12},{18,19},{17,... | collective-permute-start | bytes 1572872 | tf_op jit(solution)/shard_map/low_sums3/ppermute | solution.py:443
  144.0 24.6 %collective-permute-start.18 = (bf16[512,512]{1,0:T(8,128)(2,1)}, bf16[512,512]{1,0:T(8,128)(2,1)}, u32[]{:S(2)}, u32[]{:S(2)}) collective-permute-start(bf16[512,512]{1,0:T(8,128)(2,1)} %added.19), channel_id=1, source_target_pairs={{0,1},{1,0},{2,3},{3,2},{4,5},{5,4},{6,7},{7,6},{8,9},{9,8},{10,11... | collective-permute-start | bytes 1572872 | tf_op jit(solution)/shard_map/even3_units6/ppermute | solution.py:432

commit v5 on v4

--- a/solution.py
+++ b/solution.py
@@ -497,9 +497,9 @@
             ups = jnp.broadcast_to(adapter_up_weight, (n_tok,) + adapter_up_weight.shape)
             ups = lax.all_to_all(ups, "tok", 0, 0, tiled=True)
         up_maps = ups.reshape((n_tok * held,) + adapter_up_weight.shape[1:])
+        fifth = send(3, 0, 4, 2)
         send_low(2, after=[third])
         send(3, 1, 4, 4)
-        fifth = send(3, 0, 4, 2)
         send_low(3, after=[up_maps])
         send(3, 0, 6, 2, after=[fourth])
         complete(0, 4, 512, after=[fifth])

time: 173 us -> 173 us (level)
    ppermute x3, waiting for transfers between devices: 9.71 us -> 7.59 us  [send_low(): lax.ppermute(value, 'tp', [(time - 1, time), (n - time, n - time - 1)])]
    ppermute x11, waiting for transfers between devices: 10.7 us -> 12.6 us  [send(): moved = lax.ppermute(value, 'tp', moves)]
where the time goes in v5:
time: 173 us; the launch traced here: 172 us
  Pallas kernels  93.5 us (54%)
  starting transfers between devices  50.9 us (29%)
  waiting for transfers between devices  26 us (15%)
    ppermute x11, starting transfers between devices, send(): moved = lax.ppermute(value, 'tp', moves)  33.3 us
    pallas_call x3, Pallas kernels, other_slots(): pl.pallas_call(body, name='other_slots', grid_spec=pltpu.PrefetchScalarGr...  31.9 us
    pallas_call x10, Pallas kernels, added(): pl.pallas_call(body, name='added', grid=(rows // block,), in_specs=specs...  22.9 us
    ppermute x11, waiting for transfers between devices, send(): moved = lax.ppermute(value, 'tp', moves)  12.6 us
    pallas_call x3, Pallas kernels, finish(): pl.pallas_call(body, name='finish', grid_spec=pltpu.PrefetchScalarGridSpe...  12.3 us
    pallas_call x1, Pallas kernels, low_terms(): pl.pallas_call(body, name='low_terms', grid_spec=pltpu.PrefetchScalarGrid...  9.76 us
    ppermute x7, starting transfers between devices, fetch(): return lax.ppermute(array, 'tok', [(i, i ^ bits) for i in range(n_tok)])  7.73 us
    ppermute x3, waiting for transfers between devices, send_low(): lax.ppermute(value, 'tp', [(time - 1, time), (n - time, n - time - 1)])  7.59 us
  transfers between devices with their start and end apart: 22, of which 8 were waited for; matrix products, arithmetic and copies ran while one was open for 1% of the time, Pallas kernels for 52%

profile of v5, /device:TPU:0, one launch (start us, length us, event | category | flops | bytes accessed | tf_op | source)
XLA Modules:
  0.0 172.3 jit_solution(5730977177693160785)
XLA Ops:
  0.5 2.5 %collective-permute-start.1 = (bf16[2,2048,128]{2,1,0:T(8,128)(2,1)}, bf16[2,2048,128]{2,1,0:T(8,128)(2,1)}, u32[]{:S(2)}, u32[]{:S(2)}) collective-permute-start(bf16[2,2048,128]{2,1,0:T(8,128)(2,1)} %refs_0_.9), channel_id=1, source_target_pairs={{0,8},{4,12},{8,0},{12,4},{16,24},{20,28},{24,16},{28,20},{1,9},{5... | collective-permute-start | bytes 3145736 | tf_op jit(solution)/shard_map/maps_2/ppermute | solution.py:470
  2.9 1.5 collective-permute-start.2
  4.5 6.5 %first_piece.1 = (bf16[2048,512]{1,0:T(8,128)(2,1)}, bf16[1024,512]{1,0:T(8,128)(2,1)}) custom-call(s32[1]{0:T(128)} %bitcast.1.place_ref.which_ref, bf16[2048,2048]{1,0:T(8,128)(2,1)} %hidden_ref.11, bf16[2048,2,1024]{2,1,0:T(2,128)(2,1)} %refs_0_.8), custom_call_target="tpu_custom_call" | custom-call | flops 1 | bytes 5073750 | tf_op jit(solution)/shard_map/first_piece/pallas_call | solution.py:79
  10.9 4.5 %collective-permute-start.6 = (bf16[1024,512]{1,0:T(8,128)(2,1)}, bf16[1024,512]{1,0:T(8,128)(2,1)}, u32[]{:S(2)}, u32[]{:S(2)}) collective-permute-start(bf16[1024,512]{1,0:T(8,128)(2,1)} %get-tuple-element.12.refs_0_), channel_id=1, source_target_pairs={{0,1},{3,2},{4,5},{7,6},{8,9},{11,10},{12,13},{15,14},{16,17},{19,... | collective-permute-start | bytes 3145736 | tf_op jit(solution)/shard_map/even1_units0/ppermute | solution.py:432
  15.4 5.6 %more_rows.1.refs_1_.refs_0_ = bf16[1024,512]{1,0:T(8,128)(2,1)} custom-call(bf16[2048,2048]{1,0:T(8,128)(2,1)} %hidden_ref.11, bf16[2048,512]{1,0:T(8,128)(2,1)} %get-tuple-element.11.flat_ref, bf16[1024,512]{1,0:T(8,128)(2,1)} %get-tuple-element.12.refs_0_), custom_call_target="tpu_custom_call" | custom-call | flops 1 | bytes 4612500 | tf_op jit(solution)/shard_map/more_rows/pallas_call | solution.py:136
  21.1 2.2 %collective-permute-start.5 = (bf16[1024,512]{1,0:T(8,128)(2,1)}, bf16[1024,512]{1,0:T(8,128)(2,1)}, u32[]{:S(2)}, u32[]{:S(2)}) collective-permute-start(bf16[1024,512]{1,0:T(8,128)(2,1)} %more_rows.1.refs_1_.refs_0_), channel_id=1, source_target_pairs={{0,1},{3,2},{4,5},{7,6},{8,9},{11,10},{12,13},{15,14},{16,17},{19,... | collective-permute-start | bytes 3145736 | tf_op jit(solution)/shard_map/even1_units4/ppermute | solution.py:432
  23.3 3.8 %collective-permute-done.1.refs_3_.refs_2_ = bf16[2,2048,128]{2,1,0:T(8,128)(2,1)} collective-permute-done((bf16[2,2048,128]{2,1,0:T(8,128)(2,1)}, bf16[2,2048,128]{2,1,0:T(8,128)(2,1)}, u32[]{:S(2)}, u32[]{:S(2)}) %collective-permute-start.1) | collective-permute-done | bytes 1048608 | tf_op jit(solution)/shard_map/maps_2/ppermute | solution.py:470
  27.1 1.5 collective-permute-done.2.refs_4_
  28.6 2.1 %copied.2.refs_1_ = bf16[2,2048,128]{2,1,0:T(8,128)(2,1)} custom-call(bf16[2,2048,128]{2,1,0:T(8,128)(2,1)} %refs_0_.9, bf16[1024,512]{1,0:T(8,128)(2,1)} %more_rows.1.refs_1_.refs_0_, bf16[2,2048,128]{2,1,0:T(8,128)(2,1)} %collective-permute-done.refs_2_.refs_1_, bf16[2,2048,128]{2,1,0:T(8,128)(2,1)} %collective-permute-done.1.refs_3_.refs_2_, ...), custom_call_target="tpu_custom_call" | custom-call | flops 1 | bytes 1845000 | tf_op jit(solution)/shard_map/copied/pallas_call | solution.py:266
  30.6 1.8 %collective-permute-start.4 = (bf16[2,2048,128]{2,1,0:T(8,128)(2,1)}, bf16[2,2048,128]{2,1,0:T(8,128)(2,1)}, u32[]{:S(2)}, u32[]{:S(2)}) collective-permute-start(bf16[2,2048,128]{2,1,0:T(8,128)(2,1)} %copied.2.refs_1_), channel_id=1, source_target_pairs={{0,20},{4,16},{8,28},{12,24},{16,4},{20,0},{24,12},{28,8},{1,21},{... | collective-permute-start | bytes 3145736 | tf_op jit(solution)/shard_map/maps_5/ppermute | solution.py:470
  32.4 10.7 %other_slots.3 = (bf16[1024,512]{1,0:T(8,128)(2,1)}, bf16[1024,512]{1,0:T(8,128)(2,1)}) custom-call(s32[1]{0:T(128)} %bitcast.1.place_ref.which_ref, bf16[2048,2048]{1,0:T(8,128)(2,1)} %hidden_ref.11, bf16[2048,2,1024]{2,1,0:T(2,128)(2,1)} %refs_0_.8, bf16[2,2048,128]{2,1,0:T(8,128)(2,1)} %copied.2.refs_1_), custom_call_target="tpu_custom_call" | custom-call | flops 1 | bytes 12177000 | tf_op jit(solution)/shard_map/other_slots/pallas_call | solution.py:189
  43.1 2.5 %added.10.refs_1_ = bf16[1024,512]{1,0:T(8,128)(2,1)} custom-call(bf16[1024,512]{1,0:T(8,128)(2,1)} %get-tuple-element.12.refs_0_, bf16[1024,512]{1,0:T(8,128)(2,1)} %collective-permute-done.6.refs_1_, bf16[1024,512]{1,0:T(8,128)(2,1)} %get-tuple-element.13.refs_2_.refs_0_), custom_call_target="tpu_custom_call" | custom-call | flops 1 | bytes 2398500 | tf_op jit(solution)/shard_map/added/pallas_call | solution.py:246
  45.6 1.7 %collective-permute-start.10 = (bf16[1024,512]{1,0:T(8,128)(2,1)}, bf16[1024,512]{1,0:T(8,128)(2,1)}, u32[]{:S(2)}, u32[]{:S(2)}) collective-permute-start(bf16[1024,512]{1,0:T(8,128)(2,1)} %added.10.refs_1_), channel_id=1, source_target_pairs={{1,2},{2,1},{5,6},{6,5},{9,10},{10,9},{13,14},{14,13},{17,18},{18,... | collective-permute-start | bytes 3145736 | tf_op jit(solution)/shard_map/odd2_units0/ppermute | solution.py:432
  47.3 6.2 %collective-permute-start.9 = (bf16[1024,512]{1,0:T(8,128)(2,1)}, bf16[1024,512]{1,0:T(8,128)(2,1)}, u32[]{:S(2)}, u32[]{:S(2)}) collective-permute-start(bf16[1024,512]{1,0:T(8,128)(2,1)} %get-tuple-element.13.refs_2_.refs_0_), channel_id=1, source_target_pairs={{0,1},{3,2},{4,5},{7,6},{8,9},{11,10},{12,13},{15,14},{16,17},{19,... | collective-permute-start | bytes 3145736 | tf_op jit(solution)/shard_map/even2_units0/ppermute | solution.py:432
  53.5 10.6 %other_slots.4.refs_2_.refs_0_ = bf16[2048,512]{1,0:T(8,128)(2,1)} custom-call(s32[1]{0:T(128)} %bitcast.1.place_ref.which_ref, bf16[2048,2048]{1,0:T(8,128)(2,1)} %hidden_ref.11, bf16[2048,2,1024]{2,1,0:T(2,128)(2,1)} %refs_0_.8, bf16[1024,512]{1,0:T(8,128)(2,1)} %added.10.refs_1_), custom_call_target="tpu_custom_call" | custom-call | flops 1 | bytes 12177000 | tf_op jit(solution)/shard_map/other_slots/pallas_call | solution.py:189
  64.1 2.5 %added.11.refs_2_ = bf16[1024,512]{1,0:T(8,128)(2,1)} custom-call(bf16[1024,512]{1,0:T(8,128)(2,1)} %more_rows.1.refs_1_.refs_0_, bf16[1024,512]{1,0:T(8,128)(2,1)} %collective-permute-done.5.refs_1_, bf16[2048,512]{1,0:T(8,128)(2,1)} %other_slots.4.refs_2_.refs_0_), custom_call_target="tpu_custom_call" | custom-call | flops 1 | bytes 2398500 | tf_op jit(solution)/shard_map/added/pallas_call | solution.py:246
  66.6 2.6 %copied.3 = (bf16[2,2048,128]{2,1,0:T(8,128)(2,1)}, bf16[2,2048,128]{2,1,0:T(8,128)(2,1)}) custom-call(bf16[2,2048,128]{2,1,0:T(8,128)(2,1)} %collective-permute-done.3.refs_0_.refs_3_, bf16[2,2048,128]{2,1,0:T(8,128)(2,1)} %collective-permute-done.4.refs_1_.refs_5_, bf16[1024,512]{1,0:T(8,128)(2,1)} %added.11.refs_2_), custom_call_target="tpu_custom_call" | custom-call | flops 1 | bytes 1845000 | tf_op jit(solution)/shard_map/copied/pallas_call | solution.py:266
  69.2 1.5 collective-permute-start.8
  70.7 1.6 collective-permute-start.12
  72.3 2.1 %added.12.refs_1_ = bf16[1024,512]{1,0:T(8,128)(2,1)} custom-call(bf16[1024,512]{1,0:T(8,128)(2,1)} %get-tuple-element.16.refs_0_, bf16[2,2048,128]{2,1,0:T(8,128)(2,1)} %get-tuple-element.14.refs_1_, bf16[1024,512]{1,0:T(8,128)(2,1)} %collective-permute-done.10.refs_2_.refs_1_), custom_call_target="tpu_custom_call" | custom-call | flops 1 | bytes 2398500 | tf_op jit(solution)/shard_map/added/pallas_call | solution.py:246
  74.4 4.9 %collective-permute-start.13 = (bf16[1024,512]{1,0:T(8,128)(2,1)}, bf16[1024,512]{1,0:T(8,128)(2,1)}, u32[]{:S(2)}, u32[]{:S(2)}) collective-permute-start(bf16[1024,512]{1,0:T(8,128)(2,1)} %added.12.refs_1_), channel_id=1, source_target_pairs={{0,1},{3,2},{4,5},{7,6},{8,9},{11,10},{12,13},{15,14},{16,17},{19,... | collective-permute-start | bytes 3145736 | tf_op jit(solution)/shard_map/even2_units4/ppermute | solution.py:432
  79.3 10.6 %other_slots.5.refs_2_.refs_8_.refs_6_ = bf16[2048,512]{1,0:T(8,128)(2,1)} custom-call(s32[1]{0:T(128)} %bitcast.1.place_ref.which_ref, bf16[2048,2048]{1,0:T(8,128)(2,1)} %hidden_ref.11, bf16[2048,2,1024]{2,1,0:T(2,128)(2,1)} %refs_0_.8, bf16[1024,512]{1,0:T(8,128)(2,1)} %added.12.refs_1_), custom_call_target="tpu_custom_call" | custom-call | flops 1 | bytes 12177000 | tf_op jit(solution)/shard_map/other_slots/pallas_call | solution.py:189
  89.9 2.5 %added.13.refs_8_ = bf16[1024,512]{1,0:T(8,128)(2,1)} custom-call(bf16[1024,512]{1,0:T(8,128)(2,1)} %get-tuple-element.13.refs_2_.refs_0_, bf16[1024,512]{1,0:T(8,128)(2,1)} %collective-permute-done.9.refs_1_, bf16[2048,512]{1,0:T(8,128)(2,1)} %other_slots.5.refs_2_.refs_8_.refs_6_), custom_call_target="tpu_custom_call" | custom-call | flops 1 | bytes 2398500 | tf_op jit(solution)/shard_map/added/pallas_call | solution.py:246
  92.3 1.7 %collective-permute-start.14 = (bf16[1024,512]{1,0:T(8,128)(2,1)}, bf16[1024,512]{1,0:T(8,128)(2,1)}, u32[]{:S(2)}, u32[]{:S(2)}) collective-permute-start(bf16[1024,512]{1,0:T(8,128)(2,1)} %added.13.refs_8_), channel_id=1, source_target_pairs={{1,2},{2,1},{5,6},{6,5},{9,10},{10,9},{13,14},{14,13},{17,18},{18,... | collective-permute-start | bytes 3145736 | tf_op jit(solution)/shard_map/odd3_units0/ppermute | solution.py:432
  94.6 0.6 collective-permute-done.8.refs_7_
  95.2 9.8 %low_terms.1.refs_2_.refs_0_.refs_4_ = bf16[2048,128]{1,0:T(8,128)(2,1)} custom-call(s32[16]{0:T(128)} %fusion.place_ref, bf16[2048,2048]{1,0:T(8,128)(2,1)} %hidden_ref.11, bf16[2,2048,128]{2,1,0:T(8,128)(2,1)} %refs_0_.9, bf16[2,2048,128]{2,1,0:T(8,128)(2,1)} %collective-permute-done.refs_2_.refs_1_, ...), custom_call_target="tpu_custom_call" | custom-call | flops 1 | bytes 7933500 | tf_op jit(solution)/shard_map/low_terms/pallas_call | solution.py:311
  104.9 2.7 %collective-permute-start.11 = (bf16[2048,128]{1,0:T(8,128)(2,1)}, bf16[2048,128]{1,0:T(8,128)(2,1)}, u32[]{:S(2)}, u32[]{:S(2)}) collective-permute-start(bf16[2048,128]{1,0:T(8,128)(2,1)} %low_terms.1.refs_2_.refs_0_.refs_4_), channel_id=1, source_target_pairs={{0,1},{3,2},{4,5},{7,6},{8,9},{11,10},{12,13},{15,14},{16,17},{19,... | collective-permute-start | bytes 1572872 | tf_op jit(solution)/shard_map/low_sums1/ppermute | solution.py:443
  107.7 2.5 %added.14.refs_2_ = bf16[1024,512]{1,0:T(8,128)(2,1)} custom-call(bf16[2048,512]{1,0:T(8,128)(2,1)} %other_slots.4.refs_2_.refs_0_, bf16[1024,512]{1,0:T(8,128)(2,1)} %collective-permute-done.10.refs_2_.refs_1_, bf16[2048,128]{1,0:T(8,128)(2,1)} %low_terms.1.refs_2_.refs_0_.refs_4_, bf16[1024,512]{1,0:T(8,128)(2,1)} %collective-permute-done.12.refs_3_.refs_1_, ...), custom_call_target="tpu_custom_call" | custom-call | flops 1 | bytes 2398500 | tf_op jit(solution)/shard_map/added/pallas_call | solution.py:246
  110.1 1.2 broadcast_in_dim.3
  111.3 4.2 %all-to-all-start = ((bf16[8,2,2,64,256]{4,3,2,1,0:T(8,128)(2,1)}), bf16[8,2,2,64,256]{4,3,2,1,0:T(8,128)(2,1)}, u32[]{:S(2)}, u32[]{:S(2)}) async-start(bf16[8,2,2,64,256]{4,3,2,1,0:T(8,128)(2,1)} %broadcast_in_dim.3), calls=%async_computation | async-start | bytes 2097152 | tf_op jit(solution)/shard_map/up_maps/all_to_all | solution.py:498
  115.6 2.1 %added.15.refs_2_ = bf16[512,512]{1,0:T(8,128)(2,1)} custom-call(bf16[2048,512]{1,0:T(8,128)(2,1)} %other_slots.4.refs_2_.refs_0_, bf16[1024,512]{1,0:T(8,128)(2,1)} %collective-permute-done.12.refs_3_.refs_1_, bf16[1024,512]{1,0:T(8,128)(2,1)} %added.14.refs_2_), custom_call_target="tpu_custom_call" | custom-call | flops 1 | bytes 1199250 | tf_op jit(solution)/shard_map/added/pallas_call | solution.py:246
  117.7 1.8 %collective-permute-done.11.refs_1_.refs_5_.refs_3_ = bf16[2048,128]{1,0:T(8,128)(2,1)} collective-permute-done((bf16[2048,128]{1,0:T(8,128)(2,1)}, bf16[2048,128]{1,0:T(8,128)(2,1)}, u32[]{:S(2)}, u32[]{:S(2)}) %collective-permute-start.11) | collective-permute-done | bytes 524320 | tf_op jit(solution)/shard_map/low_sums1/ppermute | solution.py:443
  119.5 2.1 %added.16.refs_2_ = bf16[2048,128]{1,0:T(8,128)(2,1)} custom-call(bf16[2048,128]{1,0:T(8,128)(2,1)} %low_terms.1.refs_2_.refs_0_.refs_4_, bf16[2048,128]{1,0:T(8,128)(2,1)} %collective-permute-done.11.refs_1_.refs_5_.refs_3_, bf16[512,512]{1,0:T(8,128)(2,1)} %added.15.refs_2_, bf16[1024,512]{1,0:T(8,128)(2,1)} %collective-permute-done.14.refs_3_.refs_10_), custom_call_target="tpu_custom_call" | custom-call | flops 1 | bytes 1199250 | tf_op jit(solution)/shard_map/added/pallas_call | solution.py:246
  121.6 1.5 collective-permute-start.15
  123.1 2.4 %added.17.refs_2_ = bf16[1024,512]{1,0:T(8,128)(2,1)} custom-call(bf16[1024,512]{1,0:T(8,128)(2,1)} %get-tuple-element.16.refs_0_, bf16[1024,512]{1,0:T(8,128)(2,1)} %collective-permute-done.13.refs_4_.refs_1_, bf16[2048,128]{1,0:T(8,128)(2,1)} %added.16.refs_2_), custom_call_target="tpu_custom_call" | custom-call | flops 1 | bytes 2398500 | tf_op jit(solution)/shard_map/added/pallas_call | solution.py:246
  125.5 1.7 collective-permute-start.19
  127.2 5.3 %collective-permute-start.20 = (bf16[512,512]{1,0:T(8,128)(2,1)}, bf16[512,512]{1,0:T(8,128)(2,1)}, u32[]{:S(2)}, u32[]{:S(2)}) collective-permute-start(bf16[512,512]{1,0:T(8,128)(2,1)} %added.15.refs_2_), channel_id=1, source_target_pairs={{0,1},{1,0},{2,3},{3,2},{4,5},{5,4},{6,7},{7,6},{8,9},{9,8},{10,11... | collective-permute-start | bytes 1572872 | tf_op jit(solution)/shard_map/even3_units4/ppermute | solution.py:432
  132.5 2.1 %added.18.refs_2_ = bf16[2048,128]{1,0:T(8,128)(2,1)} custom-call(bf16[2048,128]{1,0:T(8,128)(2,1)} %low_terms.1.refs_2_.refs_0_.refs_4_, bf16[2048,128]{1,0:T(8,128)(2,1)} %collective-permute-done.15.refs_1_.refs_6_.refs_4_, bf16[1024,512]{1,0:T(8,128)(2,1)} %added.17.refs_2_, bf16[16,2,64,256]{3,2,1,0:T(8,128)(2,1)} %bitcast.refs_3_.refs_0_.refs_1_.refs_2_), custom_call_target="tpu_custom_call" | custom-call | flops 1 | bytes 1199250 | tf_op jit(solution)/shard_map/added/pallas_call | solution.py:246
  134.6 1.5 collective-permute-start.16
  136.1 5.9 %collective-permute-done.17.refs_3_.refs_9_ = bf16[1024,512]{1,0:T(8,128)(2,1)} collective-permute-done((bf16[1024,512]{1,0:T(8,128)(2,1)}, bf16[1024,512]{1,0:T(8,128)(2,1)}, u32[]{:S(2)}, u32[]{:S(2)}) %collective-permute-start.17) | collective-permute-done | bytes 1048608 | tf_op jit(solution)/shard_map/even3_units0/ppermute | solution.py:432
  142.0 2.1 %added.19 = bf16[512,512]{1,0:T(8,128)(2,1)} custom-call(bf16[2048,512]{1,0:T(8,128)(2,1)} %other_slots.4.refs_2_.refs_0_, bf16[1024,512]{1,0:T(8,128)(2,1)} %collective-permute-done.12.refs_3_.refs_1_, bf16[2048,128]{1,0:T(8,128)(2,1)} %added.18.refs_2_, bf16[1024,512]{1,0:T(8,128)(2,1)} %collective-permute-done.17.refs_3_.refs_9_), custom_call_target="tpu_custom_call" | custom-call | flops 1 | bytes 1199250 | tf_op jit(solution)/shard_map/added/pallas_call | solution.py:246
  144.1 3.5 %collective-permute-start.18 = (bf16[512,512]{1,0:T(8,128)(2,1)}, bf16[512,512]{1,0:T(8,128)(2,1)}, u32[]{:S(2)}, u32[]{:S(2)}) collective-permute-start(bf16[512,512]{1,0:T(8,128)(2,1)} %added.19), channel_id=1, source_target_pairs={{0,1},{1,0},{2,3},{3,2},{4,5},{5,4},{6,7},{7,6},{8,9},{9,8},{10,11... | collective-permute-start | bytes 1572872 | tf_op jit(solution)/shard_map/even3_units6/ppermute | solution.py:432
  147.6 5.6 %collective-permute-done.20.refs_11_.refs_9_ = bf16[512,512]{1,0:T(8,128)(2,1)} collective-permute-done((bf16[512,512]{1,0:T(8,128)(2,1)}, bf16[512,512]{1,0:T(8,128)(2,1)}, u32[]{:S(2)}, u32[]{:S(2)}) %collective-permute-start.20) | collective-permute-done | bytes 524320 | tf_op jit(solution)/shard_map/even3_units4/ppermute | solution.py:432
  153.2 5.8 %collective-permute-done.16.refs_7_.refs_5_ = bf16[2048,128]{1,0:T(8,128)(2,1)} collective-permute-done((bf16[2048,128]{1,0:T(8,128)(2,1)}, bf16[2048,128]{1,0:T(8,128)(2,1)}, u32[]{:S(2)}, u32[]{:S(2)}) %collective-permute-start.16) | collective-permute-done | bytes 524320 | tf_op jit(solution)/shard_map/low_sums3/ppermute | solution.py:443
  159.0 4.7 %finish.3.refs_11_ = bf16[2048,2,256]{2,1,0:T(2,128)(2,1)} custom-call(s32[16]{0:T(128)} %tenant_ref.5, bf16[16,2,64,256]{3,2,1,0:T(8,128)(2,1)} %bitcast.refs_3_.refs_0_.refs_1_.refs_2_, bf16[16,2,64,256]{3,2,1,0:T(8,128)(2,1)} %bitcast.refs_3_.refs_0_.refs_1_.refs_2_, bf16[16,2,64,256]{3,2,1,0:T(8,128)(2,1)} %bitcast.refs_3_.refs_0_.refs_1_.refs_2_, ...), custom_call_target="tpu_custom_call" | custom-call | flops 1 | bytes 3690000 | tf_op jit(solution)/shard_map/finish/pallas_call | solution.py:362
  163.8 3.9 %finish.4.refs_9_ = bf16[2048,2,256]{2,1,0:T(2,128)(2,1)} custom-call(s32[16]{0:T(128)} %tenant_ref.5, bf16[16,2,64,256]{3,2,1,0:T(8,128)(2,1)} %bitcast.refs_3_.refs_0_.refs_1_.refs_2_, bf16[16,2,64,256]{3,2,1,0:T(8,128)(2,1)} %bitcast.refs_3_.refs_0_.refs_1_.refs_2_, ...), custom_call_target="tpu_custom_call", output_to_operand_aliasing={{}: (12, {})} | custom-call | flops 1 | bytes 1845000 | tf_op jit(solution)/shard_map/finish/pallas_call | solution.py:362
  167.6 1.0 collective-permute-done.18.refs_7_
  168.6 3.7 %finish.5 = bf16[2048,2,256]{2,1,0:T(2,128)(2,1)} custom-call(s32[16]{0:T(128)} %tenant_ref.5, bf16[16,2,64,256]{3,2,1,0:T(8,128)(2,1)} %bitcast.refs_3_.refs_0_.refs_1_.refs_2_, bf16[16,2,64,256]{3,2,1,0:T(8,128)(2,1)} %bitcast.refs_3_.refs_0_.refs_1_.refs_2_, bf16[2048,128]{1,0:T(8,128)(2,1)} %low_terms.1.refs_2_.refs_0_.refs_4_, ...), custom_call_target="tpu_custom_call", output_to_operand_aliasing={{}: (10, {})} | custom-call | flops 1 | bytes 3690000 | tf_op jit(solution)/shard_map/finish/pallas_call | solution.py:362
  (23 shorter events, 1.0 us)
Async XLA Ops:
  0.0 23.3 %collective-permute-start = (bf16[2,2048,128]{2,1,0:T(8,128)(2,1)}, bf16[2,2048,128]{2,1,0:T(8,128)(2,1)}, u32[]{:S(2)}, u32[]{:S(2)}) collective-permute-start(bf16[2,2048,128]{2,1,0:T(8,128)(2,1)} %refs_0_.9), channel_id=1, source_target_pairs={{0,4},{4,0},{8,12},{12,8},{16,20},{20,16},{24,28},{28,24},{1,5},{5... | collective-permute-start | bytes 3145736 | tf_op jit(solution)/shard_map/maps_1/ppermute | solution.py:470
  0.5 26.6 %collective-permute-start.1 = (bf16[2,2048,128]{2,1,0:T(8,128)(2,1)}, bf16[2,2048,128]{2,1,0:T(8,128)(2,1)}, u32[]{:S(2)}, u32[]{:S(2)}) collective-permute-start(bf16[2,2048,128]{2,1,0:T(8,128)(2,1)} %refs_0_.9), channel_id=1, source_target_pairs={{0,8},{4,12},{8,0},{12,4},{16,24},{20,28},{24,16},{28,20},{1,9},{5... | collective-permute-start | bytes 3145736 | tf_op jit(solution)/shard_map/maps_2/ppermute | solution.py:470
  2.9 25.6 %collective-permute-start.2 = (bf16[2,2048,128]{2,1,0:T(8,128)(2,1)}, bf16[2,2048,128]{2,1,0:T(8,128)(2,1)}, u32[]{:S(2)}, u32[]{:S(2)}) collective-permute-start(bf16[2,2048,128]{2,1,0:T(8,128)(2,1)} %refs_0_.9), channel_id=1, source_target_pairs={{0,16},{4,20},{8,24},{12,28},{16,0},{20,4},{24,8},{28,12},{1,17},{... | collective-permute-start | bytes 3145736 | tf_op jit(solution)/shard_map/maps_4/ppermute | solution.py:470
  10.9 32.2 %collective-permute-start.6 = (bf16[1024,512]{1,0:T(8,128)(2,1)}, bf16[1024,512]{1,0:T(8,128)(2,1)}, u32[]{:S(2)}, u32[]{:S(2)}) collective-permute-start(bf16[1024,512]{1,0:T(8,128)(2,1)} %get-tuple-element.12.refs_0_), channel_id=1, source_target_pairs={{0,1},{3,2},{4,5},{7,6},{8,9},{11,10},{12,13},{15,14},{16,17},{19,... | collective-permute-start | bytes 3145736 | tf_op jit(solution)/shard_map/even1_units0/ppermute | solution.py:432
  21.1 43.0 %collective-permute-start.5 = (bf16[1024,512]{1,0:T(8,128)(2,1)}, bf16[1024,512]{1,0:T(8,128)(2,1)}, u32[]{:S(2)}, u32[]{:S(2)}) collective-permute-start(bf16[1024,512]{1,0:T(8,128)(2,1)} %more_rows.1.refs_1_.refs_0_), channel_id=1, source_target_pairs={{0,1},{3,2},{4,5},{7,6},{8,9},{11,10},{12,13},{15,14},{16,17},{19,... | collective-permute-start | bytes 3145736 | tf_op jit(solution)/shard_map/even1_units4/ppermute | solution.py:432
  30.6 35.9 %collective-permute-start.3 = (bf16[2,2048,128]{2,1,0:T(8,128)(2,1)}, bf16[2,2048,128]{2,1,0:T(8,128)(2,1)}, u32[]{:S(2)}, u32[]{:S(2)}) collective-permute-start(bf16[2,2048,128]{2,1,0:T(8,128)(2,1)} %copied.2.refs_1_), channel_id=1, source_target_pairs={{0,12},{4,8},{8,4},{12,0},{16,28},{20,24},{24,20},{28,16},{1,13},{... | collective-permute-start | bytes 3145736 | tf_op jit(solution)/shard_map/maps_3/ppermute | solution.py:470
  30.6 35.9 %collective-permute-start.4 = (bf16[2,2048,128]{2,1,0:T(8,128)(2,1)}, bf16[2,2048,128]{2,1,0:T(8,128)(2,1)}, u32[]{:S(2)}, u32[]{:S(2)}) collective-permute-start(bf16[2,2048,128]{2,1,0:T(8,128)(2,1)} %copied.2.refs_1_), channel_id=1, source_target_pairs={{0,20},{4,16},{8,28},{12,24},{16,4},{20,0},{24,12},{28,8},{1,21},{... | collective-permute-start | bytes 3145736 | tf_op jit(solution)/shard_map/maps_5/ppermute | solution.py:470
  45.6 26.7 %collective-permute-start.10 = (bf16[1024,512]{1,0:T(8,128)(2,1)}, bf16[1024,512]{1,0:T(8,128)(2,1)}, u32[]{:S(2)}, u32[]{:S(2)}) collective-permute-start(bf16[1024,512]{1,0:T(8,128)(2,1)} %added.10.refs_1_), channel_id=1, source_target_pairs={{1,2},{2,1},{5,6},{6,5},{9,10},{10,9},{13,14},{14,13},{17,18},{18,... | collective-permute-start | bytes 3145736 | tf_op jit(solution)/shard_map/odd2_units0/ppermute | solution.py:432
  47.3 42.6 %collective-permute-start.9 = (bf16[1024,512]{1,0:T(8,128)(2,1)}, bf16[1024,512]{1,0:T(8,128)(2,1)}, u32[]{:S(2)}, u32[]{:S(2)}) collective-permute-start(bf16[1024,512]{1,0:T(8,128)(2,1)} %get-tuple-element.13.refs_2_.refs_0_), channel_id=1, source_target_pairs={{0,1},{3,2},{4,5},{7,6},{8,9},{11,10},{12,13},{15,14},{16,17},{19,... | collective-permute-start | bytes 3145736 | tf_op jit(solution)/shard_map/even2_units0/ppermute | solution.py:432
  69.2 25.4 %collective-permute-start.7 = (bf16[2,2048,128]{2,1,0:T(8,128)(2,1)}, bf16[2,2048,128]{2,1,0:T(8,128)(2,1)}, u32[]{:S(2)}, u32[]{:S(2)}) collective-permute-start(bf16[2,2048,128]{2,1,0:T(8,128)(2,1)} %get-tuple-element.14.refs_1_), channel_id=1, source_target_pairs={{0,20},{4,16},{8,28},{12,24},{16,4},{20,0},{24,12},{28,8},{1,21},{... | collective-permute-start | bytes 3145736 | tf_op jit(solution)/shard_map/maps_6/ppermute | solution.py:470
  69.2 26.0 %collective-permute-start.8 = (bf16[2,2048,128]{2,1,0:T(8,128)(2,1)}, bf16[2,2048,128]{2,1,0:T(8,128)(2,1)}, u32[]{:S(2)}, u32[]{:S(2)}) collective-permute-start(bf16[2,2048,128]{2,1,0:T(8,128)(2,1)} %get-tuple-element.15), channel_id=1, source_target_pairs={{0,8},{4,12},{8,0},{12,4},{16,24},{20,28},{24,16},{28,20},{1,9},{5... | collective-permute-start | bytes 3145736 | tf_op jit(solution)/shard_map/maps_7/ppermute | solution.py:470
  70.7 37.0 %collective-permute-start.12 = (bf16[1024,512]{1,0:T(8,128)(2,1)}, bf16[1024,512]{1,0:T(8,128)(2,1)}, u32[]{:S(2)}, u32[]{:S(2)}) collective-permute-start(bf16[1024,512]{1,0:T(8,128)(2,1)} %added.11.refs_2_), channel_id=1, source_target_pairs={{1,2},{2,1},{5,6},{6,5},{9,10},{10,9},{13,14},{14,13},{17,18},{18,... | collective-permute-start | bytes 3145736 | tf_op jit(solution)/shard_map/odd2_units4/ppermute | solution.py:432
  74.4 33.3 %collective-permute-start.13 = (bf16[1024,512]{1,0:T(8,128)(2,1)}, bf16[1024,512]{1,0:T(8,128)(2,1)}, u32[]{:S(2)}, u32[]{:S(2)}) collective-permute-start(bf16[1024,512]{1,0:T(8,128)(2,1)} %added.12.refs_1_), channel_id=1, source_target_pairs={{0,1},{3,2},{4,5},{7,6},{8,9},{11,10},{12,13},{15,14},{16,17},{19,... | collective-permute-start | bytes 3145736 | tf_op jit(solution)/shard_map/even2_units4/ppermute | solution.py:432
  89.9 4.2 %copy-start.1 = (s32[16]{0:T(128)S(1)}, s32[16]{0:T(128)}, u32[]{:S(2)}) copy-start(s32[16]{0:T(128)} %tenant_ref.5) | copy-start | bytes 196
  92.3 25.4 %collective-permute-start.14 = (bf16[1024,512]{1,0:T(8,128)(2,1)}, bf16[1024,512]{1,0:T(8,128)(2,1)}, u32[]{:S(2)}, u32[]{:S(2)}) collective-permute-start(bf16[1024,512]{1,0:T(8,128)(2,1)} %added.13.refs_8_), channel_id=1, source_target_pairs={{1,2},{2,1},{5,6},{6,5},{9,10},{10,9},{13,14},{14,13},{17,18},{18,... | collective-permute-start | bytes 3145736 | tf_op jit(solution)/shard_map/odd3_units0/ppermute | solution.py:432
  104.9 5.2 %copy-start = (bf16[2,2,64,256]{3,2,1,0:T(8,128)(2,1)S(1)}, bf16[2,2,64,256]{3,2,1,0:T(8,128)(2,1)}, u32[]{:S(2)}) copy-start(bf16[2,2,64,256]{3,2,1,0:T(8,128)(2,1)} %param.8) | copy-start | bytes 393220
  104.9 14.6 %collective-permute-start.11 = (bf16[2048,128]{1,0:T(8,128)(2,1)}, bf16[2048,128]{1,0:T(8,128)(2,1)}, u32[]{:S(2)}, u32[]{:S(2)}) collective-permute-start(bf16[2048,128]{1,0:T(8,128)(2,1)} %low_terms.1.refs_2_.refs_0_.refs_4_), channel_id=1, source_target_pairs={{0,1},{3,2},{4,5},{7,6},{8,9},{11,10},{12,13},{15,14},{16,17},{19,... | collective-permute-start | bytes 1572872 | tf_op jit(solution)/shard_map/low_sums1/ppermute | solution.py:443
  110.1 31.9 %collective-permute-start.17 = (bf16[1024,512]{1,0:T(8,128)(2,1)}, bf16[1024,512]{1,0:T(8,128)(2,1)}, u32[]{:S(2)}, u32[]{:S(2)}) collective-permute-start(bf16[1024,512]{1,0:T(8,128)(2,1)} %added.14.refs_2_), channel_id=1, source_target_pairs={{0,1},{1,0},{2,3},{3,2},{4,5},{5,4},{6,7},{7,6},{8,9},{9,8},{10,11... | collective-permute-start | bytes 3145736 | tf_op jit(solution)/shard_map/even3_units0/ppermute | solution.py:432
  111.3 21.2 %all-to-all-start = ((bf16[8,2,2,64,256]{4,3,2,1,0:T(8,128)(2,1)}), bf16[8,2,2,64,256]{4,3,2,1,0:T(8,128)(2,1)}, u32[]{:S(2)}, u32[]{:S(2)}) async-start(bf16[8,2,2,64,256]{4,3,2,1,0:T(8,128)(2,1)} %broadcast_in_dim.3), calls=%async_computation | async-start | bytes 2097152 | tf_op jit(solution)/shard_map/up_maps/all_to_all | solution.py:498
  121.6 10.8 %collective-permute-start.15 = (bf16[2048,128]{1,0:T(8,128)(2,1)}, bf16[2048,128]{1,0:T(8,128)(2,1)}, u32[]{:S(2)}, u32[]{:S(2)}) collective-permute-start(bf16[2048,128]{1,0:T(8,128)(2,1)} %added.16.refs_2_), channel_id=1, source_target_pairs={{1,2},{2,1},{5,6},{6,5},{9,10},{10,9},{13,14},{14,13},{17,18},{18,... | collective-permute-start | bytes 1572872 | tf_op jit(solution)/shard_map/low_sums2/ppermute | solution.py:443
  125.5 38.2 %collective-permute-start.19 = (bf16[1024,512]{1,0:T(8,128)(2,1)}, bf16[1024,512]{1,0:T(8,128)(2,1)}, u32[]{:S(2)}, u32[]{:S(2)}) collective-permute-start(bf16[1024,512]{1,0:T(8,128)(2,1)} %added.17.refs_2_), channel_id=1, source_target_pairs={{1,2},{2,1},{5,6},{6,5},{9,10},{10,9},{13,14},{14,13},{17,18},{18,... | collective-permute-start | bytes 3145736 | tf_op jit(solution)/shard_map/odd3_units4/ppermute | solution.py:432
  127.2 26.0 %collective-permute-start.20 = (bf16[512,512]{1,0:T(8,128)(2,1)}, bf16[512,512]{1,0:T(8,128)(2,1)}, u32[]{:S(2)}, u32[]{:S(2)}) collective-permute-start(bf16[512,512]{1,0:T(8,128)(2,1)} %added.15.refs_2_), channel_id=1, source_target_pairs={{0,1},{1,0},{2,3},{3,2},{4,5},{5,4},{6,7},{7,6},{8,9},{9,8},{10,11... | collective-permute-start | bytes 1572872 | tf_op jit(solution)/shard_map/even3_units4/ppermute | solution.py:432
  134.6 24.4 %collective-permute-start.16 = (bf16[2048,128]{1,0:T(8,128)(2,1)}, bf16[2048,128]{1,0:T(8,128)(2,1)}, u32[]{:S(2)}, u32[]{:S(2)}) collective-permute-start(bf16[2048,128]{1,0:T(8,128)(2,1)} %added.18.refs_2_), channel_id=1, source_target_pairs={{2,3},{1,0},{6,7},{5,4},{10,11},{9,8},{14,15},{13,12},{18,19},{17,... | collective-permute-start | bytes 1572872 | tf_op jit(solution)/shard_map/low_sums3/ppermute | solution.py:443
  144.1 24.5 %collective-permute-start.18 = (bf16[512,512]{1,0:T(8,128)(2,1)}, bf16[512,512]{1,0:T(8,128)(2,1)}, u32[]{:S(2)}, u32[]{:S(2)}) collective-permute-start(bf16[512,512]{1,0:T(8,128)(2,1)} %added.19), channel_id=1, source_target_pairs={{0,1},{1,0},{2,3},{3,2},{4,5},{5,4},{6,7},{7,6},{8,9},{9,8},{10,11... | collective-permute-start | bytes 1572872 | tf_op jit(solution)/shard_map/even3_units6/ppermute | solution.py:432
